TPU v7x, 32 devices: a whole 2x2x4 slice. The times are simulated.
32 devices in a mesh: seq: 32 (over z, y, x, core), tensor: 1.
Axes of the slice: x: 2, y: 2, z: 4, core: 2. Of those that a mesh axis runs over, the one named last changes fastest.
Arguments:
- query_rows: bfloat16 [4096, 4096], P('seq', 'tensor'), may hold values from -6 to 6
- key_rows: bfloat16 [4096, 4096], P('seq', 'tensor'), may hold values from -6 to 6
- value_rows: bfloat16 [4096, 4096], P('seq', 'tensor'), may hold values from -18 to 18
- cluster_id: int32 [32, 4096], P('tensor', 'seq'), may hold values from 0 to 255, as said below
- slot_index: int32 [32, 4096], P('tensor', 'seq'), may hold values from 0 to 31, as said below
- out_weight: bfloat16 [4096, 2048], P('tensor', 'seq'), may hold values from -0.09375 to 0.09375
- grad_out: bfloat16 [4096, 2048], P(('seq', 'tensor')), may hold values from -6 to 6
Outputs:
- mixed: bfloat16 [4096, 2048], P(('seq', 'tensor'))
- grad_query: bfloat16 [4096, 4096], P('seq', 'tensor')
- grad_key: bfloat16 [4096, 4096], P('seq', 'tensor')
- grad_value: bfloat16 [4096, 4096], P('seq', 'tensor')
Inputs may be any that keep to these rules, and one draw needn't show every extreme that they name: `cluster_id`: cluster c of a head belongs to the index c // 8 of seq. Each cluster of a head holds at most 32 tokens and in every head some cluster holds exactly 32. The tokens of one index of seq go, for one head, to at most 8 slots among the clusters of one owner, and every index of seq reaches 8 for some owner in every head. `slot_index`: within one head and cluster the slots of its tokens are distinct.
All inputs are finite; a program needn't handle non-finite values.
Results may differ from a plain program's by a relative error of at most 0.025.
Values may be sent and summed in bfloat16 or wider, within the bound.
No kernel may reach another device: no remote copies, remote signals or barrier semaphores. Data moves between devices by JAX's collectives and lax.ppermute only.
A program may use at most 128 MiB of HBM per device.

v0:
```python
import math

import jax
import jax.numpy as jnp
from jax import lax
from jax.sharding import PartitionSpec as P

CLU_DEV = 8
CAP = 32


def shards(query_rows, key_rows, value_rows, cluster_id, slot_index, out_weight, grad_out):
    rows_dev = query_rows.shape[0]
    heads_dev = cluster_id.shape[0]
    head_size = query_rows.shape[1] // heads_dev
    owners = lax.axis_size("seq")
    send_most = 2 * rows_dev // owners
    buffer_rows = owners * send_most
    room = CLU_DEV * CAP
    score_scale = 1.0 / math.sqrt(head_size)
    masked_score = -1e30
    owner = cluster_id // CLU_DEV
    owner_onehot = (owner[:, :, None] == jnp.arange(owners, dtype=jnp.int32)[None, None, :]).astype(
        jnp.bfloat16
    )
    row_ids = jnp.arange(rows_dev, dtype=jnp.int32)
    lower = (row_ids[:, None] > row_ids[None, :]).astype(jnp.bfloat16)
    earlier = jnp.einsum("ij,hjo->hio", lower, owner_onehot, preferred_element_type=jnp.float32)
    rank = jnp.sum(earlier * owner_onehot.astype(jnp.float32), axis=2).astype(jnp.int32)
    place = owner * send_most + rank
    target = cluster_id % CLU_DEV * CAP + slot_index
    buffer_ids = jnp.arange(buffer_rows, dtype=jnp.int32)
    send_table = (place[:, None, :] == buffer_ids[None, :, None]).astype(jnp.bfloat16)

    def to_buffer(rows):
        split = rows.reshape(rows_dev, heads_dev, head_size)
        filled = jnp.einsum(
            "hbi,ihd->bhd", send_table, split, preferred_element_type=jnp.float32
        ).astype(rows.dtype)
        return filled.reshape(buffer_rows, heads_dev * head_size)

    def from_buffer(buffer):
        split = buffer.reshape(buffer_rows, heads_dev, head_size)
        picked = jnp.einsum(
            "hbi,bhd->ihd", send_table, split, preferred_element_type=jnp.float32
        ).astype(buffer.dtype)
        return picked.reshape(rows_dev, heads_dev * head_size)

    target_rows = (
        jnp.einsum(
            "hbi,hi->bh", send_table.astype(jnp.float32), (target - room).astype(jnp.float32)
        ).astype(jnp.int32)
        + room
    )
    arrived = lax.all_to_all(target_rows, "seq", split_axis=0, concat_axis=0, tiled=True)
    routed_query, routed_key, routed_value = (
        lax.all_to_all(to_buffer(query_rows), "seq", split_axis=0, concat_axis=0, tiled=True),
        lax.all_to_all(to_buffer(key_rows), "seq", split_axis=0, concat_axis=0, tiled=True),
        lax.all_to_all(to_buffer(value_rows), "seq", split_axis=0, concat_axis=0, tiled=True),
    )
    room_ids = jnp.arange(room, dtype=jnp.int32)
    cell_table = (arrived.T[:, None, :] == room_ids[None, :, None]).astype(jnp.bfloat16)

    def to_cells(buffer):
        split = buffer.reshape(buffer_rows, heads_dev, head_size)
        cells = jnp.einsum(
            "hrb,bhd->hrd", cell_table, split, preferred_element_type=jnp.float32
        ).astype(buffer.dtype)
        return cells.reshape(heads_dev, CLU_DEV, CAP, head_size)

    def to_returns(cells):
        flat = cells.reshape(heads_dev, room, head_size)
        picked = jnp.einsum(
            "hrb,hrd->bhd", cell_table, flat, preferred_element_type=jnp.float32
        ).astype(cells.dtype)
        return picked.reshape(buffer_rows, heads_dev * head_size)

    live = jnp.sum(cell_table.astype(jnp.float32), axis=2).reshape(heads_dev, CLU_DEV, CAP)
    query_cells = to_cells(routed_query)
    key_cells = to_cells(routed_key)
    value_cells = to_cells(routed_value)
    scores = (
        jnp.einsum("hcqd,hckd->hcqk", query_cells, key_cells, preferred_element_type=jnp.float32)
        * score_scale
    )
    scores = jnp.where(live[:, :, None, :] > 0.5, scores, masked_score)
    top = jnp.max(scores, axis=-1, keepdims=True)
    weights = jnp.exp(scores - top)
    probs = weights / jnp.sum(weights, axis=-1, keepdims=True)
    probs_low = probs.astype(jnp.bfloat16)
    attended_cells = jnp.einsum(
        "hcqk,hckd->hcqd", probs_low, value_cells, preferred_element_type=jnp.float32
    ).astype(jnp.bfloat16)
    returned = lax.all_to_all(
        to_returns(attended_cells), "seq", split_axis=0, concat_axis=0, tiled=True
    )
    attended = from_buffer(returned)
    full_weight = lax.all_gather(out_weight, "seq", axis=1, tiled=True)
    rows = attended
    mixed = lax.psum_scatter(
        jnp.dot(rows, full_weight, preferred_element_type=jnp.float32).astype(jnp.bfloat16),
        "tensor",
        scatter_dimension=0,
        tiled=True,
    )
    grad_attended = lax.dot_general(
        lax.all_gather(grad_out, "tensor", axis=0, tiled=True),
        full_weight,
        (((1,), (1,)), ((), ())),
        preferred_element_type=jnp.float32,
    )
    grad_low = grad_attended.astype(jnp.bfloat16)
    routed_grad = lax.all_to_all(
        to_buffer(grad_low), "seq", split_axis=0, concat_axis=0, tiled=True
    )
    grad_cells = to_cells(routed_grad)
    backward_low = probs.astype(jnp.bfloat16)
    delta = jnp.einsum(
        "hcqd,hcqd->hcq", grad_cells, attended_cells, preferred_element_type=jnp.float32
    )
    grad_value = jnp.einsum(
        "hcqk,hcqd->hckd", backward_low, grad_cells, preferred_element_type=jnp.float32
    ).astype(jnp.bfloat16)
    grad_probs = jnp.einsum(
        "hcqd,hckd->hcqk", grad_cells, value_cells, preferred_element_type=jnp.float32
    )
    grad_scores = (probs * (grad_probs - delta[..., None])).astype(jnp.bfloat16)
    grad_query = (
        jnp.einsum("hcqk,hckd->hcqd", grad_scores, key_cells, preferred_element_type=jnp.float32)
        * score_scale
    ).astype(jnp.bfloat16)
    grad_key = (
        jnp.einsum("hcqk,hcqd->hckd", grad_scores, query_cells, preferred_element_type=jnp.float32)
        * score_scale
    ).astype(jnp.bfloat16)
    back_query, back_key, back_value = (
        lax.all_to_all(to_returns(grad_query), "seq", split_axis=0, concat_axis=0, tiled=True),
        lax.all_to_all(to_returns(grad_key), "seq", split_axis=0, concat_axis=0, tiled=True),
        lax.all_to_all(to_returns(grad_value), "seq", split_axis=0, concat_axis=0, tiled=True),
    )
    return (mixed, from_buffer(back_query), from_buffer(back_key), from_buffer(back_value))


def solution(mesh):
    return jax.shard_map(
        shards,
        mesh=mesh,
        in_specs=(
            P("seq", "tensor"),
            P("seq", "tensor"),
            P("seq", "tensor"),
            P("tensor", "seq"),
            P("tensor", "seq"),
            P("tensor", "seq"),
            P(("seq", "tensor"), None),
        ),
        out_specs=(
            P(("seq", "tensor"), None),
            P("seq", "tensor"),
            P("seq", "tensor"),
            P("seq", "tensor"),
        ),
        check_vma=False,
    )
```

profile of v0, /device:TPU:0, one launch (start us, length us, event | category | flops | bytes accessed | tf_op | source)
XLA Modules:
  0.0 570.6 jit_solution(7814950812013451770)
XLA Ops:
  11.3 7.3 %all-to-all-start = ((s32[32,1,256]{2,1,0:T(1,128)}), s32[32,1,256]{2,1,0:T(1,128)S(1)}, u32[]{:S(2)}, u32[]{:S(2)}) async-start(s32[32,1,256]{2,1,0:T(1,128)} %reshape.167), calls=%async_computation | async-start | bytes 65536 | tf_op jit(solution)/shard_map/all_to_all | solution.py:55
  32.8 4.2 all_to_all.61
  37.0 68.6 %all-to-all-done.1 = bf16[32,8,4096]{2,1,0:T(8,128)(2,1)S(1)} async-done(((bf16[32,8,4096]{2,1,0:T(8,128)(2,1)}), bf16[32,8,4096]{2,1,0:T(8,128)(2,1)S(1)}, u32[]{:S(2)}, u32[]{:S(2)}) %all-to-all-start.1) | async-done | bytes 2097184 | tf_op jit(solution)/shard_map/all_to_all | solution.py:57
  105.5 3.5 all-to-all-start.2
  112.7 4.2 all_to_all.63
  117.0 80.9 %all-to-all-done.2 = bf16[32,8,4096]{2,1,0:T(8,128)(2,1)} async-done(((bf16[32,8,4096]{2,1,0:T(8,128)(2,1)}), bf16[32,8,4096]{2,1,0:T(8,128)(2,1)}, u32[]{:S(2)}, u32[]{:S(2)}) %all-to-all-start.2) | async-done | bytes 2097184 | tf_op jit(solution)/shard_map/all_to_all | solution.py:58
  197.9 14.0 %all-to-all-start.3 = ((bf16[32,8,4096]{2,1,0:T(8,128)(2,1)}), bf16[32,8,4096]{2,1,0:T(8,128)(2,1)}, u32[]{:S(2)}, u32[]{:S(2)}) async-start(bf16[32,8,4096]{2,1,0:T(8,128)(2,1)} %all_to_all.63), calls=%async_computation.3 | async-start | bytes 4194304 | tf_op jit(solution)/shard_map/all_to_all | solution.py:59
  211.9 9.1 %convolution_convert_fusion = bf16[128,4096]{1,0:T(8,128)(2,1)} fusion(bf16[128,2048]{1,0:T(8,128)(2,1)S(1)} %copy-done.4, bf16[4096,2048]{0,1:T(8,128)(2,1)} %all-gather.2.cloned.1.call-done), kind=kOutput, calls=%fused_computation.12 | convolution fusion | flops 2148007936 | bytes 18350080 | tf_op jit(solution)/shard_map/dot_general | solution.py:106
  225.0 4.6 copy.40
  229.6 4.2 all_to_all.67
  233.8 26.8 %all-to-all-done.3 = bf16[32,8,4096]{2,1,0:T(8,128)(2,1)} async-done(((bf16[32,8,4096]{2,1,0:T(8,128)(2,1)}), bf16[32,8,4096]{2,1,0:T(8,128)(2,1)}, u32[]{:S(2)}, u32[]{:S(2)}) %all-to-all-start.3) | async-done | bytes 2097184 | tf_op jit(solution)/shard_map/all_to_all | solution.py:59
  260.6 4.0 all-to-all-start.5
  271.9 3.5 fusion.49
  280.9 4.8 fusion.98
  285.8 27.6 %all-to-all-done.5 = bf16[32,8,4096]{2,1,0:T(8,128)(2,1)} async-done(((bf16[32,8,4096]{2,1,0:T(8,128)(2,1)}), bf16[32,8,4096]{2,1,0:T(8,128)(2,1)}, u32[]{:S(2)}, u32[]{:S(2)}) %all-to-all-start.5) | async-done | bytes 2097184 | tf_op jit(solution)/shard_map/all_to_all | solution.py:113
  326.2 4.6 copy.48
  330.8 4.2 all_to_all.71
  335.0 4.5 all-to-all-start.7
  339.6 3.6 convolution_convert_fusion.2
  346.5 4.6 copy.51
  351.1 4.2 all_to_all.73
  355.3 33.1 %all-to-all-done.7 = bf16[32,8,4096]{2,1,0:T(8,128)(2,1)} async-done(((bf16[32,8,4096]{2,1,0:T(8,128)(2,1)}), bf16[32,8,4096]{2,1,0:T(8,128)(2,1)}, u32[]{:S(2)}, u32[]{:S(2)}) %all-to-all-start.7) | async-done | bytes 2097184 | tf_op jit(solution)/shard_map/all_to_all | solution.py:138
  388.4 4.1 all-to-all-start.8
  404.1 37.3 %all-to-all-done.8 = bf16[32,8,4096]{2,1,0:T(8,128)(2,1)} async-done(((bf16[32,8,4096]{2,1,0:T(8,128)(2,1)}), bf16[32,8,4096]{2,1,0:T(8,128)(2,1)}, u32[]{:S(2)}, u32[]{:S(2)}) %all-to-all-start.8) | async-done | bytes 2097184 | tf_op jit(solution)/shard_map/all_to_all | solution.py:139
  441.4 4.0 all-to-all-start.6
  445.5 4.9 convert_bitcast_fusion.4
  450.4 4.6 copy.37
  455.0 4.2 all_to_all.65
  459.1 35.2 %all-to-all-done.6 = bf16[32,8,4096]{2,1,0:T(8,128)(2,1)S(1)} async-done(((bf16[32,8,4096]{2,1,0:T(8,128)(2,1)}), bf16[32,8,4096]{2,1,0:T(8,128)(2,1)S(1)}, u32[]{:S(2)}, u32[]{:S(2)}) %all-to-all-start.6) | async-done | bytes 2097184 | tf_op jit(solution)/shard_map/all_to_all | solution.py:137
  494.4 4.3 all-to-all-start.4
  512.1 35.5 %all-to-all-done.4 = bf16[32,8,4096]{2,1,0:T(8,128)(2,1)} async-done(((bf16[32,8,4096]{2,1,0:T(8,128)(2,1)}), bf16[32,8,4096]{2,1,0:T(8,128)(2,1)}, u32[]{:S(2)}, u32[]{:S(2)}) %all-to-all-start.4) | async-done | bytes 2097184 | tf_op jit(solution)/shard_map/all_to_all | solution.py:94
  551.2 12.4 %convolution_convert_fusion.1 = bf16[128,2048]{1,0:T(8,128)(2,1)} fusion(bf16[128,4096]{0,1:T(8,128)(2,1)S(1)} %bitcast.146, bf16[4096,2048]{0,1:T(8,128)(2,1)} %all-gather.2.cloned.1.call-done), kind=kOutput, calls=%fused_computation.39 | convolution fusion | flops 2147745792 | bytes 18350080 | tf_op jit(solution)/shard_map/dot_general | solution.py:101
  (75 shorter events, 83.4 us)
Async XLA Ops:
  7.2 11.4 %copy-start = (bf16[128,4096]{1,0:T(8,128)(2,1)S(1)}, bf16[128,4096]{1,0:T(8,128)(2,1)}, u32[]{:S(2)}) copy-start(bf16[128,4096]{1,0:T(8,128)(2,1)} %param.7) | copy-start | bytes 3145732
  7.2 204.7 %all-gather.2.cloned.1.call-start = ((), (), s32[]{:S(2)}) async-start(), calls=%async_computation.9 | async-start | bytes 17301504 | tf_op jit(solution)/shard_map/all_gather | solution.py:98
  11.3 14.6 %all-to-all-start = ((s32[32,1,256]{2,1,0:T(1,128)}), s32[32,1,256]{2,1,0:T(1,128)S(1)}, u32[]{:S(2)}, u32[]{:S(2)}) async-start(s32[32,1,256]{2,1,0:T(1,128)} %reshape.167), calls=%async_computation | async-start | bytes 65536 | tf_op jit(solution)/shard_map/all_to_all | solution.py:55
  23.2 5.8 %copy-start.5 = (bf16[128,4096]{1,0:T(8,128)(2,1)S(1)}, bf16[128,4096]{1,0:T(8,128)(2,1)}, u32[]{:S(2)}) copy-start(bf16[128,4096]{1,0:T(8,128)(2,1)} %param.8) | copy-start | bytes 3145732
  25.8 79.7 %all-to-all-start.1 = ((bf16[32,8,4096]{2,1,0:T(8,128)(2,1)}), bf16[32,8,4096]{2,1,0:T(8,128)(2,1)S(1)}, u32[]{:S(2)}, u32[]{:S(2)}) async-start(bf16[32,8,4096]{2,1,0:T(8,128)(2,1)} %all_to_all.59), calls=%async_computation.1 | async-start | bytes 4194304 | tf_op jit(solution)/shard_map/all_to_all | solution.py:57
  37.0 72.1 %copy-start.6 = (bf16[128,4096]{1,0:T(8,128)(2,1)S(1)}, bf16[128,4096]{1,0:T(8,128)(2,1)}, u32[]{:S(2)}) copy-start(bf16[128,4096]{1,0:T(8,128)(2,1)} %param.9) | copy-start | bytes 3145732
  105.5 92.3 %all-to-all-start.2 = ((bf16[32,8,4096]{2,1,0:T(8,128)(2,1)}), bf16[32,8,4096]{2,1,0:T(8,128)(2,1)}, u32[]{:S(2)}, u32[]{:S(2)}) async-start(bf16[32,8,4096]{2,1,0:T(8,128)(2,1)} %all_to_all.61), calls=%async_computation.2 | async-start | bytes 4194304 | tf_op jit(solution)/shard_map/all_to_all | solution.py:58
  116.9 94.9 %copy-start.4 = (bf16[128,2048]{1,0:T(8,128)(2,1)S(1)}, bf16[128,2048]{1,0:T(8,128)(2,1)}, u32[]{:S(2)}) copy-start(bf16[128,2048]{1,0:T(8,128)(2,1)} %param.13) | copy-start | bytes 1572868
  197.9 62.7 %all-to-all-start.3 = ((bf16[32,8,4096]{2,1,0:T(8,128)(2,1)}), bf16[32,8,4096]{2,1,0:T(8,128)(2,1)}, u32[]{:S(2)}, u32[]{:S(2)}) async-start(bf16[32,8,4096]{2,1,0:T(8,128)(2,1)} %all_to_all.63), calls=%async_computation.3 | async-start | bytes 4194304 | tf_op jit(solution)/shard_map/all_to_all | solution.py:59
  260.6 52.8 %all-to-all-start.5 = ((bf16[32,8,4096]{2,1,0:T(8,128)(2,1)}), bf16[32,8,4096]{2,1,0:T(8,128)(2,1)}, u32[]{:S(2)}, u32[]{:S(2)}) async-start(bf16[32,8,4096]{2,1,0:T(8,128)(2,1)} %all_to_all.67), calls=%async_computation.5 | async-start | bytes 4194304 | tf_op jit(solution)/shard_map/all_to_all | solution.py:113
  277.4 3.5 copy-start.2
  315.5 2.1 copy-start.8
  315.5 2.8 copy-start.9
  317.5 3.0 copy-start.7
  320.6 1.6 copy-start.3
  335.0 53.4 %all-to-all-start.7 = ((bf16[32,8,4096]{2,1,0:T(8,128)(2,1)}), bf16[32,8,4096]{2,1,0:T(8,128)(2,1)}, u32[]{:S(2)}, u32[]{:S(2)}) async-start(bf16[32,8,4096]{2,1,0:T(8,128)(2,1)} %all_to_all.71), calls=%async_computation.7 | async-start | bytes 4194304 | tf_op jit(solution)/shard_map/all_to_all | solution.py:138
  388.4 53.0 %all-to-all-start.8 = ((bf16[32,8,4096]{2,1,0:T(8,128)(2,1)}), bf16[32,8,4096]{2,1,0:T(8,128)(2,1)}, u32[]{:S(2)}, u32[]{:S(2)}) async-start(bf16[32,8,4096]{2,1,0:T(8,128)(2,1)} %all_to_all.73), calls=%async_computation.8 | async-start | bytes 4194304 | tf_op jit(solution)/shard_map/all_to_all | solution.py:139
  441.4 52.9 %all-to-all-start.6 = ((bf16[32,8,4096]{2,1,0:T(8,128)(2,1)}), bf16[32,8,4096]{2,1,0:T(8,128)(2,1)S(1)}, u32[]{:S(2)}, u32[]{:S(2)}) async-start(bf16[32,8,4096]{2,1,0:T(8,128)(2,1)} %all_to_all.69), calls=%async_computation.6 | async-start | bytes 4194304 | tf_op jit(solution)/shard_map/all_to_all | solution.py:137
  494.4 53.2 %all-to-all-start.4 = ((bf16[32,8,4096]{2,1,0:T(8,128)(2,1)}), bf16[32,8,4096]{2,1,0:T(8,128)(2,1)}, u32[]{:S(2)}, u32[]{:S(2)}) async-start(bf16[32,8,4096]{2,1,0:T(8,128)(2,1)} %all_to_all.65), calls=%async_computation.4 | async-start | bytes 4194304 | tf_op jit(solution)/shard_map/all_to_all | solution.py:94
  551.2 12.4 %copy-start.1 = (bf16[128,4096]{1,0:T(8,128)(2,1)S(1)}, bf16[128,4096]{1,0:T(8,128)(2,1)}, u32[]{:S(2)}) copy-start(bf16[128,4096]{1,0:T(8,128)(2,1)} %param.7) | copy-start | bytes 3145732
Sparse Core Ops, SparseCore 0:
  10.9 186.8 all-gather.1
where the time goes:
time: 575 us; the launch traced here: 571 us
  waiting for transfers between devices  348 us (61%)
  local copies, waits for them, and re-layouts  80.2 us (14%)
  matrix products  75 us (13%)
  starting transfers between devices  49 us (9%)
  between operations  14.7 us (3%)
    all_to_all x1, waiting for transfers between devices, shards(): lax.all_to_all(to_buffer(key_rows), 'seq', split_axis=0, concat_axis=0, t...  80.9 us
    all_to_all x1, waiting for transfers between devices, shards(): lax.all_to_all(to_buffer(query_rows), 'seq', split_axis=0, concat_axis=0,...  68.6 us
    all_to_all x1, waiting for transfers between devices, shards(): lax.all_to_all(to_returns(grad_value), 'seq', split_axis=0, concat_axis=0...  37.3 us
    all_to_all x1, waiting for transfers between devices, shards(): lax.all_to_all(to_returns(attended_cells), 'seq', split_axis=0, concat_ax...  35.5 us
    all_to_all x1, waiting for transfers between devices, shards(): lax.all_to_all(to_returns(grad_query), 'seq', split_axis=0, concat_axis=0...  35.2 us
    all_to_all x1, waiting for transfers between devices, shards(): lax.all_to_all(to_returns(grad_key), 'seq', split_axis=0, concat_axis=0,...  33.1 us
    all_to_all x1, waiting for transfers between devices, shards(): lax.all_to_all(to_buffer(grad_low), 'seq', split_axis=0, concat_axis=0, t...  27.6 us
    all_to_all x1, waiting for transfers between devices, shards(): lax.all_to_all(to_buffer(value_rows), 'seq', split_axis=0, concat_axis=0,...  26.8 us
  transfers between devices with their start and end apart: 10, of which 9 were waited for; matrix products, arithmetic and copies ran while one was open for 17% of the time, Pallas kernels for 0%

commit v1 on v0

--- a/solution.py
+++ b/solution.py
@@ -1,15 +1,249 @@
+import functools
 import math
 
 import jax
 import jax.numpy as jnp
 from jax import lax
+from jax.experimental import pallas as pl
+from jax.experimental.pallas import tpu as pltpu
 from jax.sharding import PartitionSpec as P
 
 CLU_DEV = 8
 CAP = 32
-
-
-def shards(query_rows, key_rows, value_rows, cluster_id, slot_index, out_weight, grad_out):
+TILE = 64
+WIN = TILE + 2 * CAP
+VMEM_LIMIT = 48 * 1024 * 1024
+
+
+def place_kernel(clusters, ids_ref, pos_ref, seg_rows_ref, seg_cols_ref):
+    blocks, lanes = pos_ref.shape
+    bf, f32 = jnp.bfloat16, jnp.float32
+    cluster_ids = lax.broadcasted_iota(jnp.int32, (clusters, lanes), 0).astype(f32)
+    slot_ids = lax.broadcasted_iota(jnp.int32, (CAP, lanes), 0).astype(f32)
+
+    def tables(b):
+        held = ids_ref[b].astype(f32)
+        cluster = held[0:1] * lanes + held[1:2]
+        return (
+            jnp.where(cluster_ids == cluster, 1.0, 0.0),
+            jnp.where(slot_ids == held[2:3], 1.0, 0.0),
+        )
+
+    def count(b, occupied):
+        by_cluster, by_slot = tables(b)
+        return occupied + lax.dot_general(
+            by_cluster.astype(bf), by_slot.astype(bf), (((1,), (1,)), ((), ())),
+            preferred_element_type=f32,
+        )
+
+    occupied = lax.fori_loop(0, blocks, count, jnp.zeros((clusters, CAP), f32))
+    occupied_low = occupied.astype(bf)
+    slot_from = lax.broadcasted_iota(jnp.int32, (CAP, CAP), 0)
+    slot_to = lax.broadcasted_iota(jnp.int32, (CAP, CAP), 1)
+    within = jnp.dot(
+        occupied_low, jnp.where(slot_from < slot_to, 1.0, 0.0).astype(bf),
+        preferred_element_type=f32,
+    )
+    size_col = jnp.sum(occupied, axis=1, keepdims=True)
+    sizes = jnp.broadcast_to(size_col, (clusters, 128)).astype(bf)
+    row_ids = lax.broadcasted_iota(jnp.int32, (clusters, clusters), 0)
+    col_ids = lax.broadcasted_iota(jnp.int32, (clusters, clusters), 1)
+    before = jnp.where(col_ids < row_ids, 1.0, 0.0).astype(bf)
+    start = jnp.dot(before, sizes, preferred_element_type=f32)
+    ends_col = start[:, 0:1] + size_col
+    upto = jnp.where(row_ids <= col_ids, 1.0, 0.0).astype(bf)
+    ends_row = lax.dot_general(
+        sizes, upto, (((0,), (0,)), ((), ())), preferred_element_type=f32
+    )[0:1]
+    high = jnp.floor(start * (1.0 / 64.0))
+    low = start - high * 64.0
+    high_low, low_low, within_low = high.astype(bf), low.astype(bf), within.astype(bf)
+    dims = (((0,), (0,)), ((), ()))
+
+    def place(b, carry):
+        by_cluster, by_slot = tables(b)
+        by_cluster = by_cluster.astype(bf)
+        high_of = lax.dot_general(high_low, by_cluster, dims, preferred_element_type=f32)[0:1]
+        low_of = lax.dot_general(low_low, by_cluster, dims, preferred_element_type=f32)[0:1]
+        within_of = lax.dot_general(within_low, by_cluster, dims, preferred_element_type=f32)
+        inner = jnp.sum(within_of * by_slot, axis=0, keepdims=True)
+        pos_ref[pl.ds(b, 1), :] = (high_of * 64.0 + low_of + inner).astype(jnp.int32)
+        return carry
+
+    lax.fori_loop(0, blocks, place, 0)
+    rows = blocks * lanes
+
+    def label_rows(t, carry):
+        at = (t * TILE + lax.broadcasted_iota(jnp.int32, (TILE, clusters), 0)).astype(f32)
+        label = jnp.sum(jnp.where(ends_row <= at, 1.0, 0.0), axis=1, keepdims=True)
+        seg_rows_ref[pl.ds(pl.multiple_of(t * TILE, TILE), TILE), :] = label
+        wide = t * TILE - CAP + lax.broadcasted_iota(jnp.int32, (clusters, WIN), 1)
+        label = jnp.sum(jnp.where(ends_col <= wide.astype(f32), 1.0, 0.0), axis=0, keepdims=True)
+        spot = wide[0:1]
+        seg_cols_ref[t] = jnp.where((spot >= 0) & (spot < rows), label, -1.0)
+        return carry
+
+    lax.fori_loop(0, rows // TILE, label_rows, 0)
+
+
+def place(ids, clusters):
+    blocks, _, lanes = ids.shape
+    rows = blocks * lanes
+    vmem = pl.BlockSpec(memory_space=pltpu.VMEM)
+    return pl.pallas_call(
+        functools.partial(place_kernel, clusters),
+        out_shape=(
+            jax.ShapeDtypeStruct((blocks, lanes), jnp.int32),
+            jax.ShapeDtypeStruct((rows, 1), jnp.float32),
+            jax.ShapeDtypeStruct((rows // TILE, 1, WIN), jnp.float32),
+        ),
+        in_specs=[vmem],
+        out_specs=(vmem, vmem, vmem),
+        compiler_params=pltpu.CompilerParams(vmem_limit_bytes=VMEM_LIMIT),
+        name="place",
+    )(ids)
+
+
+ROWS_AT_ONCE = 16
+
+
+def move_in(pos_ref, block_of, load, wide, sorted_ref):
+    blocks, lanes = pos_ref.shape
+
+    def one(b, carry):
+        wide[...] = load(block_of(b)).astype(jnp.float32)
+        for first in range(0, lanes, ROWS_AT_ONCE):
+            held = [wide[pl.ds(first + r, 1), :] for r in range(ROWS_AT_ONCE)]
+            for r in range(ROWS_AT_ONCE):
+                sorted_ref[pl.ds(pos_ref[b, first + r] + CAP, 1), :] = held[r]
+        return carry
+
+    lax.fori_loop(0, blocks, one, 0)
+
+
+def move_out(pos_ref, block_of, sorted_ref, offset, wide, store):
+    blocks, lanes = pos_ref.shape
+
+    def one(b, carry):
+        for first in range(0, lanes, ROWS_AT_ONCE):
+            held = [
+                sorted_ref[pl.ds(pos_ref[b, first + r] + offset, 1), :]
+                for r in range(ROWS_AT_ONCE)
+            ]
+            for r in range(ROWS_AT_ONCE):
+                wide[pl.ds(first + r, 1), :] = held[r]
+        store(block_of(b), wide[...])
+        return carry
+
+    lax.fori_loop(0, blocks, one, 0)
+
+
+def attend_kernel(
+    high, scale, unroll,
+    pos_ref, qkv_ref, grad_ref, seg_rows_ref, seg_cols_ref,
+    attended_ref, grads_ref,
+    wide, query, key, value, grad, att, grad_query, grad_key, grad_value,
+):
+    bf, f32 = jnp.bfloat16, jnp.float32
+    blocks, lanes = pos_ref.shape
+    rows = blocks * lanes
+    low = blocks // high
+
+    def straight(b):
+        return b
+
+    def swapped(b):
+        return lax.rem(b, low) * high + b // low
+
+    edge = jnp.zeros((CAP, wide.shape[1]), f32)
+    for ref in (query, key, value, grad):
+        ref[pl.ds(0, CAP), :] = edge
+        ref[pl.ds(rows + CAP, CAP), :] = edge
+    for part, ref in enumerate((query, key, value)):
+        move_in(
+            pos_ref, straight,
+            lambda b, part=part: qkv_ref[b, pl.ds(part * lanes, lanes), :], wide, ref,
+        )
+    move_in(pos_ref, swapped, lambda b: grad_ref[b], wide, grad)
+    grad_key[...] = jnp.zeros_like(grad_key)
+    grad_value[...] = jnp.zeros_like(grad_value)
+    nt = (((1,), (1,)), ((), ()))
+    tn = (((0,), (0,)), ((), ()))
+
+    def one_tile(t):
+        base = pl.multiple_of(t * TILE, TILE)
+        mine = pl.ds(pl.multiple_of(base + CAP, CAP), TILE)
+        window = pl.ds(base, WIN)
+        q = query[mine, :].astype(bf)
+        g = grad[mine, :].astype(bf)
+        k = key[window, :].astype(bf)
+        v = value[window, :].astype(bf)
+        same = seg_rows_ref[pl.ds(base, TILE), :] == seg_cols_ref[t]
+        scores = lax.dot_general(q, k, nt, preferred_element_type=f32) * scale
+        scores = jnp.where(same, scores, -1e30)
+        top = jnp.max(scores, axis=1, keepdims=True)
+        weights = jnp.exp(scores - top)
+        probs = weights / jnp.sum(weights, axis=1, keepdims=True)
+        probs_low = probs.astype(bf)
+        attended = jnp.dot(probs_low, v, preferred_element_type=f32).astype(bf).astype(f32)
+        att[pl.ds(base, TILE), :] = attended
+        delta = jnp.sum(g.astype(f32) * attended, axis=1, keepdims=True)
+        grad_probs = lax.dot_general(g, v, nt, preferred_element_type=f32)
+        grad_scores = (probs * (grad_probs - delta)).astype(bf)
+        grad_query[pl.ds(base, TILE), :] = jnp.dot(grad_scores, k, preferred_element_type=f32)
+        more_key = lax.dot_general(grad_scores, q, tn, preferred_element_type=f32)
+        more_value = lax.dot_general(probs_low, g, tn, preferred_element_type=f32)
+        return window, more_key, more_value
+
+    def tiles(step, carry):
+        for window, more_key, more_value in [one_tile(step * unroll + u) for u in range(unroll)]:
+            grad_key[window, :] += more_key
+            grad_value[window, :] += more_value
+        return carry
+
+    lax.fori_loop(0, rows // TILE // unroll, tiles, 0)
+
+    def put(part, factor):
+        def store(b, block):
+            grads_ref[b, pl.ds(part * lanes, lanes), :] = (block * factor).astype(bf)
+        return store
+
+    def put_attended(b, block):
+        attended_ref[b] = block.astype(bf)
+
+    move_out(pos_ref, swapped, att, 0, wide, put_attended)
+    move_out(pos_ref, straight, grad_query, 0, wide, put(0, scale))
+    move_out(pos_ref, straight, grad_key, CAP, wide, put(1, scale))
+    move_out(pos_ref, straight, grad_value, CAP, wide, put(2, 1.0))
+
+
+def attend(pos, qkv, grad, seg_rows, seg_cols, high):
+    blocks, lanes = pos.shape
+    rows = blocks * lanes
+    size = qkv.shape[-1]
+    f32 = jnp.float32
+    vmem = pl.BlockSpec(memory_space=pltpu.VMEM)
+    smem = pl.BlockSpec(memory_space=pltpu.SMEM)
+    padded = pltpu.VMEM((rows + 2 * CAP, size), f32)
+    plain = pltpu.VMEM((rows, size), f32)
+    return pl.pallas_call(
+        functools.partial(attend_kernel, high, 1.0 / math.sqrt(size), 4),
+        out_shape=(
+            jax.ShapeDtypeStruct((blocks, lanes, size), jnp.bfloat16),
+            jax.ShapeDtypeStruct((blocks, 3 * lanes, size), jnp.bfloat16),
+        ),
+        in_specs=[smem, vmem, vmem, vmem, vmem],
+        out_specs=(vmem, vmem),
+        scratch_shapes=[
+            pltpu.VMEM((lanes, size), f32),
+            padded, padded, padded, padded, plain, plain, padded, padded,
+        ],
+        compiler_params=pltpu.CompilerParams(vmem_limit_bytes=VMEM_LIMIT),
+        name="attend",
+    )(pos, qkv, grad, seg_rows, seg_cols)
+
+
+def by_clusters(query_rows, key_rows, value_rows, cluster_id, slot_index, out_weight, grad_out):
     rows_dev = query_rows.shape[0]
     heads_dev = cluster_id.shape[0]
     head_size = query_rows.shape[1] // heads_dev
@@ -141,7 +375,75 @@
     return (mixed, from_buffer(back_query), from_buffer(back_key), from_buffer(back_value))
 
 
+def by_heads(query_rows, key_rows, value_rows, cluster_id, slot_index, out_weight, grad_out):
+    rows_dev, width = query_rows.shape
+    heads_dev = cluster_id.shape[0]
+    head_size = width // heads_dev
+    owners = lax.axis_size("seq")
+    columns_dev = out_weight.shape[1]
+    columns = owners * columns_dev
+    high, low = split(owners)
+    planes = [[h * low + p for p in range(low)] for h in range(high)]
+    stacks = [[h * low + p for h in range(high)] for p in range(low)]
+    bf, f32 = jnp.bfloat16, jnp.float32
+
+    def exchange(rows, groups=None):
+        return lax.all_to_all(
+            rows, "seq", split_axis=0, concat_axis=0, tiled=True, axis_index_groups=groups
+        )
+
+    def of_heads(rows):
+        return rows.reshape(rows_dev, heads_dev, head_size).transpose(1, 0, 2)
+
+    def of_rows(heads):
+        return heads.transpose(1, 0, 2).reshape(rows_dev, width)
+
+    weight_rows = out_weight.T.reshape(columns_dev, heads_dev, head_size).transpose(1, 0, 2)
+    ids = jnp.stack([cluster_id // rows_dev, cluster_id % rows_dev, slot_index], axis=1)
+    ids = jnp.pad(ids, ((0, 0), (0, 13), (0, 0))).astype(bf)
+    first = exchange(jnp.concatenate([weight_rows, ids], axis=1))
+    grad_out_stack = lax.all_gather(grad_out, "seq", axis=0, tiled=True, axis_index_groups=stacks)
+    head_weight = first[:, :columns_dev].reshape(columns, head_size)
+    plane_weight = lax.all_gather(head_weight, "seq", axis=0, axis_index_groups=planes)
+    pos, seg_rows, seg_cols = place(first[:, columns_dev:], CLU_DEV * owners)
+    qkv = exchange(
+        jnp.concatenate([of_heads(query_rows), of_heads(key_rows), of_heads(value_rows)], axis=1)
+    )
+    grad_plane = lax.dot_general(
+        plane_weight, grad_out_stack, (((1,), (1,)), ((), ())), preferred_element_type=f32
+    ).astype(bf)
+    grad_head = exchange(grad_plane.transpose(0, 2, 1), planes)
+    grad_head = grad_head.reshape(owners, rows_dev, head_size)
+    attended, grads = attend(pos, qkv, grad_head, seg_rows, seg_cols, high)
+    attended_plane = exchange(attended.reshape(low, high * rows_dev, head_size), planes)
+    back = exchange(grads)
+    partial = lax.dot_general(
+        attended_plane, plane_weight, (((0, 2), (0, 2)), ((), ())), preferred_element_type=f32
+    ).astype(bf)
+    mixed = lax.psum_scatter(
+        partial, "seq", scatter_dimension=0, tiled=True, axis_index_groups=stacks
+    )
+    grad_query, grad_key, grad_value = (
+        of_rows(back[:, part * rows_dev : (part + 1) * rows_dev]) for part in range(3)
+    )
+    return mixed, grad_query, grad_key, grad_value
+
+
+def split(owners):
+    high = 1
+    while 4 * high * high <= owners:
+        high *= 2
+    return high, owners // high
+
+
 def solution(mesh):
+    def shards(*args):
+        heads_dev = args[3].shape[0]
+        owners = lax.axis_size("seq")
+        if heads_dev == owners and lax.axis_size("tensor") == 1:
+            return by_heads(*args)
+        return by_clusters(*args)
+
     return jax.shard_map(
         shards,
         mesh=mesh,

time: 575 us -> 428 us (0.74)
  waiting for transfers between devices: 348 us -> 207 us
  Pallas kernels: 0 us -> 96.4 us
  matrix products: 75 us -> 12.1 us
  blocking collectives: 0 us -> 57.3 us
  local copies, waits for them, and re-layouts: 80.2 us -> 24.8 us
  starting transfers between devices: 49 us -> 11 us
    all_to_all x9 -> x3, waiting for transfers between devices: 348 us -> 149 us  [exchange(): lax.all_to_all(rows, 'seq', split_axis=0, concat_axis=0, tiled=True, axis...]
    pallas_call x0 -> x2, Pallas kernels: none -> 96.4 us  [the longest x1 73.7 us: attend(): pl.pallas_call(functools.partial(attend_kernel, high, 1.0 / math.sqrt(siz...]
    dot_general x25 -> x2, matrix products: 70.1 us -> 12.1 us  [the longest x1 6.22 us: by_heads(): lax.dot_general(plane_weight, grad_out_stack, (((1,), (1,)), ((), ())), p...]
    all_gather x1 -> x2, waiting for transfers between devices: 0.02 us -> 57.6 us  [the longest x1 38.1 us: by_heads(): lax.all_gather(head_weight, 'seq', axis=0, axis_index_groups=planes)]
    all_to_all x0 -> x2, blocking collectives: none -> 57.3 us  [exchange(): lax.all_to_all(rows, 'seq', split_axis=0, concat_axis=0, tiled=True, axis...]
    all_to_all x9 -> x3, starting transfers between devices: 49 us -> 10.9 us  [exchange(): lax.all_to_all(rows, 'seq', split_axis=0, concat_axis=0, tiled=True, axis...]
    all_to_all x9 -> x1, local copies, waits for them, and re-layouts: 30.4 us -> 0.65 us  [exchange(): lax.all_to_all(rows, 'seq', split_axis=0, concat_axis=0, tiled=True, axis...]
    convert_element_type x8 -> x0, local copies, waits for them, and re-layouts: 28.5 us -> none  [the longest x4 17.2 us: to_returns(): picked = jnp.einsum('hrb,hrd->bhd', cell_table, flat, preferred_element_t...]
  transfers between devices with their start and end apart: 10 -> 6, of which waited for: 9 -> 5; matrix products, arithmetic and copies ran while one was open for 17% -> 8% of each run, Pallas kernels for 0% -> 5%
where the time goes in v1:
time: 428 us
  waiting for transfers between devices  207 us (48%)
  Pallas kernels  96.4 us (23%)
  blocking collectives  57.3 us (13%)
  local copies, waits for them, and re-layouts  24.8 us (6%)
  between operations  13.9 us (3%)
  matrix products  12.1 us (3%)
  starting transfers between devices  11 us (3%)
  other arithmetic  4.83 us (1%)
    all_to_all x3, waiting for transfers between devices, exchange(): lax.all_to_all(rows, 'seq', split_axis=0, concat_axis=0, tiled=True, axis...  149 us
    pallas_call x1, Pallas kernels, attend(): pl.pallas_call(functools.partial(attend_kernel, high, 1.0 / math.sqrt(siz...  73.7 us
    all_to_all x2, blocking collectives, exchange(): lax.all_to_all(rows, 'seq', split_axis=0, concat_axis=0, tiled=True, axis...  57.3 us
    all_gather x1, waiting for transfers between devices, by_heads(): lax.all_gather(head_weight, 'seq', axis=0, axis_index_groups=planes)  38.1 us
    pallas_call x1, Pallas kernels, place(): pl.pallas_call(functools.partial(place_kernel, clusters), out_shape=(jax....  22.7 us
    all_gather x1, waiting for transfers between devices, by_heads(): lax.all_gather(grad_out, 'seq', axis=0, tiled=True, axis_index_groups=sta...  19.5 us
    unnamed x12, local copies, waits for them, and re-layouts  11.7 us
    all_to_all x3, starting transfers between devices, exchange(): lax.all_to_all(rows, 'seq', split_axis=0, concat_axis=0, tiled=True, axis...  10.9 us
  transfers between devices with their start and end apart: 6, of which 5 were waited for; matrix products, arithmetic and copies ran while one was open for 8% of the time, Pallas kernels for 5%

profile of v1, /device:TPU:0, one launch (start us, length us, event | category | flops | bytes accessed | tf_op | source)
XLA Modules:
  0.0 427.7 jit_solution(3653199938652331179)
XLA Ops:
  8.0 0.7 convert_bitcast_fusion
  8.7 0.7 fusion.18
  9.8 38.8 %all_to_all.25 = bf16[32,80,128]{2,1,0:T(8,128)(2,1)S(1)} all-to-all(bf16[32,80,128]{2,1,0:T(8,128)(2,1)S(1)} %pad_maximum_fusion.1), channel_id=1, replica_groups=mesh['seq'=32,'tensor'=1] {'seq'}, dimensions={0} | all-to-all | bytes 1310720 | tf_op jit(solution)/shard_map/all_to_all | solution.py:391
  48.5 0.9 slice.21
  49.4 19.5 %all-gather.5.cloned.1.call-done = bf16[512,2048]{1,0:T(8,128)(2,1)} async-done(((bf16[128,2048]{1,0:T(8,128)(2,1)}), bf16[512,2048]{1,0:T(8,128)(2,1)}) %all-gather.5.cloned.1.call-update) | async-done | bytes 2097168 | tf_op jit(solution)/shard_map/all_gather | solution.py:405
  69.0 38.1 %all-gather.3.cloned.1.call-done = bf16[8,2048,128]{2,1,0:T(8,128)(2,1)} async-done(((bf16[1,2048,128]{2,1,0:T(8,128)(2,1)}), bf16[8,2048,128]{2,1,0:T(8,128)(2,1)}) %all-gather.3.cloned.1.call-update) | async-done | bytes 4194320 | tf_op jit(solution)/shard_map/all_gather | solution.py:407
  107.0 6.2 %fusion.5 = bf16[8,512,128]{1,2,0:T(8,128)(2,1)} fusion(bf16[8,2048,128]{2,1,0:T(8,128)(2,1)} %all-gather.3.cloned.1.call-done, bf16[512,2048]{1,0:T(8,128)(2,1)} %all-gather.5.cloned.1.call-done), kind=kOutput, calls=%fused_computation.5 | convolution fusion | flops 2148007936 | bytes 7340032 | tf_op jit(solution)/shard_map/dot_general | solution.py:412
  113.3 3.6 all-to-all-start.2
  116.8 1.6 copy.56
  118.4 1.3 copy.57
  119.8 1.6 copy.58
  121.4 1.3 copy.59
  122.7 1.6 copy.60
  124.3 1.3 copy.61
  125.6 3.2 pad_maximum_fusion
  128.9 3.3 all-to-all-done.2
  132.2 3.8 all-to-all-start.1
  136.0 22.7 %place.1 = (s32[32,128]{1,0:T(8,128)S(1)}, f32[4096,1]{1,0:T(8,128)S(1)}, f32[64,1,128]{2,1,0:T(1,128)S(1)}) custom-call(bf16[32,16,128]{2,1,0:T(8,128)(2,1)S(1)} %slice.20.ids_ref), custom_call_target="tpu_custom_call" | custom-call | tf_op jit(solution)/shard_map/place/pallas_call | solution.py:93
  158.7 1.3 copy-done.1
  160.7 46.7 %all-to-all-done.1.qkv_ref = bf16[32,384,128]{2,1,0:T(8,128)(2,1)} async-done(((bf16[32,384,128]{2,1,0:T(8,128)(2,1)}), bf16[32,384,128]{2,1,0:T(8,128)(2,1)}, u32[]{:S(2)}, u32[]{:S(2)}) %all-to-all-start.1) | async-done | bytes 3145760 | tf_op jit(solution)/shard_map/all_to_all | solution.py:391
  207.5 1.6 copy-done.2
  209.0 73.7 %attend.1 = (bf16[32,128,128]{2,1,0:T(8,128)(2,1)S(1)}, bf16[32,384,128]{2,1,0:T(8,128)(2,1)}) custom-call(s32[32,128]{1,0:T(8,128)S(1)} %get-tuple-element.9.pos_ref, bf16[32,384,128]{2,1,0:T(8,128)(2,1)} %all-to-all-done.1.qkv_ref, bf16[32,128,128]{2,1,0:T(8,128)(2,1)S(1)} %bitcast.46, f32[4096,1]{1,0:T(8,128)S(1)} %copy-done.2, ...), custom_call_target="tpu_custom_call" | custom-call | tf_op jit(solution)/shard_map/attend/pallas_call | solution.py:229
  282.7 18.6 %all_to_all.26 = bf16[8,512,128]{2,1,0:T(8,128)(2,1)S(1)} all-to-all(bf16[8,512,128]{2,1,0:T(8,128)(2,1)S(1)} %bitcast.47), channel_id=1, replica_groups={{0,1,2,3,4,5,6,7},{8,9,10,11,12,13,14,15},{16,17,18,19,20,21,22,23},{24..., dimensions={0} | all-to-all | bytes 2097152 | tf_op jit(solution)/shard_map/all_to_all | solution.py:391
  301.3 3.5 all-to-all-start.4
  304.9 5.9 %bitcast_convert_fusion = bf16[512,2048]{1,0:T(8,128)(2,1)} fusion(bf16[8,512,128]{2,1,0:T(8,128)(2,1)S(1)} %all_to_all.26, bf16[8,2048,128]{2,1,0:T(8,128)(2,1)} %all-gather.3.cloned.1.call-done), kind=kOutput, calls=%fused_computation | convolution fusion | flops 2148532224 | bytes 7340032 | tf_op jit(solution)/shard_map/dot_general | solution.py:420
  310.8 98.9 %all-to-all-done.4 = bf16[32,384,128]{2,1,0:T(8,128)(2,1)} async-done(((bf16[32,384,128]{2,1,0:T(8,128)(2,1)}), bf16[32,384,128]{2,1,0:T(8,128)(2,1)}, u32[]{:S(2)}, u32[]{:S(2)}) %all-to-all-start.4) | async-done | bytes 3145760 | tf_op jit(solution)/shard_map/all_to_all | solution.py:391
  409.7 3.5 slice_bitcast_fusion
  413.3 1.6 copy.66
  414.9 1.3 copy.69
  416.2 1.6 copy.65
  417.8 1.3 copy.68
  419.8 1.3 copy.67
  (20 shorter events, 2.5 us)
Async XLA Ops:
  7.2 2.4 copy-start
  7.2 61.8 %all-gather.5.cloned.1.call-start = ((), (), s32[]{:S(2)}) async-start(), calls=%async_computation.7 | async-start | bytes 2621440 | tf_op jit(solution)/shard_map/all_gather | solution.py:405
  7.9 99.1 %all-gather.3.cloned.1.call-start = ((), (), s32[]{:S(2)}) async-start(), calls=%async_computation.6 | async-start | bytes 4718592 | tf_op jit(solution)/shard_map/all_gather | solution.py:407
  113.3 18.9 %all-to-all-start.2 = ((bf16[8,512,128]{1,2,0:T(8,128)(2,1)}), bf16[8,512,128]{1,2,0:T(8,128)(2,1)S(1)}, u32[]{:S(2)}, u32[]{:S(2)}) async-start(bf16[8,512,128]{1,2,0:T(8,128)(2,1)} %fusion.5), calls=%async_computation.2 | async-start | bytes 2097152 | tf_op jit(solution)/shard_map/all_to_all | solution.py:391
  132.2 75.3 %all-to-all-start.1 = ((bf16[32,384,128]{2,1,0:T(8,128)(2,1)}), bf16[32,384,128]{2,1,0:T(8,128)(2,1)}, u32[]{:S(2)}, u32[]{:S(2)}) async-start(bf16[32,384,128]{2,1,0:T(8,128)(2,1)} %pad_maximum_fusion), calls=%async_computation.1 | async-start | bytes 6291456 | tf_op jit(solution)/shard_map/all_to_all | solution.py:391
  158.7 1.3 copy-start.1
  207.5 1.6 copy-start.2
  301.3 108.4 %all-to-all-start.4 = ((bf16[32,384,128]{2,1,0:T(8,128)(2,1)}), bf16[32,384,128]{2,1,0:T(8,128)(2,1)}, u32[]{:S(2)}, u32[]{:S(2)}) async-start(bf16[32,384,128]{2,1,0:T(8,128)(2,1)} %get-tuple-element.13), calls=%async_computation.5 | async-start | bytes 6291456 | tf_op jit(solution)/shard_map/all_to_all | solution.py:391
  304.8 116.3 %reduce-scatter.2.cloned.1.call-start = ((), (), s32[]{:S(2)}) async-start(), calls=%async_computation.8 | async-start | bytes 2621440 | tf_op jit(solution)/shard_map/reduce_scatter | solution.py:423
Sparse Core Ops, SparseCore 0:
  9.6 59.3 all-gather.4
  71.4 35.5 all-gather.2
  310.9 76.7 reduce-scatter.1

commit v2 on v1

--- a/solution.py
+++ b/solution.py
@@ -12,10 +12,16 @@
 CAP = 32
 TILE = 64
 WIN = TILE + 2 * CAP
-VMEM_LIMIT = 48 * 1024 * 1024
-
-
-def place_kernel(clusters, ids_ref, pos_ref, seg_rows_ref, seg_cols_ref):
+MASKED = -1e30
+UNROLL = 8
+VMEM = pl.BlockSpec(memory_space=pltpu.VMEM)
+SMEM = pl.BlockSpec(memory_space=pltpu.SMEM)
+PARAMS = pltpu.CompilerParams(vmem_limit_bytes=48 * 1024 * 1024)
+NT = (((1,), (1,)), ((), ()))
+TN = (((0,), (0,)), ((), ()))
+
+
+def place_kernel(clusters, ids_ref, pos_ref, bias_ref):
     blocks, lanes = pos_ref.shape
     bf, f32 = jnp.bfloat16, jnp.float32
     cluster_ids = lax.broadcasted_iota(jnp.int32, (clusters, lanes), 0).astype(f32)
@@ -73,33 +79,32 @@
     lax.fori_loop(0, blocks, place, 0)
     rows = blocks * lanes
 
-    def label_rows(t, carry):
+    def labels(t, carry):
         at = (t * TILE + lax.broadcasted_iota(jnp.int32, (TILE, clusters), 0)).astype(f32)
-        label = jnp.sum(jnp.where(ends_row <= at, 1.0, 0.0), axis=1, keepdims=True)
-        seg_rows_ref[pl.ds(pl.multiple_of(t * TILE, TILE), TILE), :] = label
+        mine = jnp.sum(jnp.where(ends_row <= at, 1.0, 0.0), axis=1, keepdims=True)
         wide = t * TILE - CAP + lax.broadcasted_iota(jnp.int32, (clusters, WIN), 1)
-        label = jnp.sum(jnp.where(ends_col <= wide.astype(f32), 1.0, 0.0), axis=0, keepdims=True)
+        other = jnp.sum(jnp.where(ends_col <= wide.astype(f32), 1.0, 0.0), axis=0, keepdims=True)
         spot = wide[0:1]
-        seg_cols_ref[t] = jnp.where((spot >= 0) & (spot < rows), label, -1.0)
+        other = jnp.where((spot >= 0) & (spot < rows), other, -1.0)
+        at = pl.ds(pl.multiple_of(t * TILE, TILE), TILE)
+        bias_ref[at, :] = jnp.where(mine == other, 0.0, MASKED).astype(bf)
         return carry
 
-    lax.fori_loop(0, rows // TILE, label_rows, 0)
+    lax.fori_loop(0, rows // TILE, labels, 0)
 
 
 def place(ids, clusters):
     blocks, _, lanes = ids.shape
     rows = blocks * lanes
-    vmem = pl.BlockSpec(memory_space=pltpu.VMEM)
     return pl.pallas_call(
         functools.partial(place_kernel, clusters),
         out_shape=(
             jax.ShapeDtypeStruct((blocks, lanes), jnp.int32),
-            jax.ShapeDtypeStruct((rows, 1), jnp.float32),
-            jax.ShapeDtypeStruct((rows // TILE, 1, WIN), jnp.float32),
+            jax.ShapeDtypeStruct((rows, WIN), jnp.bfloat16),
         ),
-        in_specs=[vmem],
-        out_specs=(vmem, vmem, vmem),
-        compiler_params=pltpu.CompilerParams(vmem_limit_bytes=VMEM_LIMIT),
+        in_specs=[VMEM],
+        out_specs=(VMEM, VMEM),
+        compiler_params=PARAMS,
         name="place",
     )(ids)
 
@@ -107,7 +112,7 @@
 ROWS_AT_ONCE = 16
 
 
-def move_in(pos_ref, block_of, load, wide, sorted_ref):
+def move_in(pos_ref, block_of, load, wide, sorted_ref, offset):
     blocks, lanes = pos_ref.shape
 
     def one(b, carry):
@@ -115,13 +120,13 @@
         for first in range(0, lanes, ROWS_AT_ONCE):
             held = [wide[pl.ds(first + r, 1), :] for r in range(ROWS_AT_ONCE)]
             for r in range(ROWS_AT_ONCE):
-                sorted_ref[pl.ds(pos_ref[b, first + r] + CAP, 1), :] = held[r]
+                sorted_ref[pl.ds(pos_ref[b, first + r] + offset, 1), :] = held[r]
         return carry
 
     lax.fori_loop(0, blocks, one, 0)
 
 
-def move_out(pos_ref, block_of, sorted_ref, offset, wide, store):
+def move_out(pos_ref, sorted_ref, offset, wide, store):
     blocks, lanes = pos_ref.shape
 
     def one(b, carry):
@@ -132,115 +137,220 @@
             ]
             for r in range(ROWS_AT_ONCE):
                 wide[pl.ds(first + r, 1), :] = held[r]
-        store(block_of(b), wide[...])
+        store(b, wide[...])
         return carry
 
     lax.fori_loop(0, blocks, one, 0)
 
 
-def attend_kernel(
-    high, scale, unroll,
-    pos_ref, qkv_ref, grad_ref, seg_rows_ref, seg_cols_ref,
-    attended_ref, grads_ref,
-    wide, query, key, value, grad, att, grad_query, grad_key, grad_value,
+def tiles_of(step):
+    bases = [pl.multiple_of((step * UNROLL + u) * TILE, TILE) for u in range(UNROLL)]
+    tiles = [pl.ds(base, TILE) for base in bases]
+    windows = [pl.ds(base, WIN) for base in bases]
+    inner = [pl.ds(pl.multiple_of(base + CAP, CAP), TILE) for base in bases]
+    return tiles, windows, inner
+
+
+def forward_kernel(
+    low, scale,
+    pos_ref, qkv_ref, bias_ref,
+    attended_ref, sorted_ref, query_ref, key_ref, value_ref, probs_ref,
+    wide, query, key, value, att,
 ):
     bf, f32 = jnp.bfloat16, jnp.float32
     blocks, lanes = pos_ref.shape
     rows = blocks * lanes
-    low = blocks // high
-
-    def straight(b):
-        return b
-
-    def swapped(b):
-        return lax.rem(b, low) * high + b // low
-
+    high = blocks // low
     edge = jnp.zeros((CAP, wide.shape[1]), f32)
-    for ref in (query, key, value, grad):
+    for part, (ref, out) in enumerate(
+        ((query, query_ref), (key, key_ref), (value, value_ref))
+    ):
         ref[pl.ds(0, CAP), :] = edge
         ref[pl.ds(rows + CAP, CAP), :] = edge
-    for part, ref in enumerate((query, key, value)):
         move_in(
-            pos_ref, straight,
-            lambda b, part=part: qkv_ref[b, pl.ds(part * lanes, lanes), :], wide, ref,
+            pos_ref, lambda b: b,
+            lambda b, part=part: qkv_ref[b, pl.ds(part * lanes, lanes), :], wide, ref, CAP,
         )
-    move_in(pos_ref, swapped, lambda b: grad_ref[b], wide, grad)
+        out[...] = ref[...].astype(bf)
+
+    def some(step, carry):
+        tiles, windows, inner = tiles_of(step)
+        qs = [query_ref[at, :] for at in inner]
+        ks = [key_ref[at, :] for at in windows]
+        vs = [value_ref[at, :] for at in windows]
+        biases = [bias_ref[at, :].astype(f32) for at in tiles]
+        scores = [lax.dot_general(q, k, NT, preferred_element_type=f32) for q, k in zip(qs, ks)]
+        scores = [s * scale + bias for s, bias in zip(scores, biases)]
+        tops = [jnp.max(s, axis=1, keepdims=True) for s in scores]
+        weights = [jnp.exp(s - top) for s, top in zip(scores, tops)]
+        sums = [jnp.sum(w, axis=1, keepdims=True) for w in weights]
+        probs = [w / total for w, total in zip(weights, sums)]
+        attended = [
+            jnp.dot(p.astype(bf), v, preferred_element_type=f32) for p, v in zip(probs, vs)
+        ]
+        for at, p, one in zip(tiles, probs, attended):
+            probs_ref[at, :] = p
+            att[at, :] = one
+            sorted_ref[at, :] = one.astype(bf)
+        return carry
+
+    lax.fori_loop(0, rows // TILE // UNROLL, some, 0)
+
+    def put(b, block):
+        attended_ref[lax.rem(b, low) * high + b // low] = block.astype(bf)
+
+    move_out(pos_ref, att, 0, wide, put)
+
+
+def forward(pos, qkv, bias, low):
+    blocks, lanes = pos.shape
+    rows = blocks * lanes
+    size = qkv.shape[-1]
+    bf = jnp.bfloat16
+    padded = jax.ShapeDtypeStruct((rows + 2 * CAP, size), bf)
+    sorted_rows = pltpu.VMEM((rows + 2 * CAP, size), jnp.float32)
+    return pl.pallas_call(
+        functools.partial(forward_kernel, low, 1.0 / math.sqrt(size)),
+        out_shape=(
+            jax.ShapeDtypeStruct((blocks, lanes, size), bf),
+            jax.ShapeDtypeStruct((rows, size), bf),
+            padded, padded, padded,
+            jax.ShapeDtypeStruct((rows, WIN), jnp.float32),
+        ),
+        in_specs=[SMEM, VMEM, VMEM],
+        out_specs=(VMEM,) * 6,
+        scratch_shapes=[
+            pltpu.VMEM((lanes, size), jnp.float32),
+            sorted_rows, sorted_rows, sorted_rows,
+            pltpu.VMEM((rows, size), jnp.float32),
+        ],
+        compiler_params=PARAMS,
+        name="forward",
+    )(pos, qkv, bias)
+
+
+def backward_kernel(
+    low, scale,
+    pos_ref, grad_ref, sorted_ref, query_ref, key_ref, value_ref, probs_ref,
+    grads_ref,
+    wide, grad, grad_query, grad_key, grad_value,
+):
+    bf, f32 = jnp.bfloat16, jnp.float32
+    blocks, lanes = pos_ref.shape
+    rows = blocks * lanes
+    high = blocks // low
+    move_in(
+        pos_ref, lambda b: lax.rem(b, low) * high + b // low,
+        lambda b: grad_ref[b], wide, grad, 0,
+    )
     grad_key[...] = jnp.zeros_like(grad_key)
     grad_value[...] = jnp.zeros_like(grad_value)
-    nt = (((1,), (1,)), ((), ()))
-    tn = (((0,), (0,)), ((), ()))
-
-    def one_tile(t):
-        base = pl.multiple_of(t * TILE, TILE)
-        mine = pl.ds(pl.multiple_of(base + CAP, CAP), TILE)
-        window = pl.ds(base, WIN)
-        q = query[mine, :].astype(bf)
-        g = grad[mine, :].astype(bf)
-        k = key[window, :].astype(bf)
-        v = value[window, :].astype(bf)
-        same = seg_rows_ref[pl.ds(base, TILE), :] == seg_cols_ref[t]
-        scores = lax.dot_general(q, k, nt, preferred_element_type=f32) * scale
-        scores = jnp.where(same, scores, -1e30)
-        top = jnp.max(scores, axis=1, keepdims=True)
-        weights = jnp.exp(scores - top)
-        probs = weights / jnp.sum(weights, axis=1, keepdims=True)
-        probs_low = probs.astype(bf)
-        attended = jnp.dot(probs_low, v, preferred_element_type=f32).astype(bf).astype(f32)
-        att[pl.ds(base, TILE), :] = attended
-        delta = jnp.sum(g.astype(f32) * attended, axis=1, keepdims=True)
-        grad_probs = lax.dot_general(g, v, nt, preferred_element_type=f32)
-        grad_scores = (probs * (grad_probs - delta)).astype(bf)
-        grad_query[pl.ds(base, TILE), :] = jnp.dot(grad_scores, k, preferred_element_type=f32)
-        more_key = lax.dot_general(grad_scores, q, tn, preferred_element_type=f32)
-        more_value = lax.dot_general(probs_low, g, tn, preferred_element_type=f32)
-        return window, more_key, more_value
-
-    def tiles(step, carry):
-        for window, more_key, more_value in [one_tile(step * unroll + u) for u in range(unroll)]:
-            grad_key[window, :] += more_key
-            grad_value[window, :] += more_value
+
+    def some(step, carry):
+        tiles, windows, inner = tiles_of(step)
+        gs = [grad[at, :].astype(bf) for at in tiles]
+        qs = [query_ref[at, :] for at in inner]
+        ks = [key_ref[at, :] for at in windows]
+        vs = [value_ref[at, :] for at in windows]
+        probs = [probs_ref[at, :] for at in tiles]
+        attended = [sorted_ref[at, :].astype(f32) for at in tiles]
+        grad_probs = [lax.dot_general(g, v, NT, preferred_element_type=f32) for g, v in zip(gs, vs)]
+        lows = [p.astype(bf) for p in probs]
+        more_values = [
+            lax.dot_general(p, g, TN, preferred_element_type=f32) for p, g in zip(lows, gs)
+        ]
+        deltas = [
+            jnp.sum(g.astype(f32) * one, axis=1, keepdims=True) for g, one in zip(gs, attended)
+        ]
+        grad_scores = [
+            (p * (gp - delta)).astype(bf) for p, gp, delta in zip(probs, grad_probs, deltas)
+        ]
+        grad_queries = [jnp.dot(d, k, preferred_element_type=f32) for d, k in zip(grad_scores, ks)]
+        more_keys = [
+            lax.dot_general(d, q, TN, preferred_element_type=f32) for d, q in zip(grad_scores, qs)
+        ]
+        for at, one in zip(tiles, grad_queries):
+            grad_query[at, :] = one
+        for at, more_key, more_value in zip(windows, more_keys, more_values):
+            grad_key[at, :] += more_key
+            grad_value[at, :] += more_value
         return carry
 
-    lax.fori_loop(0, rows // TILE // unroll, tiles, 0)
+    lax.fori_loop(0, rows // TILE // UNROLL, some, 0)
 
     def put(part, factor):
         def store(b, block):
             grads_ref[b, pl.ds(part * lanes, lanes), :] = (block * factor).astype(bf)
         return store
 
-    def put_attended(b, block):
-        attended_ref[b] = block.astype(bf)
-
-    move_out(pos_ref, swapped, att, 0, wide, put_attended)
-    move_out(pos_ref, straight, grad_query, 0, wide, put(0, scale))
-    move_out(pos_ref, straight, grad_key, CAP, wide, put(1, scale))
-    move_out(pos_ref, straight, grad_value, CAP, wide, put(2, 1.0))
-
-
-def attend(pos, qkv, grad, seg_rows, seg_cols, high):
+    move_out(pos_ref, grad_query, 0, wide, put(0, scale))
+    move_out(pos_ref, grad_key, CAP, wide, put(1, scale))
+    move_out(pos_ref, grad_value, CAP, wide, put(2, 1.0))
+
+
+def backward(pos, grad, kept, low):
     blocks, lanes = pos.shape
     rows = blocks * lanes
-    size = qkv.shape[-1]
+    size = grad.shape[-1]
     f32 = jnp.float32
-    vmem = pl.BlockSpec(memory_space=pltpu.VMEM)
-    smem = pl.BlockSpec(memory_space=pltpu.SMEM)
+    plain = pltpu.VMEM((rows, size), f32)
     padded = pltpu.VMEM((rows + 2 * CAP, size), f32)
-    plain = pltpu.VMEM((rows, size), f32)
     return pl.pallas_call(
-        functools.partial(attend_kernel, high, 1.0 / math.sqrt(size), 4),
-        out_shape=(
-            jax.ShapeDtypeStruct((blocks, lanes, size), jnp.bfloat16),
-            jax.ShapeDtypeStruct((blocks, 3 * lanes, size), jnp.bfloat16),
-        ),
-        in_specs=[smem, vmem, vmem, vmem, vmem],
-        out_specs=(vmem, vmem),
-        scratch_shapes=[
-            pltpu.VMEM((lanes, size), f32),
-            padded, padded, padded, padded, plain, plain, padded, padded,
-        ],
-        compiler_params=pltpu.CompilerParams(vmem_limit_bytes=VMEM_LIMIT),
-        name="attend",
-    )(pos, qkv, grad, seg_rows, seg_cols)
+        functools.partial(backward_kernel, low, 1.0 / math.sqrt(size)),
+        out_shape=jax.ShapeDtypeStruct((blocks, 3 * lanes, size), jnp.bfloat16),
+        in_specs=[SMEM] + [VMEM] * 6,
+        out_specs=VMEM,
+        scratch_shapes=[pltpu.VMEM((lanes, size), f32), plain, plain, padded, padded],
+        compiler_params=PARAMS,
+        name="backward",
+    )(pos, grad, *kept)
+
+
+def pack_kernel(*refs):
+    out_ref = refs[-1]
+    heads, rows, size = out_ref.shape
+    rows = rows // (len(refs) - 1)
+    for part, ref in enumerate(refs[:-1]):
+        for h in range(heads):
+            out_ref[h, pl.ds(part * rows, rows), :] = ref[:, pl.ds(h * size, size)]
+
+
+def pack(arrays, heads):
+    rows, width = arrays[0].shape
+    size = width // heads
+    step = math.gcd(heads, 8)
+    return pl.pallas_call(
+        pack_kernel,
+        grid=(heads // step,),
+        out_shape=jax.ShapeDtypeStruct((heads, len(arrays) * rows, size), arrays[0].dtype),
+        in_specs=[pl.BlockSpec((rows, step * size), lambda i: (0, i))] * len(arrays),
+        out_specs=pl.BlockSpec((step, len(arrays) * rows, size), lambda i: (i, 0, 0)),
+        compiler_params=PARAMS,
+        name="pack",
+    )(*arrays)
+
+
+def unpack_kernel(in_ref, *refs):
+    heads, rows, size = in_ref.shape
+    rows = rows // len(refs)
+    for part, ref in enumerate(refs):
+        for h in range(heads):
+            ref[:, pl.ds(h * size, size)] = in_ref[h, pl.ds(part * rows, rows), :]
+
+
+def unpack(packed, parts):
+    heads, rows, size = packed.shape
+    rows = rows // parts
+    step = math.gcd(heads, 8)
+    return pl.pallas_call(
+        unpack_kernel,
+        grid=(heads // step,),
+        out_shape=(jax.ShapeDtypeStruct((rows, heads * size), packed.dtype),) * parts,
+        in_specs=[pl.BlockSpec((step, parts * rows, size), lambda i: (i, 0, 0))],
+        out_specs=(pl.BlockSpec((rows, step * size), lambda i: (0, i)),) * parts,
+        compiler_params=PARAMS,
+        name="unpack",
+    )(packed)
 
 
 def by_clusters(query_rows, key_rows, value_rows, cluster_id, slot_index, out_weight, grad_out):
@@ -392,30 +502,26 @@
             rows, "seq", split_axis=0, concat_axis=0, tiled=True, axis_index_groups=groups
         )
 
-    def of_heads(rows):
-        return rows.reshape(rows_dev, heads_dev, head_size).transpose(1, 0, 2)
-
-    def of_rows(heads):
-        return heads.transpose(1, 0, 2).reshape(rows_dev, width)
-
     weight_rows = out_weight.T.reshape(columns_dev, heads_dev, head_size).transpose(1, 0, 2)
     ids = jnp.stack([cluster_id // rows_dev, cluster_id % rows_dev, slot_index], axis=1)
     ids = jnp.pad(ids, ((0, 0), (0, 13), (0, 0))).astype(bf)
     first = exchange(jnp.concatenate([weight_rows, ids], axis=1))
     grad_out_stack = lax.all_gather(grad_out, "seq", axis=0, tiled=True, axis_index_groups=stacks)
+    packed = pack((query_rows, key_rows, value_rows), heads_dev)
+    packed, first = lax.optimization_barrier((packed, first))
+    qkv = exchange(packed)
     head_weight = first[:, :columns_dev].reshape(columns, head_size)
     plane_weight = lax.all_gather(head_weight, "seq", axis=0, axis_index_groups=planes)
-    pos, seg_rows, seg_cols = place(first[:, columns_dev:], CLU_DEV * owners)
-    qkv = exchange(
-        jnp.concatenate([of_heads(query_rows), of_heads(key_rows), of_heads(value_rows)], axis=1)
-    )
+    pos, bias = place(first[:, columns_dev:], CLU_DEV * owners)
     grad_plane = lax.dot_general(
         plane_weight, grad_out_stack, (((1,), (1,)), ((), ())), preferred_element_type=f32
     ).astype(bf)
-    grad_head = exchange(grad_plane.transpose(0, 2, 1), planes)
-    grad_head = grad_head.reshape(owners, rows_dev, head_size)
-    attended, grads = attend(pos, qkv, grad_head, seg_rows, seg_cols, high)
+    grad_plane = grad_plane.transpose(0, 2, 1)
+    grad_plane, qkv = lax.optimization_barrier((grad_plane, qkv))
+    grad_head = exchange(grad_plane, planes).reshape(owners, rows_dev, head_size)
+    attended, *kept = forward(pos, qkv, bias, low)
     attended_plane = exchange(attended.reshape(low, high * rows_dev, head_size), planes)
+    grads = backward(pos, grad_head, kept, low)
     back = exchange(grads)
     partial = lax.dot_general(
         attended_plane, plane_weight, (((0, 2), (0, 2)), ((), ())), preferred_element_type=f32
@@ -423,10 +529,7 @@
     mixed = lax.psum_scatter(
         partial, "seq", scatter_dimension=0, tiled=True, axis_index_groups=stacks
     )
-    grad_query, grad_key, grad_value = (
-        of_rows(back[:, part * rows_dev : (part + 1) * rows_dev]) for part in range(3)
-    )
-    return mixed, grad_query, grad_key, grad_value
+    return (mixed, *unpack(back, 3))
 
 
 def split(owners):

time: 428 us -> 355 us (0.83)
  blocking collectives: 57.3 us -> 0 us
  Pallas kernels: 96.4 us -> 76.6 us
  starting transfers between devices: 11 us -> 27.1 us
  local copies, waits for them, and re-layouts: 24.8 us -> 10.6 us
    all_to_all x2 -> x0, blocking collectives: 57.3 us -> none  [exchange(): lax.all_to_all(rows, 'seq', split_axis=0, concat_axis=0, tiled=True, axis...]
    all_to_all x3 -> x5, waiting for transfers between devices: 149 us -> 127 us  [exchange(): lax.all_to_all(rows, 'seq', split_axis=0, concat_axis=0, tiled=True, axis...]
    pallas_call x1 -> x4, Pallas kernels: 73.7 us -> 53.7 us  [the longest x1 23.3 us: backward(): pl.pallas_call(functools.partial(backward_kernel, low, 1.0 / math.sqrt(si...]
    all_to_all x3 -> x5, starting transfers between devices: 10.9 us -> 27 us  [exchange(): lax.all_to_all(rows, 'seq', split_axis=0, concat_axis=0, tiled=True, axis...]
    all_gather x1, waiting for transfers between devices: 38.1 us -> 52.1 us  [by_heads(): lax.all_gather(head_weight, 'seq', axis=0, axis_index_groups=planes)]
    all_gather x1, waiting for transfers between devices: 19.5 us -> 31 us  [by_heads(): lax.all_gather(grad_out, 'seq', axis=0, tiled=True, axis_index_groups=sta...]
    transpose x4 -> x0, local copies, waits for them, and re-layouts: 7.41 us -> none  [of_rows(): return heads.transpose(1, 0, 2).reshape(rows_dev, width)]
    unnamed x12 -> x20, local copies, waits for them, and re-layouts: 11.7 us -> 7.93 us
  transfers between devices with their start and end apart: 6 -> 8, of which waited for: 5 -> 4; matrix products, arithmetic and copies ran while one was open for 8% -> 5% of each run, Pallas kernels for 5% -> 22%
where the time goes in v2:
time: 355 us; the launch traced here: 354 us
  waiting for transfers between devices  211 us (59%)
  Pallas kernels  76.6 us (22%)
  starting transfers between devices  27.1 us (8%)
  between operations  13.9 us (4%)
  matrix products  12.5 us (4%)
  local copies, waits for them, and re-layouts  10.6 us (3%)
    all_to_all x5, waiting for transfers between devices, exchange(): lax.all_to_all(rows, 'seq', split_axis=0, concat_axis=0, tiled=True, axis...  127 us
    all_gather x1, waiting for transfers between devices, by_heads(): lax.all_gather(head_weight, 'seq', axis=0, axis_index_groups=planes)  52.1 us
    all_gather x1, waiting for transfers between devices, by_heads(): lax.all_gather(grad_out, 'seq', axis=0, tiled=True, axis_index_groups=sta...  31 us
    all_to_all x5, starting transfers between devices, exchange(): lax.all_to_all(rows, 'seq', split_axis=0, concat_axis=0, tiled=True, axis...  27 us
    pallas_call x1, Pallas kernels, backward(): pl.pallas_call(functools.partial(backward_kernel, low, 1.0 / math.sqrt(si...  23.3 us
    pallas_call x1, Pallas kernels, forward(): pl.pallas_call(functools.partial(forward_kernel, low, 1.0 / math.sqrt(siz...  23.3 us
    pallas_call x1, Pallas kernels, place(): pl.pallas_call(functools.partial(place_kernel, clusters), out_shape=(jax....  22.9 us
    unnamed x20, local copies, waits for them, and re-layouts  7.93 us
  transfers between devices with their start and end apart: 8, of which 4 were waited for; matrix products, arithmetic and copies ran while one was open for 5% of the time, Pallas kernels for 22%

profile of v2, /device:TPU:0, one launch (start us, length us, event | category | flops | bytes accessed | tf_op | source)
XLA Modules:
  0.0 353.9 jit_solution(6357328632491984584)
XLA Ops:
  7.2 0.7 all-gather.5.cloned.1.call-update
  7.9 0.9 convert_bitcast_fusion
  8.8 0.7 fusion.18
  9.6 0.1 fusion.12
  9.7 0.1 bitcast_bitcast_fusion
  9.9 0.9 pad_maximum_fusion
  10.7 7.3 %all-to-all-start = ((bf16[32,80,128]{2,1,0:T(8,128)(2,1)}), bf16[32,80,128]{2,1,0:T(8,128)(2,1)S(1)}, u32[]{:S(2)}, u32[]{:S(2)}) async-start(bf16[32,80,128]{2,1,0:T(8,128)(2,1)} %pad_maximum_fusion), calls=%async_computation | async-start | bytes 1310720 | tf_op jit(solution)/shard_map/all_to_all | solution.py:501
  18.1 1.3 copy-done.8
  19.4 2.6 pack.1
  22.0 28.2 %all-to-all-done = bf16[32,80,128]{2,1,0:T(8,128)(2,1)S(1)} async-done(((bf16[32,80,128]{2,1,0:T(8,128)(2,1)}), bf16[32,80,128]{2,1,0:T(8,128)(2,1)S(1)}, u32[]{:S(2)}, u32[]{:S(2)}) %all-to-all-start) | async-done | bytes 655392 | tf_op jit(solution)/shard_map/all_to_all | solution.py:501
  50.2 0.9 slice.7
  51.0 6.5 %all-to-all-start.1 = ((bf16[32,384,128]{2,1,0:T(8,128)(2,1)}), bf16[32,384,128]{2,1,0:T(8,128)(2,1)}, u32[]{:S(2)}, u32[]{:S(2)}) async-start(bf16[32,384,128]{2,1,0:T(8,128)(2,1)} %pack.1), calls=%async_computation.1 | async-start | bytes 6291456 | tf_op jit(solution)/shard_map/all_to_all | solution.py:501
  57.6 31.0 %all-gather.5.cloned.1.call-done = bf16[512,2048]{1,0:T(8,128)(2,1)} async-done(((bf16[128,2048]{1,0:T(8,128)(2,1)}), bf16[512,2048]{1,0:T(8,128)(2,1)}) %all-gather.5.cloned.1.call-update) | async-done | bytes 2097168 | tf_op jit(solution)/shard_map/all_gather | solution.py:509
  88.5 52.1 %all-gather.3.cloned.1.call-done = bf16[8,2048,128]{2,1,0:T(8,128)(2,1)} async-done(((bf16[1,2048,128]{2,1,0:T(8,128)(2,1)}), bf16[8,2048,128]{2,1,0:T(8,128)(2,1)}) %all-gather.3.cloned.1.call-update) | async-done | bytes 4194320 | tf_op jit(solution)/shard_map/all_gather | solution.py:514
  140.7 6.2 %fusion.5 = bf16[8,512,128]{1,2,0:T(8,128)(2,1)} fusion(bf16[8,2048,128]{2,1,0:T(8,128)(2,1)} %all-gather.3.cloned.1.call-done, bf16[512,2048]{1,0:T(8,128)(2,1)} %all-gather.5.cloned.1.call-done), kind=kOutput, calls=%fused_computation.4 | convolution fusion | flops 2148007936 | bytes 7340032 | tf_op jit(solution)/shard_map/dot_general | solution.py:516
  146.9 3.6 %all-to-all-start.3 = ((bf16[8,512,128]{1,2,0:T(8,128)(2,1)}), bf16[8,512,128]{1,2,0:T(8,128)(2,1)S(1)}, u32[]{:S(2)}, u32[]{:S(2)}) async-start(bf16[8,512,128]{1,2,0:T(8,128)(2,1)} %fusion.5), calls=%async_computation.4 | async-start | bytes 2097152 | tf_op jit(solution)/shard_map/all_to_all | solution.py:501
  150.5 22.9 %place.1 = (s32[32,128]{1,0:T(8,128)S(1)}, bf16[4096,128]{1,0:T(8,128)(2,1)S(1)}) custom-call(bf16[32,16,128]{2,1,0:T(8,128)(2,1)S(1)} %slice.6.ids_ref), custom_call_target="tpu_custom_call" | custom-call | tf_op jit(solution)/shard_map/place/pallas_call | solution.py:99
  173.4 23.3 %forward.1 = (bf16[32,128,128]{2,1,0:T(8,128)(2,1)}, bf16[4096,128]{1,0:T(8,128)(2,1)S(1)}, bf16[4160,128]{1,0:T(8,128)(2,1)S(1)}, bf16[4160,128]{1,0:T(8,128)(2...) custom-call(s32[32,128]{1,0:T(8,128)S(1)} %get-tuple-element.20.pos_ref, ...), custom_call_target="tpu_custom_call" | custom-call | tf_op jit(solution)/shard_map/forward/pallas_call | solution.py:212
  196.7 1.0 copy-done.1
  197.7 1.0 copy-done.4
  198.7 1.0 copy-done.9
  199.6 4.3 %all-to-all-start.2 = ((bf16[8,512,128]{2,1,0:T(8,128)(2,1)}), bf16[8,512,128]{2,1,0:T(8,128)(2,1)}, u32[]{:S(2)}, u32[]{:S(2)}) async-start(bf16[8,512,128]{2,1,0:T(8,128)(2,1)} %bitcast.8), calls=%async_computation.2 | async-start | bytes 2097152 | tf_op jit(solution)/shard_map/all_to_all | solution.py:501
  203.9 1.6 copy.33
  205.5 1.2 copy-done.2
  206.8 1.2 copy-done.3
  208.0 1.2 copy-done.5
  209.2 23.3 %backward.1 = bf16[32,384,128]{2,1,0:T(8,128)(2,1)} custom-call(s32[32,128]{1,0:T(8,128)S(1)} %get-tuple-element.20.pos_ref, bf16[32,128,128]{2,1,0:T(8,128)(2,1)S(1)} %bitcast.31, bf16[4096,128]{1,0:T(8,128)(2,1)S(1)} %copy-done.5, bf16[4160,128]{1,0:T(8,128)(2,1)S(1)} %get-tuple-element.27.query_ref, bf16[4160,128]{1,0:T(8,128)(2,1)S(1)} %copy-done.2, ...), custom_call_target="tpu_custom_call" | custom-call | tf_op jit(solution)/shard_map/backward/pallas_call | solution.py:298
  232.6 5.3 %all-to-all-start.4 = ((bf16[32,384,128]{2,1,0:T(8,128)(2,1)}), bf16[32,384,128]{2,1,0:T(8,128)(2,1)}, u32[]{:S(2)}, u32[]{:S(2)}) async-start(bf16[32,384,128]{2,1,0:T(8,128)(2,1)} %backward.1), calls=%async_computation.5 | async-start | bytes 6291456 | tf_op jit(solution)/shard_map/all_to_all | solution.py:501
  237.9 0.0 reduce-scatter.2.cloned.1.call-start
  238.0 6.2 %bitcast_convert_fusion = bf16[512,2048]{1,0:T(8,128)(2,1)} fusion(bf16[8,512,128]{2,1,0:T(8,128)(2,1)} %all-to-all-done.2, bf16[8,2048,128]{2,1,0:T(8,128)(2,1)} %all-gather.3.cloned.1.call-done), kind=kOutput, calls=%fused_computation | convolution fusion | flops 2148532224 | bytes 7340032 | tf_op jit(solution)/shard_map/dot_general | solution.py:526
  244.2 98.6 %all-to-all-done.4.in_ref = bf16[32,384,128]{2,1,0:T(8,128)(2,1)} async-done(((bf16[32,384,128]{2,1,0:T(8,128)(2,1)}), bf16[32,384,128]{2,1,0:T(8,128)(2,1)}, u32[]{:S(2)}, u32[]{:S(2)}) %all-to-all-start.4) | async-done | bytes 3145760 | tf_op jit(solution)/shard_map/all_to_all | solution.py:501
  342.8 4.5 %unpack.1 = (bf16[128,4096]{1,0:T(8,128)(2,1)}, bf16[128,4096]{1,0:T(8,128)(2,1)}, bf16[128,4096]{1,0:T(8,128)(2,1)}) custom-call(bf16[32,384,128]{2,1,0:T(8,128)(2,1)} %all-to-all-done.4.in_ref), custom_call_target="tpu_custom_call" | custom-call | tf_op jit(solution)/shard_map/unpack/pallas_call | solution.py:345
  (25 shorter events, 0.2 us)
Async XLA Ops:
  7.2 2.5 copy-start
  7.2 81.3 %all-gather.5.cloned.1.call-start = ((), (), s32[]{:S(2)}) async-start(), calls=%async_computation.7 | async-start | bytes 2621440 | tf_op jit(solution)/shard_map/all_gather | solution.py:509
  7.9 10.2 %copy-start.6 = (bf16[128,4096]{1,0:T(8,128)(2,1)S(1)}, bf16[128,4096]{1,0:T(8,128)(2,1)}, u32[]{:S(2)}) copy-start(bf16[128,4096]{1,0:T(8,128)(2,1)} %refs_0_.1) | copy-start | bytes 3145732
  7.9 10.2 %copy-start.7 = (bf16[128,4096]{1,0:T(8,128)(2,1)S(1)}, bf16[128,4096]{1,0:T(8,128)(2,1)}, u32[]{:S(2)}) copy-start(bf16[128,4096]{1,0:T(8,128)(2,1)} %refs_1_.1) | copy-start | bytes 3145732
  10.7 39.4 %all-to-all-start = ((bf16[32,80,128]{2,1,0:T(8,128)(2,1)}), bf16[32,80,128]{2,1,0:T(8,128)(2,1)S(1)}, u32[]{:S(2)}, u32[]{:S(2)}) async-start(bf16[32,80,128]{2,1,0:T(8,128)(2,1)} %pad_maximum_fusion), calls=%async_computation | async-start | bytes 1310720 | tf_op jit(solution)/shard_map/all_to_all | solution.py:501
  18.1 122.6 %all-gather.3.cloned.1.call-start = ((), (), s32[]{:S(2)}) async-start(), calls=%async_computation.6 | async-start | bytes 4718592 | tf_op jit(solution)/shard_map/all_gather | solution.py:514
  18.1 1.3 copy-start.8
  51.0 95.8 %all-to-all-start.1 = ((bf16[32,384,128]{2,1,0:T(8,128)(2,1)}), bf16[32,384,128]{2,1,0:T(8,128)(2,1)}, u32[]{:S(2)}, u32[]{:S(2)}) async-start(bf16[32,384,128]{2,1,0:T(8,128)(2,1)} %pack.1), calls=%async_computation.1 | async-start | bytes 6291456 | tf_op jit(solution)/shard_map/all_to_all | solution.py:501
  146.9 51.8 %all-to-all-start.3 = ((bf16[8,512,128]{1,2,0:T(8,128)(2,1)}), bf16[8,512,128]{1,2,0:T(8,128)(2,1)S(1)}, u32[]{:S(2)}, u32[]{:S(2)}) async-start(bf16[8,512,128]{1,2,0:T(8,128)(2,1)} %fusion.5), calls=%async_computation.4 | async-start | bytes 2097152 | tf_op jit(solution)/shard_map/all_to_all | solution.py:501
  196.7 1.0 copy-start.1
  197.7 1.0 copy-start.4
  198.7 1.0 copy-start.9
  199.6 32.9 %all-to-all-start.2 = ((bf16[8,512,128]{2,1,0:T(8,128)(2,1)}), bf16[8,512,128]{2,1,0:T(8,128)(2,1)}, u32[]{:S(2)}, u32[]{:S(2)}) async-start(bf16[8,512,128]{2,1,0:T(8,128)(2,1)} %bitcast.8), calls=%async_computation.2 | async-start | bytes 2097152 | tf_op jit(solution)/shard_map/all_to_all | solution.py:501
  205.5 1.2 copy-start.2
  206.8 1.2 copy-start.3
  208.0 1.2 copy-start.5
  232.6 110.3 %all-to-all-start.4 = ((bf16[32,384,128]{2,1,0:T(8,128)(2,1)}), bf16[32,384,128]{2,1,0:T(8,128)(2,1)}, u32[]{:S(2)}, u32[]{:S(2)}) async-start(bf16[32,384,128]{2,1,0:T(8,128)(2,1)} %backward.1), calls=%async_computation.5 | async-start | bytes 6291456 | tf_op jit(solution)/shard_map/all_to_all | solution.py:501
  237.9 109.4 %reduce-scatter.2.cloned.1.call-start = ((), (), s32[]{:S(2)}) async-start(), calls=%async_computation.8 | async-start | bytes 2621440 | tf_op jit(solution)/shard_map/reduce_scatter | solution.py:529
Sparse Core Ops, SparseCore 0:
  9.6 78.8 all-gather.4
  91.0 49.6 all-gather.2
  244.4 76.7 reduce-scatter.1

commit v3 on v2

--- a/solution.py
+++ b/solution.py
@@ -17,6 +17,12 @@
 VMEM = pl.BlockSpec(memory_space=pltpu.VMEM)
 SMEM = pl.BlockSpec(memory_space=pltpu.SMEM)
 PARAMS = pltpu.CompilerParams(vmem_limit_bytes=48 * 1024 * 1024)
+
+
+def lasts(micros):
+    return pl.CostEstimate(flops=0, bytes_accessed=int(micros * 3.5e6), transcendentals=0)
+
+
 NT = (((1,), (1,)), ((), ()))
 TN = (((0,), (0,)), ((), ()))
 
@@ -35,14 +41,15 @@
             jnp.where(slot_ids == held[2:3], 1.0, 0.0),
         )
 
-    def count(b, occupied):
-        by_cluster, by_slot = tables(b)
+    def count(step, occupied):
+        some = [tables(step * 4 + u) for u in range(4)]
+        by_cluster = jnp.concatenate([t[0] for t in some], axis=1).astype(bf)
+        by_slot = jnp.concatenate([t[1] for t in some], axis=1).astype(bf)
         return occupied + lax.dot_general(
-            by_cluster.astype(bf), by_slot.astype(bf), (((1,), (1,)), ((), ())),
-            preferred_element_type=f32,
+            by_cluster, by_slot, NT, preferred_element_type=f32
         )
 
-    occupied = lax.fori_loop(0, blocks, count, jnp.zeros((clusters, CAP), f32))
+    occupied = lax.fori_loop(0, blocks // 4, count, jnp.zeros((clusters, CAP), f32))
     occupied_low = occupied.astype(bf)
     slot_from = lax.broadcasted_iota(jnp.int32, (CAP, CAP), 0)
     slot_to = lax.broadcasted_iota(jnp.int32, (CAP, CAP), 1)
@@ -63,34 +70,44 @@
     )[0:1]
     high = jnp.floor(start * (1.0 / 64.0))
     low = start - high * 64.0
-    high_low, low_low, within_low = high.astype(bf), low.astype(bf), within.astype(bf)
-    dims = (((0,), (0,)), ((), ()))
-
-    def place(b, carry):
-        by_cluster, by_slot = tables(b)
-        by_cluster = by_cluster.astype(bf)
-        high_of = lax.dot_general(high_low, by_cluster, dims, preferred_element_type=f32)[0:1]
-        low_of = lax.dot_general(low_low, by_cluster, dims, preferred_element_type=f32)[0:1]
-        within_of = lax.dot_general(within_low, by_cluster, dims, preferred_element_type=f32)
-        inner = jnp.sum(within_of * by_slot, axis=0, keepdims=True)
-        pos_ref[pl.ds(b, 1), :] = (high_of * 64.0 + low_of + inner).astype(jnp.int32)
-        return carry
-
-    lax.fori_loop(0, blocks, place, 0)
+    lookup = jnp.concatenate([within, high[:, :CAP], low[:, :CAP]], axis=1).astype(bf)
+
+    def find(step, carry):
+        some = [tables(step * 4 + u) for u in range(4)]
+        found = [
+            lax.dot_general(lookup, by_cluster.astype(bf), TN, preferred_element_type=f32)
+            for by_cluster, _ in some
+        ]
+        for u in range(4):
+            inner = jnp.sum(found[u][:CAP] * some[u][1], axis=0, keepdims=True)
+            outer = found[u][CAP : CAP + 1] * 64.0 + found[u][2 * CAP : 2 * CAP + 1]
+            pos_ref[pl.ds(step * 4 + u, 1), :] = (outer + inner).astype(jnp.int32)
+        return carry
+
+    lax.fori_loop(0, blocks // 4, find, 0)
     rows = blocks * lanes
 
-    def labels(t, carry):
-        at = (t * TILE + lax.broadcasted_iota(jnp.int32, (TILE, clusters), 0)).astype(f32)
-        mine = jnp.sum(jnp.where(ends_row <= at, 1.0, 0.0), axis=1, keepdims=True)
-        wide = t * TILE - CAP + lax.broadcasted_iota(jnp.int32, (clusters, WIN), 1)
-        other = jnp.sum(jnp.where(ends_col <= wide.astype(f32), 1.0, 0.0), axis=0, keepdims=True)
-        spot = wide[0:1]
-        other = jnp.where((spot >= 0) & (spot < rows), other, -1.0)
-        at = pl.ds(pl.multiple_of(t * TILE, TILE), TILE)
-        bias_ref[at, :] = jnp.where(mine == other, 0.0, MASKED).astype(bf)
-        return carry
-
-    lax.fori_loop(0, rows // TILE, labels, 0)
+    ones = jnp.ones((clusters, WIN), bf)
+    few = jnp.ones((8, clusters), bf)
+
+    def labels(step, carry):
+        mines, others = [], []
+        for u in range(UNROLL):
+            t = step * UNROLL + u
+            at = (t * TILE + lax.broadcasted_iota(jnp.int32, (TILE, clusters), 0)).astype(f32)
+            ended = jnp.where(ends_row <= at, 1.0, 0.0).astype(bf)
+            mines.append(jnp.dot(ended, ones, preferred_element_type=f32))
+            wide = t * TILE - CAP + lax.broadcasted_iota(jnp.int32, (clusters, WIN), 1)
+            ended = jnp.where(ends_col <= wide.astype(f32), 1.0, 0.0).astype(bf)
+            other = jnp.dot(few, ended, preferred_element_type=f32)[0:1]
+            spot = wide[0:1]
+            others.append(jnp.where((spot >= 0) & (spot < rows), other, -1.0))
+        for u in range(UNROLL):
+            at = pl.ds(pl.multiple_of((step * UNROLL + u) * TILE, TILE), TILE)
+            bias_ref[at, :] = jnp.where(mines[u] == others[u], 0.0, MASKED).astype(bf)
+        return carry
+
+    lax.fori_loop(0, rows // TILE // UNROLL, labels, 0)
 
 
 def place(ids, clusters):
@@ -105,6 +122,7 @@
         in_specs=[VMEM],
         out_specs=(VMEM, VMEM),
         compiler_params=PARAMS,
+        cost_estimate=lasts(10),
         name="place",
     )(ids)
 
@@ -112,35 +130,37 @@
 ROWS_AT_ONCE = 16
 
 
-def move_in(pos_ref, block_of, load, wide, sorted_ref, offset):
-    blocks, lanes = pos_ref.shape
-
-    def one(b, carry):
-        wide[...] = load(block_of(b)).astype(jnp.float32)
+def move_in(pos_ref, block_of, load, wide, sorted_ref, offset, count):
+    lanes = pos_ref.shape[1]
+
+    def one(r, carry):
+        b = block_of(r)
+        wide[...] = load(r).astype(jnp.float32)
         for first in range(0, lanes, ROWS_AT_ONCE):
-            held = [wide[pl.ds(first + r, 1), :] for r in range(ROWS_AT_ONCE)]
-            for r in range(ROWS_AT_ONCE):
-                sorted_ref[pl.ds(pos_ref[b, first + r] + offset, 1), :] = held[r]
-        return carry
-
-    lax.fori_loop(0, blocks, one, 0)
-
-
-def move_out(pos_ref, sorted_ref, offset, wide, store):
-    blocks, lanes = pos_ref.shape
-
-    def one(b, carry):
+            held = [wide[pl.ds(first + row, 1), :] for row in range(ROWS_AT_ONCE)]
+            for row in range(ROWS_AT_ONCE):
+                sorted_ref[pl.ds(pos_ref[b, first + row] + offset, 1), :] = held[row]
+        return carry
+
+    lax.fori_loop(0, count, one, 0)
+
+
+def move_out(pos_ref, block_of, sorted_ref, offset, wide, store, count):
+    lanes = pos_ref.shape[1]
+
+    def one(r, carry):
+        b = block_of(r)
         for first in range(0, lanes, ROWS_AT_ONCE):
             held = [
-                sorted_ref[pl.ds(pos_ref[b, first + r] + offset, 1), :]
-                for r in range(ROWS_AT_ONCE)
+                sorted_ref[pl.ds(pos_ref[b, first + row] + offset, 1), :]
+                for row in range(ROWS_AT_ONCE)
             ]
-            for r in range(ROWS_AT_ONCE):
-                wide[pl.ds(first + r, 1), :] = held[r]
-        store(b, wide[...])
-        return carry
-
-    lax.fori_loop(0, blocks, one, 0)
+            for row in range(ROWS_AT_ONCE):
+                wide[pl.ds(first + row, 1), :] = held[row]
+        store(r, wide[...])
+        return carry
+
+    lax.fori_loop(0, count, one, 0)
 
 
 def tiles_of(step):
@@ -151,25 +171,19 @@
     return tiles, windows, inner
 
 
-def forward_kernel(
-    low, scale,
-    pos_ref, qkv_ref, bias_ref,
-    attended_ref, sorted_ref, query_ref, key_ref, value_ref, probs_ref,
-    wide, query, key, value, att,
+def scores_kernel(
+    scale, pos_ref, rows_ref, bias_ref, query_ref, key_ref, probs_ref, wide, query, key
 ):
     bf, f32 = jnp.bfloat16, jnp.float32
     blocks, lanes = pos_ref.shape
     rows = blocks * lanes
-    high = blocks // low
     edge = jnp.zeros((CAP, wide.shape[1]), f32)
-    for part, (ref, out) in enumerate(
-        ((query, query_ref), (key, key_ref), (value, value_ref))
-    ):
+    for part, (ref, out) in enumerate(((query, query_ref), (key, key_ref))):
         ref[pl.ds(0, CAP), :] = edge
         ref[pl.ds(rows + CAP, CAP), :] = edge
         move_in(
             pos_ref, lambda b: b,
-            lambda b, part=part: qkv_ref[b, pl.ds(part * lanes, lanes), :], wide, ref, CAP,
+            lambda b, part=part: rows_ref[b, pl.ds(part * lanes, lanes), :], wide, ref, CAP, blocks,
         )
         out[...] = ref[...].astype(bf)
 
@@ -177,88 +191,106 @@
         tiles, windows, inner = tiles_of(step)
         qs = [query_ref[at, :] for at in inner]
         ks = [key_ref[at, :] for at in windows]
-        vs = [value_ref[at, :] for at in windows]
         biases = [bias_ref[at, :].astype(f32) for at in tiles]
         scores = [lax.dot_general(q, k, NT, preferred_element_type=f32) for q, k in zip(qs, ks)]
         scores = [s * scale + bias for s, bias in zip(scores, biases)]
         tops = [jnp.max(s, axis=1, keepdims=True) for s in scores]
         weights = [jnp.exp(s - top) for s, top in zip(scores, tops)]
         sums = [jnp.sum(w, axis=1, keepdims=True) for w in weights]
-        probs = [w / total for w, total in zip(weights, sums)]
-        attended = [
-            jnp.dot(p.astype(bf), v, preferred_element_type=f32) for p, v in zip(probs, vs)
-        ]
-        for at, p, one in zip(tiles, probs, attended):
-            probs_ref[at, :] = p
+        for at, w, total in zip(tiles, weights, sums):
+            probs_ref[at, :] = w / total
+        return carry
+
+    lax.fori_loop(0, rows // TILE // UNROLL, some, 0)
+
+
+def attend_kernel(
+    low, me_ref, pos_ref, rows_ref, probs_ref, *refs
+):
+    parts, (sorted_ref, value_ref, wide, value, att) = refs[:low], refs[low:]
+    bf, f32 = jnp.bfloat16, jnp.float32
+    blocks, lanes = pos_ref.shape
+    rows = blocks * lanes
+    high = blocks // low
+    edge = jnp.zeros((CAP, wide.shape[1]), f32)
+    value[pl.ds(0, CAP), :] = edge
+    value[pl.ds(rows + CAP, CAP), :] = edge
+    move_in(pos_ref, lambda b: b, lambda b: rows_ref[b], wide, value, CAP, blocks)
+    value_ref[...] = value[...].astype(bf)
+
+    def some(step, carry):
+        tiles, windows, _ = tiles_of(step)
+        vs = [value_ref[at, :] for at in windows]
+        probs = [probs_ref[at, :].astype(bf) for at in tiles]
+        attended = [jnp.dot(p, v, preferred_element_type=f32) for p, v in zip(probs, vs)]
+        for at, one in zip(tiles, attended):
             att[at, :] = one
             sorted_ref[at, :] = one.astype(bf)
         return carry
 
     lax.fori_loop(0, rows // TILE // UNROLL, some, 0)
 
+    for k in range(low):
+        def put(r, block, k=k):
+            parts[k][pl.ds(pl.multiple_of(r * lanes, lanes), lanes), :] = block.astype(bf)
+
+        move_out(pos_ref, lambda r, k=k: r * low + (me_ref[0] ^ k), att, 0, wide, put, high)
+
+
+def value_kernel(
+    low, me_ref, pos_ref, probs_ref, *refs
+):
+    parts, (out_ref, sorted_ref, wide, grad, grad_value) = refs[:low], refs[low:]
+    bf, f32 = jnp.bfloat16, jnp.float32
+    blocks, lanes = pos_ref.shape
+    rows = blocks * lanes
+    high = blocks // low
+    for k in range(low):
+        def block_of(r, k=k):
+            return r * low + (me_ref[0] ^ k)
+
+        def load(r, k=k):
+            return parts[k][pl.ds(pl.multiple_of(r * lanes, lanes), lanes), :]
+
+        move_in(pos_ref, block_of, load, wide, grad, 0, high)
+    sorted_ref[...] = grad[...].astype(bf)
+    grad_value[...] = jnp.zeros_like(grad_value)
+
+    def some(step, carry):
+        tiles, windows, _ = tiles_of(step)
+        gs = [sorted_ref[at, :] for at in tiles]
+        probs = [probs_ref[at, :].astype(bf) for at in tiles]
+        more = [lax.dot_general(p, g, TN, preferred_element_type=f32) for p, g in zip(probs, gs)]
+        for at, one in zip(windows, more):
+            grad_value[at, :] += one
+        return carry
+
+    lax.fori_loop(0, rows // TILE // UNROLL, some, 0)
+
     def put(b, block):
-        attended_ref[lax.rem(b, low) * high + b // low] = block.astype(bf)
-
-    move_out(pos_ref, att, 0, wide, put)
-
-
-def forward(pos, qkv, bias, low):
-    blocks, lanes = pos.shape
-    rows = blocks * lanes
-    size = qkv.shape[-1]
-    bf = jnp.bfloat16
-    padded = jax.ShapeDtypeStruct((rows + 2 * CAP, size), bf)
-    sorted_rows = pltpu.VMEM((rows + 2 * CAP, size), jnp.float32)
-    return pl.pallas_call(
-        functools.partial(forward_kernel, low, 1.0 / math.sqrt(size)),
-        out_shape=(
-            jax.ShapeDtypeStruct((blocks, lanes, size), bf),
-            jax.ShapeDtypeStruct((rows, size), bf),
-            padded, padded, padded,
-            jax.ShapeDtypeStruct((rows, WIN), jnp.float32),
-        ),
-        in_specs=[SMEM, VMEM, VMEM],
-        out_specs=(VMEM,) * 6,
-        scratch_shapes=[
-            pltpu.VMEM((lanes, size), jnp.float32),
-            sorted_rows, sorted_rows, sorted_rows,
-            pltpu.VMEM((rows, size), jnp.float32),
-        ],
-        compiler_params=PARAMS,
-        name="forward",
-    )(pos, qkv, bias)
-
-
-def backward_kernel(
-    low, scale,
-    pos_ref, grad_ref, sorted_ref, query_ref, key_ref, value_ref, probs_ref,
-    grads_ref,
-    wide, grad, grad_query, grad_key, grad_value,
+        out_ref[b] = block.astype(bf)
+
+    move_out(pos_ref, lambda b: b, grad_value, CAP, wide, put, blocks)
+
+
+def rest_kernel(
+    scale, pos_ref, grad_ref, sorted_ref, query_ref, key_ref, value_ref, probs_ref,
+    out_ref, wide, grad_query, grad_key,
 ):
     bf, f32 = jnp.bfloat16, jnp.float32
     blocks, lanes = pos_ref.shape
     rows = blocks * lanes
-    high = blocks // low
-    move_in(
-        pos_ref, lambda b: lax.rem(b, low) * high + b // low,
-        lambda b: grad_ref[b], wide, grad, 0,
-    )
     grad_key[...] = jnp.zeros_like(grad_key)
-    grad_value[...] = jnp.zeros_like(grad_value)
 
     def some(step, carry):
         tiles, windows, inner = tiles_of(step)
-        gs = [grad[at, :].astype(bf) for at in tiles]
+        gs = [grad_ref[at, :] for at in tiles]
         qs = [query_ref[at, :] for at in inner]
         ks = [key_ref[at, :] for at in windows]
         vs = [value_ref[at, :] for at in windows]
         probs = [probs_ref[at, :] for at in tiles]
         attended = [sorted_ref[at, :].astype(f32) for at in tiles]
         grad_probs = [lax.dot_general(g, v, NT, preferred_element_type=f32) for g, v in zip(gs, vs)]
-        lows = [p.astype(bf) for p in probs]
-        more_values = [
-            lax.dot_general(p, g, TN, preferred_element_type=f32) for p, g in zip(lows, gs)
-        ]
         deltas = [
             jnp.sum(g.astype(f32) * one, axis=1, keepdims=True) for g, one in zip(gs, attended)
         ]
@@ -271,61 +303,160 @@
         ]
         for at, one in zip(tiles, grad_queries):
             grad_query[at, :] = one
-        for at, more_key, more_value in zip(windows, more_keys, more_values):
-            grad_key[at, :] += more_key
-            grad_value[at, :] += more_value
+        for at, one in zip(windows, more_keys):
+            grad_key[at, :] += one
         return carry
 
     lax.fori_loop(0, rows // TILE // UNROLL, some, 0)
 
-    def put(part, factor):
+    def put(part):
         def store(b, block):
-            grads_ref[b, pl.ds(part * lanes, lanes), :] = (block * factor).astype(bf)
+            out_ref[b, pl.ds(part * lanes, lanes), :] = (block * scale).astype(bf)
         return store
 
-    move_out(pos_ref, grad_query, 0, wide, put(0, scale))
-    move_out(pos_ref, grad_key, CAP, wide, put(1, scale))
-    move_out(pos_ref, grad_value, CAP, wide, put(2, 1.0))
-
-
-def backward(pos, grad, kept, low):
+    move_out(pos_ref, lambda b: b, grad_query, 0, wide, put(0), blocks)
+    move_out(pos_ref, lambda b: b, grad_key, CAP, wide, put(1), blocks)
+
+
+def project_back_kernel(low, rows_ref, *refs):
+    bf, f32 = jnp.bfloat16, jnp.float32
+    weights, outs = refs[:low], refs[low:]
+    for k in range(0, low, 2):
+        weight = jnp.concatenate([weights[k][...], weights[k + 1][...]], axis=1)
+        both = jnp.dot(rows_ref[...], weight, preferred_element_type=f32).astype(bf)
+        size = both.shape[1] // 2
+        outs[k][...] = both[:, :size]
+        outs[k + 1][...] = both[:, size:]
+
+
+def project_kernel(low, chunk, *refs):
+    bf, f32 = jnp.bfloat16, jnp.float32
+    weights, parts, out_ref = refs[:low], refs[low:-1], refs[-1]
+    rows = jnp.concatenate([ref[...] for ref in parts], axis=1)
+
+    def one(c, carry):
+        at = pl.ds(pl.multiple_of(c * chunk, chunk), chunk)
+        weight = jnp.concatenate([ref[at, :] for ref in weights], axis=1)
+        out_ref[:, at] = lax.dot_general(rows, weight, NT, preferred_element_type=f32).astype(bf)
+        return carry
+
+    lax.fori_loop(0, out_ref.shape[1] // chunk, one, 0)
+
+
+def place_in_plane(low):
+    index = lax.axis_index("seq")
+    return jnp.stack([index % low, index // low]).astype(jnp.int32)
+
+
+def project_back(weights, rows):
+    low = len(weights)
+    size = weights[0].shape[1]
+    return pl.pallas_call(
+        functools.partial(project_back_kernel, low),
+        out_shape=(jax.ShapeDtypeStruct((rows.shape[0], size), jnp.bfloat16),) * low,
+        in_specs=[VMEM] * (1 + low),
+        out_specs=(VMEM,) * low,
+        compiler_params=PARAMS,
+        cost_estimate=lasts(8),
+        name="project_back",
+    )(rows, *weights)
+
+
+def project(weights, parts):
+    low = len(weights)
+    columns = weights[0].shape[0]
+    return pl.pallas_call(
+        functools.partial(project_kernel, low, math.gcd(columns, 512)),
+        out_shape=jax.ShapeDtypeStruct((parts[0].shape[0], columns), jnp.bfloat16),
+        in_specs=[VMEM] * (2 * low),
+        out_specs=VMEM,
+        compiler_params=PARAMS,
+        cost_estimate=lasts(6),
+        name="project",
+    )(*weights, *parts)
+
+
+def head_kernels(pos, size, low):
     blocks, lanes = pos.shape
     rows = blocks * lanes
-    size = grad.shape[-1]
-    f32 = jnp.float32
-    plain = pltpu.VMEM((rows, size), f32)
-    padded = pltpu.VMEM((rows + 2 * CAP, size), f32)
-    return pl.pallas_call(
-        functools.partial(backward_kernel, low, 1.0 / math.sqrt(size)),
-        out_shape=jax.ShapeDtypeStruct((blocks, 3 * lanes, size), jnp.bfloat16),
-        in_specs=[SMEM] + [VMEM] * 6,
-        out_specs=VMEM,
-        scratch_shapes=[pltpu.VMEM((lanes, size), f32), plain, plain, padded, padded],
-        compiler_params=PARAMS,
-        name="backward",
-    )(pos, grad, *kept)
+    bf, f32 = jnp.bfloat16, jnp.float32
+    scale = 1.0 / math.sqrt(size)
+    plain, padded = (rows, size), (rows + 2 * CAP, size)
+    me = place_in_plane(low)
+
+    def call(kernel, operands, outs, scratch, micros, name):
+        return pl.pallas_call(
+            kernel,
+            out_shape=tuple(jax.ShapeDtypeStruct(shape, kind) for shape, kind in outs),
+            in_specs=[SMEM if x.dtype == jnp.int32 else VMEM for x in operands],
+            out_specs=(VMEM,) * len(outs),
+            scratch_shapes=[pltpu.VMEM(shape, f32) for shape in ((lanes, size), *scratch)],
+            compiler_params=PARAMS,
+            cost_estimate=lasts(micros),
+            name=name,
+        )(*operands)
+
+    def scores(query_key, bias):
+        return call(
+            functools.partial(scores_kernel, scale), (pos, query_key, bias),
+            ((padded, bf), (padded, bf), ((rows, WIN), f32)), (padded, padded), 12, "scores",
+        )
+
+    def attend(value, probs):
+        return call(
+            functools.partial(attend_kernel, low), (me, pos, value, probs),
+            (((blocks // low * lanes, size), bf),) * low + ((plain, bf), (padded, bf)),
+            (padded, plain), 12, "attend",
+        )
+
+    def grad_value(grads, probs):
+        return call(
+            functools.partial(value_kernel, low), (me, pos, probs, *grads),
+            (((blocks, lanes, size), bf), (plain, bf)), (plain, padded), 12, "grad_value",
+        )
+
+    def rest(grad, attended, query, key, value, probs):
+        return call(
+            functools.partial(rest_kernel, scale),
+            (pos, grad, attended, query, key, value, probs),
+            (((blocks, 2 * lanes, size), bf),), (plain, padded), 16, "rest",
+        )[0]
+
+    return scores, attend, grad_value, rest
 
 
 def pack_kernel(*refs):
     out_ref = refs[-1]
-    heads, rows, size = out_ref.shape
-    rows = rows // (len(refs) - 1)
-    for part, ref in enumerate(refs[:-1]):
-        for h in range(heads):
-            out_ref[h, pl.ds(part * rows, rows), :] = ref[:, pl.ds(h * size, size)]
+    size = out_ref.shape[2]
+    first = 0
+    for ref in refs[:-1]:
+        rows = ref.shape[-2]
+        for h in range(out_ref.shape[0]):
+            if len(ref.shape) == 3:
+                out_ref[h, pl.ds(first, rows), :] = ref[h]
+            else:
+                out_ref[h, pl.ds(first, rows), :] = ref[:, pl.ds(h * size, size)]
+        first += rows
 
 
 def pack(arrays, heads):
-    rows, width = arrays[0].shape
-    size = width // heads
+    rows = sum(array.shape[-2] for array in arrays)
+    size = arrays[0].shape[1] // heads
     step = math.gcd(heads, 8)
+
+    def block(array):
+        if array.ndim == 3:
+            return pl.BlockSpec((step, *array.shape[1:]), lambda i: (i, 0, 0))
+        return pl.BlockSpec((array.shape[0], step * size), lambda i: (0, i))
+
     return pl.pallas_call(
         pack_kernel,
         grid=(heads // step,),
-        out_shape=jax.ShapeDtypeStruct((heads, len(arrays) * rows, size), arrays[0].dtype),
-        in_specs=[pl.BlockSpec((rows, step * size), lambda i: (0, i))] * len(arrays),
-        out_specs=pl.BlockSpec((step, len(arrays) * rows, size), lambda i: (i, 0, 0)),
+        out_shape=jax.ShapeDtypeStruct((heads, rows, size), arrays[0].dtype),
+        in_specs=[block(array) for array in arrays],
+        out_specs=pl.BlockSpec((step, rows, size), lambda i: (i, 0, 0)),
         compiler_params=PARAMS,
+        cost_estimate=lasts(3),
         name="pack",
     )(*arrays)
 
@@ -349,6 +480,7 @@
         in_specs=[pl.BlockSpec((step, parts * rows, size), lambda i: (i, 0, 0))],
         out_specs=(pl.BlockSpec((rows, step * size), lambda i: (0, i)),) * parts,
         compiler_params=PARAMS,
+        cost_estimate=lasts(3),
         name="unpack",
     )(packed)
 
@@ -491,45 +623,57 @@
     head_size = width // heads_dev
     owners = lax.axis_size("seq")
     columns_dev = out_weight.shape[1]
-    columns = owners * columns_dev
     high, low = split(owners)
-    planes = [[h * low + p for p in range(low)] for h in range(high)]
     stacks = [[h * low + p for h in range(high)] for p in range(low)]
-    bf, f32 = jnp.bfloat16, jnp.float32
-
-    def exchange(rows, groups=None):
-        return lax.all_to_all(
-            rows, "seq", split_axis=0, concat_axis=0, tiled=True, axis_index_groups=groups
-        )
+    bf = jnp.bfloat16
+    together = lax.optimization_barrier
+
+    def exchange(rows):
+        return lax.all_to_all(rows, "seq", split_axis=0, concat_axis=0, tiled=True)
+
+    def swap(blocks, step=1):
+        pairs = [[(i, i ^ (k * step)) for i in range(owners)] for k in range(len(blocks))]
+        return [blocks[0]] + [
+            lax.ppermute(blocks[k], "seq", pairs[k]) for k in range(1, len(blocks))
+        ]
+
+    def gather_plane(block):
+        near = swap([block] * (low // 2), 2)
+        other = [(i, i ^ 1) for i in range(owners)]
+        return [x for one in near for x in (one, lax.ppermute(one, "seq", other))]
 
     weight_rows = out_weight.T.reshape(columns_dev, heads_dev, head_size).transpose(1, 0, 2)
     ids = jnp.stack([cluster_id // rows_dev, cluster_id % rows_dev, slot_index], axis=1)
     ids = jnp.pad(ids, ((0, 0), (0, 13), (0, 0))).astype(bf)
     first = exchange(jnp.concatenate([weight_rows, ids], axis=1))
     grad_out_stack = lax.all_gather(grad_out, "seq", axis=0, tiled=True, axis_index_groups=stacks)
-    packed = pack((query_rows, key_rows, value_rows), heads_dev)
-    packed, first = lax.optimization_barrier((packed, first))
-    qkv = exchange(packed)
-    head_weight = first[:, :columns_dev].reshape(columns, head_size)
-    plane_weight = lax.all_gather(head_weight, "seq", axis=0, axis_index_groups=planes)
+    packed = pack((query_rows, key_rows), heads_dev)
+    packed_value = pack((value_rows,), heads_dev)
+    packed, packed_value, first = together((packed, packed_value, first))
+    arrived = exchange(packed)
+    weights = gather_plane(first[:, :columns_dev].reshape(owners * columns_dev, head_size))
     pos, bias = place(first[:, columns_dev:], CLU_DEV * owners)
-    grad_plane = lax.dot_general(
-        plane_weight, grad_out_stack, (((1,), (1,)), ((), ())), preferred_element_type=f32
-    ).astype(bf)
-    grad_plane = grad_plane.transpose(0, 2, 1)
-    grad_plane, qkv = lax.optimization_barrier((grad_plane, qkv))
-    grad_head = exchange(grad_plane, planes).reshape(owners, rows_dev, head_size)
-    attended, *kept = forward(pos, qkv, bias, low)
-    attended_plane = exchange(attended.reshape(low, high * rows_dev, head_size), planes)
-    grads = backward(pos, grad_head, kept, low)
+    packed_value, arrived, pos, bias, weights = together(
+        (packed_value, arrived, pos, bias, weights)
+    )
+    value = exchange(packed_value)
+    grad_heads = swap(project_back(weights, grad_out_stack))
+    scores, attend, grad_of_value, rest = head_kernels(pos, head_size, low)
+    query, key, probs = scores(arrived, bias)
+    grad_value, grad_sorted = grad_of_value(grad_heads, probs)
+    value, grad_value = together((value, grad_value))
+    *attended, att_sorted, value_sorted = attend(value, probs)
+    back_value = exchange(grad_value)
+    attended = swap(attended)
+    grads = rest(grad_sorted, att_sorted, query, key, value_sorted, probs)
+    grads, attended = together((grads, attended))
+    grads, back_value = together((grads, back_value))
     back = exchange(grads)
-    partial = lax.dot_general(
-        attended_plane, plane_weight, (((0, 2), (0, 2)), ((), ())), preferred_element_type=f32
-    ).astype(bf)
+    partial = project(weights, attended)
     mixed = lax.psum_scatter(
         partial, "seq", scatter_dimension=0, tiled=True, axis_index_groups=stacks
     )
-    return (mixed, *unpack(back, 3))
+    return (mixed, *unpack(back, 2), *unpack(back_value, 1))
 
 
 def split(owners):
@@ -543,7 +687,7 @@
     def shards(*args):
         heads_dev = args[3].shape[0]
         owners = lax.axis_size("seq")
-        if heads_dev == owners and lax.axis_size("tensor") == 1:
+        if heads_dev == owners and owners & (owners - 1) == 0 and lax.axis_size("tensor") == 1:
             return by_heads(*args)
         return by_clusters(*args)
 

time: 355 us -> 315 us (0.89)
  waiting for transfers between devices: 211 us -> 163 us
  starting transfers between devices: 27.1 us -> 43.7 us
  matrix products: 12.5 us -> 0 us
    all_gather x1 -> x0, waiting for transfers between devices: 52.1 us -> none  [by_heads(): lax.all_gather(head_weight, 'seq', axis=0, axis_index_groups=planes)]
    ppermute x0 -> x21, waiting for transfers between devices: none -> 45.1 us  [the longest x17 45.1 us: swap(): lax.ppermute(blocks[k], 'seq', pairs[k])]
    all_gather x1, waiting for transfers between devices: 31 us -> 0.02 us  [by_heads(): lax.all_gather(grad_out, 'seq', axis=0, tiled=True, axis_index_groups=sta...]
    ppermute x0 -> x21, starting transfers between devices: none -> 18.1 us  [the longest x17 18.1 us: swap(): lax.ppermute(blocks[k], 'seq', pairs[k])]
    pallas_call x1, Pallas kernels: 22.9 us -> 6.85 us  [place(): pl.pallas_call(functools.partial(place_kernel, clusters), out_shape=(jax....]
    pallas_call x2 -> x6, Pallas kernels: 46.6 us -> 59.8 us  [the longest x4 50.8 us: call(): pl.pallas_call(kernel, out_shape=tuple((jax.ShapeDtypeStruct(shape, kind)...]
    dot_general x2 -> x0, matrix products: 12.5 us -> none  [the longest x1 6.24 us: by_heads(): lax.dot_general(attended_plane, plane_weight, (((0, 2), (0, 2)), ((), ())...]
    all_to_all x5, waiting for transfers between devices: 127 us -> 117 us  [exchange(): return lax.all_to_all(rows, 'seq', split_axis=0, concat_axis=0, tiled=True)]
  transfers between devices with their start and end apart: 8 -> 28, of which waited for: 4 -> 8; matrix products, arithmetic and copies ran while one was open for 5% -> 1% of each run, Pallas kernels for 22% -> 24%
where the time goes in v3:
time: 315 us; the launch traced here: 314 us
  waiting for transfers between devices  163 us (52%)
  Pallas kernels  76 us (24%)
  starting transfers between devices  43.7 us (14%)
  between operations  14.5 us (5%)
  local copies, waits for them, and re-layouts  14.1 us (4%)
    all_to_all x5, waiting for transfers between devices, exchange(): return lax.all_to_all(rows, 'seq', split_axis=0, concat_axis=0, tiled=True)  117 us
    pallas_call x4, Pallas kernels, call(): pl.pallas_call(kernel, out_shape=tuple((jax.ShapeDtypeStruct(shape, kind)...  50.8 us
    ppermute x17, waiting for transfers between devices, swap(): lax.ppermute(blocks[k], 'seq', pairs[k])  45.1 us
    all_to_all x5, starting transfers between devices, exchange(): return lax.all_to_all(rows, 'seq', split_axis=0, concat_axis=0, tiled=True)  25.5 us
    ppermute x17, starting transfers between devices, swap(): lax.ppermute(blocks[k], 'seq', pairs[k])  18.1 us
    unnamed x66, local copies, waits for them, and re-layouts  11.7 us
    pallas_call x1, Pallas kernels, place(): pl.pallas_call(functools.partial(place_kernel, clusters), out_shape=(jax....  6.85 us
  transfers between devices with their start and end apart: 28, of which 8 were waited for; matrix products, arithmetic and copies ran while one was open for 1% of the time, Pallas kernels for 24%

profile of v3, /device:TPU:0, one launch (start us, length us, event | category | flops | bytes accessed | tf_op | source)
XLA Modules:
  0.0 314.1 jit_solution(4745193491368412542)
XLA Ops:
  10.0 7.4 %all-to-all-start = ((bf16[32,80,128]{2,1,0:T(8,128)(2,1)}), bf16[32,80,128]{2,1,0:T(8,128)(2,1)}, u32[]{:S(2)}, u32[]{:S(2)}) async-start(bf16[32,80,128]{2,1,0:T(8,128)(2,1)} %pad_maximum_fusion), calls=%async_computation | async-start | bytes 1310720 | tf_op jit(solution)/shard_map/all_to_all | solution.py:632
  17.4 1.7 pack.3
  19.1 2.1 pack.2
  21.2 14.1 %all-to-all-done = bf16[32,80,128]{2,1,0:T(8,128)(2,1)} async-done(((bf16[32,80,128]{2,1,0:T(8,128)(2,1)}), bf16[32,80,128]{2,1,0:T(8,128)(2,1)}, u32[]{:S(2)}, u32[]{:S(2)}) %all-to-all-start) | async-done | bytes 655392 | tf_op jit(solution)/shard_map/all_to_all | solution.py:632
  35.3 3.6 %all-to-all-start.1 = ((bf16[32,256,128]{2,1,0:T(8,128)(2,1)}), bf16[32,256,128]{2,1,0:T(8,128)(2,1)}, u32[]{:S(2)}, u32[]{:S(2)}) async-start(bf16[32,256,128]{2,1,0:T(8,128)(2,1)} %pack.2), calls=%async_computation.1 | async-start | bytes 4194304 | tf_op jit(solution)/shard_map/all_to_all | solution.py:632
  40.8 2.7 collective-permute-start.5
  44.3 28.6 %collective-permute-done.5.refs_6_ = bf16[2048,128]{1,0:T(8,128)(2,1)S(1)} collective-permute-done((bf16[2048,128]{1,0:T(8,128)(2,1)S(1)}, bf16[2048,128]{1,0:T(8,128)(2,1)S(1)}, u32[]{:S(2)}, u32[]{:S(2)}) %collective-permute-start.5) | collective-permute-done | bytes 524320 | tf_op jit(solution)/shard_map/ppermute | solution.py:637
  72.9 9.5 %collective-permute-done.3.refs_4_ = bf16[2048,128]{1,0:T(8,128)(2,1)S(1)} collective-permute-done((bf16[2048,128]{1,0:T(8,128)(2,1)S(1)}, bf16[2048,128]{1,0:T(8,128)(2,1)S(1)}, u32[]{:S(2)}, u32[]{:S(2)}) %collective-permute-start.3) | collective-permute-done | bytes 524320 | tf_op jit(solution)/shard_map/ppermute | solution.py:637
  82.4 3.1 %collective-permute-done.1.refs_2_ = bf16[2048,128]{1,0:T(8,128)(2,1)S(1)} collective-permute-done((bf16[2048,128]{1,0:T(8,128)(2,1)S(1)}, bf16[2048,128]{1,0:T(8,128)(2,1)S(1)}, u32[]{:S(2)}, u32[]{:S(2)}) %collective-permute-start.1) | collective-permute-done | bytes 524320 | tf_op jit(solution)/shard_map/ppermute | solution.py:637
  86.6 6.8 %place.1 = (s32[32,128]{1,0:T(8,128)S(1)}, bf16[4096,128]{1,0:T(8,128)(2,1)S(1)}) custom-call(bf16[32,16,128]{2,1,0:T(8,128)(2,1)S(1)} %slice.6.ids_ref), custom_call_target="tpu_custom_call" | custom-call | bytes 35000000 | tf_op jit(solution)/shard_map/place/pallas_call | solution.py:116
  96.9 24.4 %all-to-all-done.1.rows_ref = bf16[32,256,128]{2,1,0:T(8,128)(2,1)} async-done(((bf16[32,256,128]{2,1,0:T(8,128)(2,1)}), bf16[32,256,128]{2,1,0:T(8,128)(2,1)}, u32[]{:S(2)}, u32[]{:S(2)}) %all-to-all-start.1) | async-done | bytes 2097184 | tf_op jit(solution)/shard_map/all_to_all | solution.py:632
  121.4 4.3 %all-to-all-start.2 = ((bf16[32,128,128]{2,1,0:T(8,128)(2,1)}), bf16[32,128,128]{2,1,0:T(8,128)(2,1)}, u32[]{:S(2)}, u32[]{:S(2)}) async-start(bf16[32,128,128]{2,1,0:T(8,128)(2,1)} %pack.3), calls=%async_computation.2 | async-start | bytes 2097152 | tf_op jit(solution)/shard_map/all_to_all | solution.py:632
  128.8 4.7 %project_back.1 = (bf16[512,128]{1,0:T(8,128)(2,1)S(1)}, bf16[512,128]{1,0:T(8,128)(2,1)S(1)}, bf16[512,128]{1,0:T(8,128)(2,1)S(1)}, bf16[512,128]{1,0:T(8,128)(...) custom-call(bf16[512,2048]{1,0:T(8,128)(2,1)} %all-gather.2.cloned.1, ...), custom_call_target="tpu_custom_call" | custom-call | bytes 28000000 | tf_op jit(solution)/shard_map/project_back/pallas_call | solution.py:354
  133.8 1.7 collective-permute-start.8
  135.5 1.7 collective-permute-start.10
  137.3 2.6 collective-permute-start.12
  139.9 2.3 collective-permute-done.8.refs_2_
  143.4 1.2 copy-done.24
  144.7 12.5 %scores.1 = (bf16[4160,128]{1,0:T(8,128)(2,1)S(1)}, bf16[4160,128]{1,0:T(8,128)(2,1)S(1)}, f32[4096,128]{1,0:T(8,128)S(1)}) custom-call(s32[32,128]{1,0:T(8,128)S(1)} %get-tuple-element.72.pos_ref, bf16[32,256,128]{2,1,0:T(8,128)(2,1)} %all-to-all-done.1.rows_ref, bf16[4096,128]{1,0:T(8,128)(2,1)S(1)} %copy-done.24), custom_call_target="tpu_custom_call" | custom-call | bytes 42000000 | tf_op jit(solution)/shard_map/scores/pallas_call | solution.py:388
  159.2 11.6 %grad_value.1 = (bf16[32,128,128]{2,1,0:T(8,128)(2,1)S(1)}, bf16[4096,128]{1,0:T(8,128)(2,1)S(1)}) custom-call(s32[2]{0:T(128)S(1)} %pad_add_fusion.me_ref, s32[32,128]{1,0:T(8,128)S(1)} %get-tuple-element.72.pos_ref, f32[4096,128]{1,0:T(8,128)S(1)} %get-tuple-element.75.probs_ref, bf16[512,128]{1,0:T(8,128)(2,1)S(1)} %get-tuple-element.76.refs_0_, ...), custom_call_target="tpu_custom_call" | custom-call | bytes 42000000 | tf_op jit(solution)/shard_map/grad_value/pallas_call | solution.py:388
  172.7 4.2 %all-to-all-start.3 = ((bf16[32,128,128]{2,1,0:T(8,128)(2,1)}), bf16[32,128,128]{2,1,0:T(8,128)(2,1)}, u32[]{:S(2)}, u32[]{:S(2)}) async-start(bf16[32,128,128]{2,1,0:T(8,128)(2,1)} %copy-done.28), calls=%async_computation.4 | async-start | bytes 2097152 | tf_op jit(solution)/shard_map/all_to_all | solution.py:632
  177.0 11.2 %attend.1 = (bf16[512,128]{1,0:T(8,128)(2,1)S(1)}, bf16[512,128]{1,0:T(8,128)(2,1)S(1)}, bf16[512,128]{1,0:T(8,128)(2,1)S(1)}, bf16[512,128]{1,0:T(8,128)(2,1)S(...) custom-call(s32[2]{0:T(128)S(1)} %copy-done.32, ...), custom_call_target="tpu_custom_call" | custom-call | bytes 42000000 | tf_op jit(solution)/shard_map/attend/pallas_call | solution.py:388
  188.5 1.5 collective-permute-start.15
  190.1 1.7 collective-permute-start.17
  192.0 2.4 collective-permute-start.19
  194.4 1.5 collective-permute-done.15.refs_10_
  196.8 15.6 %rest.1 = bf16[32,256,128]{2,1,0:T(8,128)(2,1)} custom-call(s32[32,128]{1,0:T(8,128)S(1)} %get-tuple-element.72.pos_ref, bf16[4096,128]{1,0:T(8,128)(2,1)S(1)} %copy-done.26, bf16[4096,128]{1,0:T(8,128)(2,1)S(1)} %get-tuple-element.88.sorted_ref, bf16[4160,128]{1,0:T(8,128)(2,1)S(1)} %copy-done.20, bf16[4160,128]{1,0:T(8,128)(2,1)S(1)} %copy-done.22, ...), custom_call_target="tpu_custom_call" | custom-call | bytes 56000000 | tf_op jit(solution)/shard_map/rest/pallas_call | solution.py:388
  212.4 4.4 %project.1 = bf16[512,2048]{1,0:T(8,128)(2,1)} custom-call(bf16[2048,128]{1,0:T(8,128)(2,1)S(1)} %bitcast.22, bf16[2048,128]{1,0:T(8,128)(2,1)S(1)} %copy-done.9, bf16[2048,128]{1,0:T(8,128)(2,1)S(1)} %copy-done.7, bf16[2048,128]{1,0:T(8,128)(2,1)S(1)} %copy-done.18, bf16[2048,128]{1,0:T(8,128)(2,1)S(1)} %copy-done.5, bf16[2048,128]{1,0:T(8,128)(2,1)S(1)} %copy-done.15, ...), custom_call_target="tpu_custom_call" | custom-call | bytes 21000000 | tf_op jit(solution)/shard_map/project/pallas_call | solution.py:368
  216.8 6.0 %all-to-all-start.4 = ((bf16[32,256,128]{2,1,0:T(8,128)(2,1)}), bf16[32,256,128]{2,1,0:T(8,128)(2,1)S(1)}, u32[]{:S(2)}, u32[]{:S(2)}) async-start(bf16[32,256,128]{2,1,0:T(8,128)(2,1)} %rest.1), calls=%async_computation.5 | async-start | bytes 4194304 | tf_op jit(solution)/shard_map/all_to_all | solution.py:632
  222.8 3.5 %unpack.3 = bf16[128,4096]{1,0:T(8,128)(2,1)} custom-call(bf16[32,128,128]{2,1,0:T(8,128)(2,1)} %all-to-all-done.3.in_ref), custom_call_target="tpu_custom_call" | custom-call | bytes 10500000 | tf_op jit(solution)/shard_map/unpack/pallas_call | solution.py:476
  226.3 78.9 %all-to-all-done.4.in_ref = bf16[32,256,128]{2,1,0:T(8,128)(2,1)S(1)} async-done(((bf16[32,256,128]{2,1,0:T(8,128)(2,1)}), bf16[32,256,128]{2,1,0:T(8,128)(2,1)S(1)}, u32[]{:S(2)}, u32[]{:S(2)}) %all-to-all-start.4) | async-done | bytes 2097184 | tf_op jit(solution)/shard_map/all_to_all | solution.py:632
  305.2 2.0 unpack.2
  (114 shorter events, 20.2 us)
Async XLA Ops:
  10.0 25.3 %all-to-all-start = ((bf16[32,80,128]{2,1,0:T(8,128)(2,1)}), bf16[32,80,128]{2,1,0:T(8,128)(2,1)}, u32[]{:S(2)}, u32[]{:S(2)}) async-start(bf16[32,80,128]{2,1,0:T(8,128)(2,1)} %pad_maximum_fusion), calls=%async_computation | async-start | bytes 1310720 | tf_op jit(solution)/shard_map/all_to_all | solution.py:632
  35.3 86.1 %all-to-all-start.1 = ((bf16[32,256,128]{2,1,0:T(8,128)(2,1)}), bf16[32,256,128]{2,1,0:T(8,128)(2,1)}, u32[]{:S(2)}, u32[]{:S(2)}) async-start(bf16[32,256,128]{2,1,0:T(8,128)(2,1)} %pack.2), calls=%async_computation.1 | async-start | bytes 4194304 | tf_op jit(solution)/shard_map/all_to_all | solution.py:632
  38.9 86.7 %all-gather.2.cloned.1.call-start = ((), (), s32[]{:S(2)}) async-start(), calls=%async_computation.6 | async-start | bytes 2621440 | tf_op jit(solution)/shard_map/all_gather | solution.py:649
  40.8 32.1 %collective-permute-start.5 = (bf16[2048,128]{1,0:T(8,128)(2,1)S(1)}, bf16[2048,128]{1,0:T(8,128)(2,1)S(1)}, u32[]{:S(2)}, u32[]{:S(2)}) collective-permute-start(bf16[2048,128]{1,0:T(8,128)(2,1)S(1)} %bitcast.17), channel_id=1, source_target_pairs={{0,6},{1,7},{2,4},{3,5},{4,2},{5,3},{6,0},{7,1},{8,14},{9,15},{10,... | collective-permute-start | bytes 1572872 | tf_op jit(solution)/shard_map/ppermute | solution.py:637
  43.4 39.0 %collective-permute-start.3 = (bf16[2048,128]{1,0:T(8,128)(2,1)S(1)}, bf16[2048,128]{1,0:T(8,128)(2,1)S(1)}, u32[]{:S(2)}, u32[]{:S(2)}) collective-permute-start(bf16[2048,128]{1,0:T(8,128)(2,1)S(1)} %bitcast.18), channel_id=1, source_target_pairs={{0,4},{1,5},{2,6},{3,7},{4,0},{5,1},{6,2},{7,3},{8,12},{9,13},{10,... | collective-permute-start | bytes 1572872 | tf_op jit(solution)/shard_map/ppermute | solution.py:637
  44.0 41.6 %collective-permute-start.1 = (bf16[2048,128]{1,0:T(8,128)(2,1)S(1)}, bf16[2048,128]{1,0:T(8,128)(2,1)S(1)}, u32[]{:S(2)}, u32[]{:S(2)}) collective-permute-start(bf16[2048,128]{1,0:T(8,128)(2,1)S(1)} %bitcast.19), channel_id=1, source_target_pairs={{0,2},{1,3},{2,0},{3,1},{4,6},{5,7},{6,4},{7,5},{8,10},{9,11},{10,... | collective-permute-start | bytes 1572872 | tf_op jit(solution)/shard_map/ppermute | solution.py:637
  44.3 50.2 %collective-permute-start = (bf16[2048,128]{1,0:T(8,128)(2,1)S(1)}, bf16[2048,128]{1,0:T(8,128)(2,1)S(1)}, u32[]{:S(2)}, u32[]{:S(2)}) collective-permute-start(bf16[2048,128]{1,0:T(8,128)(2,1)S(1)} %bitcast.20), channel_id=1, source_target_pairs={{0,1},{1,0},{2,3},{3,2},{4,5},{5,4},{6,7},{7,6},{8,9},{9,8},{10,11... | collective-permute-start | bytes 1572872 | tf_op jit(solution)/shard_map/ppermute | solution.py:643
  72.9 60.6 %copy-start.2 = (bf16[2048,128]{1,0:T(8,128)(2,1)}, bf16[2048,128]{1,0:T(8,128)(2,1)S(1)}, u32[]{:S(2)}) copy-start(bf16[2048,128]{1,0:T(8,128)(2,1)S(1)} %collective-permute-done.5.refs_6_) | copy-start | bytes 1572868
  72.9 21.6 %collective-permute-start.6 = (bf16[2048,128]{1,0:T(8,128)(2,1)S(1)}, bf16[2048,128]{1,0:T(8,128)(2,1)S(1)}, u32[]{:S(2)}, u32[]{:S(2)}) collective-permute-start(bf16[2048,128]{1,0:T(8,128)(2,1)S(1)} %collective-permute-done.5.refs_6_), channel_id=1, source_target_pairs={{0,1},{1,0},{2,3},{3,2},{4,5},{5,4},{6,7},{7,6},{8,9},{9,8},{10,11... | collective-permute-start | bytes 1572872 | tf_op jit(solution)/shard_map/ppermute | solution.py:643
  82.4 51.1 %copy-start.4 = (bf16[2048,128]{1,0:T(8,128)(2,1)}, bf16[2048,128]{1,0:T(8,128)(2,1)S(1)}, u32[]{:S(2)}) copy-start(bf16[2048,128]{1,0:T(8,128)(2,1)S(1)} %collective-permute-done.3.refs_4_) | copy-start | bytes 1572868
  82.4 12.9 %collective-permute-start.4 = (bf16[2048,128]{1,0:T(8,128)(2,1)S(1)}, bf16[2048,128]{1,0:T(8,128)(2,1)S(1)}, u32[]{:S(2)}, u32[]{:S(2)}) collective-permute-start(bf16[2048,128]{1,0:T(8,128)(2,1)S(1)} %collective-permute-done.3.refs_4_), channel_id=1, source_target_pairs={{0,1},{1,0},{2,3},{3,2},{4,5},{5,4},{6,7},{7,6},{8,9},{9,8},{10,11... | collective-permute-start | bytes 1572872 | tf_op jit(solution)/shard_map/ppermute | solution.py:643
  85.6 48.0 %copy-start.6 = (bf16[2048,128]{1,0:T(8,128)(2,1)}, bf16[2048,128]{1,0:T(8,128)(2,1)S(1)}, u32[]{:S(2)}) copy-start(bf16[2048,128]{1,0:T(8,128)(2,1)S(1)} %collective-permute-done.1.refs_2_) | copy-start | bytes 1572868
  85.6 10.6 %collective-permute-start.2 = (bf16[2048,128]{1,0:T(8,128)(2,1)S(1)}, bf16[2048,128]{1,0:T(8,128)(2,1)S(1)}, u32[]{:S(2)}, u32[]{:S(2)}) collective-permute-start(bf16[2048,128]{1,0:T(8,128)(2,1)S(1)} %collective-permute-done.1.refs_2_), channel_id=1, source_target_pairs={{0,1},{1,0},{2,3},{3,2},{4,5},{5,4},{6,7},{7,6},{8,9},{9,8},{10,11... | collective-permute-start | bytes 1572872 | tf_op jit(solution)/shard_map/ppermute | solution.py:643
  94.5 39.1 %copy-start.8 = (bf16[2048,128]{1,0:T(8,128)(2,1)}, bf16[2048,128]{1,0:T(8,128)(2,1)S(1)}, u32[]{:S(2)}) copy-start(bf16[2048,128]{1,0:T(8,128)(2,1)S(1)} %collective-permute-done.refs_1_) | copy-start | bytes 1572868
  121.4 51.3 %all-to-all-start.2 = ((bf16[32,128,128]{2,1,0:T(8,128)(2,1)}), bf16[32,128,128]{2,1,0:T(8,128)(2,1)}, u32[]{:S(2)}, u32[]{:S(2)}) async-start(bf16[32,128,128]{2,1,0:T(8,128)(2,1)} %pack.3), calls=%async_computation.2 | async-start | bytes 2097152 | tf_op jit(solution)/shard_map/all_to_all | solution.py:632
  133.6 3.7 %collective-permute-start.7 = (bf16[512,128]{1,0:T(8,128)(2,1)S(1)}, bf16[512,128]{1,0:T(8,128)(2,1)S(1)}, u32[]{:S(2)}, u32[]{:S(2)}) collective-permute-start(bf16[512,128]{1,0:T(8,128)(2,1)S(1)} %get-tuple-element.77), channel_id=1, source_target_pairs={{0,1},{1,0},{2,3},{3,2},{4,5},{5,4},{6,7},{7,6},{8,9},{9,8},{10,11... | collective-permute-start | bytes 393224 | tf_op jit(solution)/shard_map/ppermute | solution.py:637
  133.8 8.4 %collective-permute-start.8 = (bf16[512,128]{1,0:T(8,128)(2,1)S(1)}, bf16[512,128]{1,0:T(8,128)(2,1)S(1)}, u32[]{:S(2)}, u32[]{:S(2)}) collective-permute-start(bf16[512,128]{1,0:T(8,128)(2,1)S(1)} %get-tuple-element.78), channel_id=1, source_target_pairs={{0,2},{1,3},{2,0},{3,1},{4,6},{5,7},{6,4},{7,5},{8,10},{9,11},{10,... | collective-permute-start | bytes 393224 | tf_op jit(solution)/shard_map/ppermute | solution.py:637
  135.5 23.6 %collective-permute-start.9 = (bf16[512,128]{1,0:T(8,128)(2,1)}, bf16[512,128]{1,0:T(8,128)(2,1)}, u32[]{:S(2)}, u32[]{:S(2)}) collective-permute-start(bf16[512,128]{1,0:T(8,128)(2,1)} %get-tuple-element.79), channel_id=1, source_target_pairs={{0,3},{1,2},{2,1},{3,0},{4,7},{5,6},{6,5},{7,4},{8,11},{9,10},{10,... | collective-permute-start | bytes 393224 | tf_op jit(solution)/shard_map/ppermute | solution.py:637
  135.5 23.6 %collective-permute-start.10 = (bf16[512,128]{1,0:T(8,128)(2,1)}, bf16[512,128]{1,0:T(8,128)(2,1)}, u32[]{:S(2)}, u32[]{:S(2)}) collective-permute-start(bf16[512,128]{1,0:T(8,128)(2,1)} %get-tuple-element.80), channel_id=1, source_target_pairs={{0,4},{1,5},{2,6},{3,7},{4,0},{5,1},{6,2},{7,3},{8,12},{9,13},{10,... | collective-permute-start | bytes 393224 | tf_op jit(solution)/shard_map/ppermute | solution.py:637
  137.2 21.9 %collective-permute-start.11 = (bf16[512,128]{1,0:T(8,128)(2,1)}, bf16[512,128]{1,0:T(8,128)(2,1)}, u32[]{:S(2)}, u32[]{:S(2)}) collective-permute-start(bf16[512,128]{1,0:T(8,128)(2,1)} %get-tuple-element.81), channel_id=1, source_target_pairs={{0,5},{1,4},{2,7},{3,6},{4,1},{5,0},{6,3},{7,2},{8,13},{9,12},{10,... | collective-permute-start | bytes 393224 | tf_op jit(solution)/shard_map/ppermute | solution.py:637
  137.3 21.8 %collective-permute-start.12 = (bf16[512,128]{1,0:T(8,128)(2,1)}, bf16[512,128]{1,0:T(8,128)(2,1)}, u32[]{:S(2)}, u32[]{:S(2)}) collective-permute-start(bf16[512,128]{1,0:T(8,128)(2,1)} %get-tuple-element.82), channel_id=1, source_target_pairs={{0,6},{1,7},{2,4},{3,5},{4,2},{5,3},{6,0},{7,1},{8,14},{9,15},{10,... | collective-permute-start | bytes 393224 | tf_op jit(solution)/shard_map/ppermute | solution.py:637
  142.2 16.9 %collective-permute-start.13 = (bf16[512,128]{1,0:T(8,128)(2,1)}, bf16[512,128]{1,0:T(8,128)(2,1)}, u32[]{:S(2)}, u32[]{:S(2)}) collective-permute-start(bf16[512,128]{1,0:T(8,128)(2,1)} %get-tuple-element.83), channel_id=1, source_target_pairs={{0,7},{1,6},{2,5},{3,4},{4,3},{5,2},{6,1},{7,0},{8,15},{9,14},{10,... | collective-permute-start | bytes 393224 | tf_op jit(solution)/shard_map/ppermute | solution.py:637
  172.7 44.1 %all-to-all-start.3 = ((bf16[32,128,128]{2,1,0:T(8,128)(2,1)}), bf16[32,128,128]{2,1,0:T(8,128)(2,1)}, u32[]{:S(2)}, u32[]{:S(2)}) async-start(bf16[32,128,128]{2,1,0:T(8,128)(2,1)} %copy-done.28), calls=%async_computation.4 | async-start | bytes 2097152 | tf_op jit(solution)/shard_map/all_to_all | solution.py:632
  176.9 130.4 %reduce-scatter.2.cloned.1.call-start = ((), (), s32[]{:S(2)}) async-start(), calls=%async_computation.7 | async-start | bytes 2621440 | tf_op jit(solution)/shard_map/reduce_scatter | solution.py:673
  188.1 3.9 %collective-permute-start.14 = (bf16[512,128]{1,0:T(8,128)(2,1)S(1)}, bf16[512,128]{1,0:T(8,128)(2,1)S(1)}, u32[]{:S(2)}, u32[]{:S(2)}) collective-permute-start(bf16[512,128]{1,0:T(8,128)(2,1)S(1)} %get-tuple-element.93), channel_id=1, source_target_pairs={{0,1},{1,0},{2,3},{3,2},{4,5},{5,4},{6,7},{7,6},{8,9},{9,8},{10,11... | collective-permute-start | bytes 393224 | tf_op jit(solution)/shard_map/ppermute | solution.py:637
  188.5 7.4 %collective-permute-start.15 = (bf16[512,128]{1,0:T(8,128)(2,1)S(1)}, bf16[512,128]{1,0:T(8,128)(2,1)S(1)}, u32[]{:S(2)}, u32[]{:S(2)}) collective-permute-start(bf16[512,128]{1,0:T(8,128)(2,1)S(1)} %get-tuple-element.94), channel_id=1, source_target_pairs={{0,2},{1,3},{2,0},{3,1},{4,6},{5,7},{6,4},{7,5},{8,10},{9,11},{10,... | collective-permute-start | bytes 393224 | tf_op jit(solution)/shard_map/ppermute | solution.py:637
  190.0 22.3 %collective-permute-start.16 = (bf16[512,128]{1,0:T(8,128)(2,1)S(1)}, bf16[512,128]{1,0:T(8,128)(2,1)S(1)}, u32[]{:S(2)}, u32[]{:S(2)}) collective-permute-start(bf16[512,128]{1,0:T(8,128)(2,1)S(1)} %get-tuple-element.95), channel_id=1, source_target_pairs={{0,3},{1,2},{2,1},{3,0},{4,7},{5,6},{6,5},{7,4},{8,11},{9,10},{10,... | collective-permute-start | bytes 393224 | tf_op jit(solution)/shard_map/ppermute | solution.py:637
  190.1 22.3 %collective-permute-start.17 = (bf16[512,128]{1,0:T(8,128)(2,1)S(1)}, bf16[512,128]{1,0:T(8,128)(2,1)S(1)}, u32[]{:S(2)}, u32[]{:S(2)}) collective-permute-start(bf16[512,128]{1,0:T(8,128)(2,1)S(1)} %get-tuple-element.96), channel_id=1, source_target_pairs={{0,4},{1,5},{2,6},{3,7},{4,0},{5,1},{6,2},{7,3},{8,12},{9,13},{10,... | collective-permute-start | bytes 393224 | tf_op jit(solution)/shard_map/ppermute | solution.py:637
  191.7 20.6 %collective-permute-start.18 = (bf16[512,128]{1,0:T(8,128)(2,1)S(1)}, bf16[512,128]{1,0:T(8,128)(2,1)S(1)}, u32[]{:S(2)}, u32[]{:S(2)}) collective-permute-start(bf16[512,128]{1,0:T(8,128)(2,1)S(1)} %get-tuple-element.97), channel_id=1, source_target_pairs={{0,5},{1,4},{2,7},{3,6},{4,1},{5,0},{6,3},{7,2},{8,13},{9,12},{10,... | collective-permute-start | bytes 393224 | tf_op jit(solution)/shard_map/ppermute | solution.py:637
  192.0 20.3 %collective-permute-start.19 = (bf16[512,128]{1,0:T(8,128)(2,1)S(1)}, bf16[512,128]{1,0:T(8,128)(2,1)S(1)}, u32[]{:S(2)}, u32[]{:S(2)}) collective-permute-start(bf16[512,128]{1,0:T(8,128)(2,1)S(1)} %get-tuple-element.98), channel_id=1, source_target_pairs={{0,6},{1,7},{2,4},{3,5},{4,2},{5,3},{6,0},{7,1},{8,14},{9,15},{10,... | collective-permute-start | bytes 393224 | tf_op jit(solution)/shard_map/ppermute | solution.py:637
  195.9 16.4 %collective-permute-start.20 = (bf16[512,128]{1,0:T(8,128)(2,1)S(1)}, bf16[512,128]{1,0:T(8,128)(2,1)S(1)}, u32[]{:S(2)}, u32[]{:S(2)}) collective-permute-start(bf16[512,128]{1,0:T(8,128)(2,1)S(1)} %get-tuple-element.99), channel_id=1, source_target_pairs={{0,7},{1,6},{2,5},{3,4},{4,3},{5,2},{6,1},{7,0},{8,15},{9,14},{10,... | collective-permute-start | bytes 393224 | tf_op jit(solution)/shard_map/ppermute | solution.py:637
  216.8 88.4 %all-to-all-start.4 = ((bf16[32,256,128]{2,1,0:T(8,128)(2,1)}), bf16[32,256,128]{2,1,0:T(8,128)(2,1)S(1)}, u32[]{:S(2)}, u32[]{:S(2)}) async-start(bf16[32,256,128]{2,1,0:T(8,128)(2,1)} %rest.1), calls=%async_computation.5 | async-start | bytes 4194304 | tf_op jit(solution)/shard_map/all_to_all | solution.py:632
  (29 other events, 236.4 us)
Sparse Core Ops, SparseCore 0:
  41.4 79.8 all-gather.1
  216.9 76.8 reduce-scatter.1

commit v4 on v3

--- a/solution.py
+++ b/solution.py
@@ -16,7 +16,9 @@
 UNROLL = 8
 VMEM = pl.BlockSpec(memory_space=pltpu.VMEM)
 SMEM = pl.BlockSpec(memory_space=pltpu.SMEM)
-PARAMS = pltpu.CompilerParams(vmem_limit_bytes=48 * 1024 * 1024)
+HBM = pl.BlockSpec(memory_space=pltpu.HBM)
+PARAMS = pltpu.CompilerParams(vmem_limit_bytes=61 * 1024 * 1024)
+SMALL = pltpu.CompilerParams(vmem_limit_bytes=16 * 1024 * 1024)
 
 
 def lasts(micros):
@@ -25,6 +27,50 @@
 
 NT = (((1,), (1,)), ((), ()))
 TN = (((0,), (0,)), ((), ()))
+
+
+def run(kernel, operands, outs, scratch, micros, name, late=0):
+    where = [SMEM if x.dtype == jnp.int32 else HBM for x in operands]
+    held = [pltpu.VMEM(x.shape, x.dtype) for x, spec in zip(operands, where) if spec is HBM]
+
+    def body(*refs):
+        given, rest = refs[: len(operands)], refs[len(operands) :]
+        slots, sems, rest = rest[-1 - len(held) : -1], rest[-1], rest[: -1 - len(held)]
+        copies, arrays = [], []
+        for ref, spec in zip(given, where):
+            if spec is HBM:
+                slot = slots[len(copies)]
+                copies.append(pltpu.make_async_copy(ref, slot, sems.at[len(copies)]))
+                ref = slot
+            arrays.append(ref)
+        for copy in copies:
+            copy.start()
+        now = len(copies) - late
+        for copy in copies[:now]:
+            copy.wait()
+        if late:
+            def arrive():
+                for copy in copies[now:]:
+                    copy.wait()
+
+            kernel(arrive, *arrays, *rest)
+        else:
+            kernel(*arrays, *rest)
+
+    return pl.pallas_call(
+        body,
+        out_shape=tuple(jax.ShapeDtypeStruct(shape, kind) for shape, kind in outs),
+        in_specs=where,
+        out_specs=(VMEM,) * len(outs),
+        scratch_shapes=[
+            *(pltpu.VMEM(shape, kind) for shape, kind in scratch),
+            *held,
+            pltpu.SemaphoreType.DMA((len(held),)),
+        ],
+        compiler_params=PARAMS,
+        cost_estimate=lasts(micros),
+        name=name,
+    )(*operands)
 
 
 def place_kernel(clusters, ids_ref, pos_ref, bias_ref):
@@ -81,7 +127,7 @@
         for u in range(4):
             inner = jnp.sum(found[u][:CAP] * some[u][1], axis=0, keepdims=True)
             outer = found[u][CAP : CAP + 1] * 64.0 + found[u][2 * CAP : 2 * CAP + 1]
-            pos_ref[pl.ds(step * 4 + u, 1), :] = (outer + inner).astype(jnp.int32)
+            pos_ref[pl.ds(step * 4 + u, 1), :] = (outer + inner).astype(jnp.int32) + CAP
         return carry
 
     lax.fori_loop(0, blocks // 4, find, 0)
@@ -112,52 +158,48 @@
 
 def place(ids, clusters):
     blocks, _, lanes = ids.shape
-    rows = blocks * lanes
-    return pl.pallas_call(
-        functools.partial(place_kernel, clusters),
-        out_shape=(
-            jax.ShapeDtypeStruct((blocks, lanes), jnp.int32),
-            jax.ShapeDtypeStruct((rows, WIN), jnp.bfloat16),
-        ),
-        in_specs=[VMEM],
-        out_specs=(VMEM, VMEM),
-        compiler_params=PARAMS,
-        cost_estimate=lasts(10),
-        name="place",
-    )(ids)
+    return run(
+        functools.partial(place_kernel, clusters), (ids,),
+        (((blocks, lanes), jnp.int32), ((blocks * lanes, WIN), jnp.bfloat16)), (), 8, "place",
+    )
 
 
 ROWS_AT_ONCE = 16
 
 
-def move_in(pos_ref, block_of, load, wide, sorted_ref, offset, count):
+def move_in(pos_ref, block_of, loads, wides, sorted_refs, count):
     lanes = pos_ref.shape[1]
 
     def one(r, carry):
         b = block_of(r)
-        wide[...] = load(r).astype(jnp.float32)
+        for load, wide in zip(loads, wides):
+            wide[...] = load(r).astype(jnp.float32)
         for first in range(0, lanes, ROWS_AT_ONCE):
-            held = [wide[pl.ds(first + row, 1), :] for row in range(ROWS_AT_ONCE)]
-            for row in range(ROWS_AT_ONCE):
-                sorted_ref[pl.ds(pos_ref[b, first + row] + offset, 1), :] = held[row]
+            rows = range(first, first + ROWS_AT_ONCE)
+            places = [pl.ds(pos_ref[b, row], 1) for row in rows]
+            held = [[wide[pl.ds(row, 1), :] for row in rows] for wide in wides]
+            for i, at in enumerate(places):
+                for ref, some in zip(sorted_refs, held):
+                    ref[at, :] = some[i]
         return carry
 
     lax.fori_loop(0, count, one, 0)
 
 
-def move_out(pos_ref, block_of, sorted_ref, offset, wide, store, count):
+def move_out(pos_ref, block_of, sorted_refs, wides, stores, count):
     lanes = pos_ref.shape[1]
 
     def one(r, carry):
         b = block_of(r)
         for first in range(0, lanes, ROWS_AT_ONCE):
-            held = [
-                sorted_ref[pl.ds(pos_ref[b, first + row] + offset, 1), :]
-                for row in range(ROWS_AT_ONCE)
-            ]
-            for row in range(ROWS_AT_ONCE):
-                wide[pl.ds(first + row, 1), :] = held[row]
-        store(r, wide[...])
+            rows = range(first, first + ROWS_AT_ONCE)
+            places = [pl.ds(pos_ref[b, row], 1) for row in rows]
+            held = [[ref[at, :] for at in places] for ref in sorted_refs]
+            for i, row in enumerate(rows):
+                for wide, some in zip(wides, held):
+                    wide[pl.ds(row, 1), :] = some[i]
+        for store, wide in zip(stores, wides):
+            store(r, wide[...])
         return carry
 
     lax.fori_loop(0, count, one, 0)
@@ -172,20 +214,24 @@
 
 
 def scores_kernel(
-    scale, pos_ref, rows_ref, bias_ref, query_ref, key_ref, probs_ref, wide, query, key
+    scale, arrive, pos_ref, rows_ref, bias_ref, query_ref, key_ref, probs_ref,
+    wide, query, key, more,
 ):
     bf, f32 = jnp.bfloat16, jnp.float32
     blocks, lanes = pos_ref.shape
     rows = blocks * lanes
     edge = jnp.zeros((CAP, wide.shape[1]), f32)
-    for part, (ref, out) in enumerate(((query, query_ref), (key, key_ref))):
+    for ref in (query, key):
         ref[pl.ds(0, CAP), :] = edge
         ref[pl.ds(rows + CAP, CAP), :] = edge
-        move_in(
-            pos_ref, lambda b: b,
-            lambda b, part=part: rows_ref[b, pl.ds(part * lanes, lanes), :], wide, ref, CAP, blocks,
-        )
-        out[...] = ref[...].astype(bf)
+    move_in(
+        pos_ref, lambda b: b,
+        [lambda b, part=part: rows_ref[b, pl.ds(part * lanes, lanes), :] for part in range(2)],
+        [wide, more], [query, key], blocks,
+    )
+    query_ref[...] = query[...].astype(bf)
+    key_ref[...] = key[...].astype(bf)
+    arrive()
 
     def some(step, carry):
         tiles, windows, inner = tiles_of(step)
@@ -198,14 +244,14 @@
         weights = [jnp.exp(s - top) for s, top in zip(scores, tops)]
         sums = [jnp.sum(w, axis=1, keepdims=True) for w in weights]
         for at, w, total in zip(tiles, weights, sums):
-            probs_ref[at, :] = w / total
+            probs_ref[at, :] = (w / total).astype(bf)
         return carry
 
     lax.fori_loop(0, rows // TILE // UNROLL, some, 0)
 
 
 def attend_kernel(
-    low, me_ref, pos_ref, rows_ref, probs_ref, *refs
+    low, arrive, me_ref, pos_ref, rows_ref, probs_ref, *refs
 ):
     parts, (sorted_ref, value_ref, wide, value, att) = refs[:low], refs[low:]
     bf, f32 = jnp.bfloat16, jnp.float32
@@ -215,16 +261,17 @@
     edge = jnp.zeros((CAP, wide.shape[1]), f32)
     value[pl.ds(0, CAP), :] = edge
     value[pl.ds(rows + CAP, CAP), :] = edge
-    move_in(pos_ref, lambda b: b, lambda b: rows_ref[b], wide, value, CAP, blocks)
+    move_in(pos_ref, lambda b: b, [lambda b: rows_ref[b]], [wide], [value], blocks)
     value_ref[...] = value[...].astype(bf)
+    arrive()
 
     def some(step, carry):
-        tiles, windows, _ = tiles_of(step)
+        tiles, windows, inner = tiles_of(step)
         vs = [value_ref[at, :] for at in windows]
-        probs = [probs_ref[at, :].astype(bf) for at in tiles]
+        probs = [probs_ref[at, :] for at in tiles]
         attended = [jnp.dot(p, v, preferred_element_type=f32) for p, v in zip(probs, vs)]
-        for at, one in zip(tiles, attended):
-            att[at, :] = one
+        for at, to, one in zip(tiles, inner, attended):
+            att[to, :] = one
             sorted_ref[at, :] = one.astype(bf)
         return carry
 
@@ -234,32 +281,36 @@
         def put(r, block, k=k):
             parts[k][pl.ds(pl.multiple_of(r * lanes, lanes), lanes), :] = block.astype(bf)
 
-        move_out(pos_ref, lambda r, k=k: r * low + (me_ref[0] ^ k), att, 0, wide, put, high)
+        move_out(
+            pos_ref, lambda r, k=k: (me_ref[1] ^ r) * low + (me_ref[0] ^ k),
+            [att], [wide], [put], high,
+        )
 
 
 def value_kernel(
-    low, me_ref, pos_ref, probs_ref, *refs
+    low, arrive, me_ref, pos_ref, *refs
 ):
-    parts, (out_ref, sorted_ref, wide, grad, grad_value) = refs[:low], refs[low:]
+    parts, (probs_ref, out_ref, sorted_ref, wide, grad, grad_value) = refs[:low], refs[low:]
     bf, f32 = jnp.bfloat16, jnp.float32
     blocks, lanes = pos_ref.shape
     rows = blocks * lanes
     high = blocks // low
     for k in range(low):
         def block_of(r, k=k):
-            return r * low + (me_ref[0] ^ k)
+            return (me_ref[1] ^ r) * low + (me_ref[0] ^ k)
 
         def load(r, k=k):
             return parts[k][pl.ds(pl.multiple_of(r * lanes, lanes), lanes), :]
 
-        move_in(pos_ref, block_of, load, wide, grad, 0, high)
-    sorted_ref[...] = grad[...].astype(bf)
+        move_in(pos_ref, block_of, [load], [wide], [grad], high)
+    sorted_ref[...] = grad[pl.ds(CAP, rows), :].astype(bf)
     grad_value[...] = jnp.zeros_like(grad_value)
+    arrive()
 
     def some(step, carry):
         tiles, windows, _ = tiles_of(step)
         gs = [sorted_ref[at, :] for at in tiles]
-        probs = [probs_ref[at, :].astype(bf) for at in tiles]
+        probs = [probs_ref[at, :] for at in tiles]
         more = [lax.dot_general(p, g, TN, preferred_element_type=f32) for p, g in zip(probs, gs)]
         for at, one in zip(windows, more):
             grad_value[at, :] += one
@@ -270,12 +321,12 @@
     def put(b, block):
         out_ref[b] = block.astype(bf)
 
-    move_out(pos_ref, lambda b: b, grad_value, CAP, wide, put, blocks)
+    move_out(pos_ref, lambda b: b, [grad_value], [wide], [put], blocks)
 
 
 def rest_kernel(
     scale, pos_ref, grad_ref, sorted_ref, query_ref, key_ref, value_ref, probs_ref,
-    out_ref, wide, grad_query, grad_key,
+    out_ref, wide, grad_query, grad_key, more,
 ):
     bf, f32 = jnp.bfloat16, jnp.float32
     blocks, lanes = pos_ref.shape
@@ -295,13 +346,14 @@
             jnp.sum(g.astype(f32) * one, axis=1, keepdims=True) for g, one in zip(gs, attended)
         ]
         grad_scores = [
-            (p * (gp - delta)).astype(bf) for p, gp, delta in zip(probs, grad_probs, deltas)
+            (p.astype(f32) * (gp - delta)).astype(bf)
+            for p, gp, delta in zip(probs, grad_probs, deltas)
         ]
         grad_queries = [jnp.dot(d, k, preferred_element_type=f32) for d, k in zip(grad_scores, ks)]
         more_keys = [
             lax.dot_general(d, q, TN, preferred_element_type=f32) for d, q in zip(grad_scores, qs)
         ]
-        for at, one in zip(tiles, grad_queries):
+        for at, one in zip(inner, grad_queries):
             grad_query[at, :] = one
         for at, one in zip(windows, more_keys):
             grad_key[at, :] += one
@@ -314,13 +366,17 @@
             out_ref[b, pl.ds(part * lanes, lanes), :] = (block * scale).astype(bf)
         return store
 
-    move_out(pos_ref, lambda b: b, grad_query, 0, wide, put(0), blocks)
-    move_out(pos_ref, lambda b: b, grad_key, CAP, wide, put(1), blocks)
-
-
-def project_back_kernel(low, rows_ref, *refs):
-    bf, f32 = jnp.bfloat16, jnp.float32
-    weights, outs = refs[:low], refs[low:]
+    move_out(
+        pos_ref, lambda b: b, [grad_query, grad_key], [wide, more], [put(0), put(1)], blocks
+    )
+
+
+def project_back_kernel(low, *refs):
+    bf, f32 = jnp.bfloat16, jnp.float32
+    weights, blocks, outs, rows_ref = refs[:low], refs[low : -1 - low], refs[-1 - low : -1], refs[-1]
+    rows = blocks[0].shape[0]
+    for r, block in enumerate(blocks):
+        rows_ref[pl.ds(r * rows, rows), :] = block[...]
     for k in range(0, low, 2):
         weight = jnp.concatenate([weights[k][...], weights[k + 1][...]], axis=1)
         both = jnp.dot(rows_ref[...], weight, preferred_element_type=f32).astype(bf)
@@ -331,16 +387,19 @@
 
 def project_kernel(low, chunk, *refs):
     bf, f32 = jnp.bfloat16, jnp.float32
-    weights, parts, out_ref = refs[:low], refs[low:-1], refs[-1]
+    weights, parts, outs = refs[:low], refs[low : 2 * low], refs[2 * low :]
     rows = jnp.concatenate([ref[...] for ref in parts], axis=1)
+    count, columns = outs[0].shape
 
     def one(c, carry):
         at = pl.ds(pl.multiple_of(c * chunk, chunk), chunk)
         weight = jnp.concatenate([ref[at, :] for ref in weights], axis=1)
-        out_ref[:, at] = lax.dot_general(rows, weight, NT, preferred_element_type=f32).astype(bf)
-        return carry
-
-    lax.fori_loop(0, out_ref.shape[1] // chunk, one, 0)
+        mixed = lax.dot_general(rows, weight, NT, preferred_element_type=f32).astype(bf)
+        for r, out in enumerate(outs):
+            out[:, at] = mixed[r * count : (r + 1) * count]
+        return carry
+
+    lax.fori_loop(0, columns // chunk, one, 0)
 
 
 def place_in_plane(low):
@@ -348,32 +407,22 @@
     return jnp.stack([index % low, index // low]).astype(jnp.int32)
 
 
-def project_back(weights, rows):
-    low = len(weights)
+def project_back(weights, blocks):
+    low, bf = len(weights), jnp.bfloat16
     size = weights[0].shape[1]
-    return pl.pallas_call(
-        functools.partial(project_back_kernel, low),
-        out_shape=(jax.ShapeDtypeStruct((rows.shape[0], size), jnp.bfloat16),) * low,
-        in_specs=[VMEM] * (1 + low),
-        out_specs=(VMEM,) * low,
-        compiler_params=PARAMS,
-        cost_estimate=lasts(8),
-        name="project_back",
-    )(rows, *weights)
-
-
-def project(weights, parts):
-    low = len(weights)
-    columns = weights[0].shape[0]
-    return pl.pallas_call(
-        functools.partial(project_kernel, low, math.gcd(columns, 512)),
-        out_shape=jax.ShapeDtypeStruct((parts[0].shape[0], columns), jnp.bfloat16),
-        in_specs=[VMEM] * (2 * low),
-        out_specs=VMEM,
-        compiler_params=PARAMS,
-        cost_estimate=lasts(6),
-        name="project",
-    )(*weights, *parts)
+    rows, depth = blocks[0].shape[0] * len(blocks), blocks[0].shape[1]
+    return run(
+        functools.partial(project_back_kernel, low), (*weights, *blocks),
+        (((rows, size), bf),) * low, (((rows, depth), bf),), 8, "project_back",
+    )
+
+
+def project(weights, parts, high):
+    low, columns = len(weights), weights[0].shape[0]
+    return run(
+        functools.partial(project_kernel, low, math.gcd(columns, 512)), (*weights, *parts),
+        (((parts[0].shape[0] // high, columns), jnp.bfloat16),) * high, (), 6, "project",
+    )
 
 
 def head_kernels(pos, size, low):
@@ -381,45 +430,37 @@
     rows = blocks * lanes
     bf, f32 = jnp.bfloat16, jnp.float32
     scale = 1.0 / math.sqrt(size)
-    plain, padded = (rows, size), (rows + 2 * CAP, size)
+    plain, padded, wide = (rows, size), (rows + 2 * CAP, size), (lanes, size)
     me = place_in_plane(low)
 
-    def call(kernel, operands, outs, scratch, micros, name):
-        return pl.pallas_call(
-            kernel,
-            out_shape=tuple(jax.ShapeDtypeStruct(shape, kind) for shape, kind in outs),
-            in_specs=[SMEM if x.dtype == jnp.int32 else VMEM for x in operands],
-            out_specs=(VMEM,) * len(outs),
-            scratch_shapes=[pltpu.VMEM(shape, f32) for shape in ((lanes, size), *scratch)],
-            compiler_params=PARAMS,
-            cost_estimate=lasts(micros),
-            name=name,
-        )(*operands)
+    def call(kernel, operands, outs, scratch, micros, name, late=0):
+        scratch = [(shape, f32) for shape in (wide, *scratch)]
+        return run(kernel, operands, outs, scratch, micros, name, late)
 
     def scores(query_key, bias):
         return call(
             functools.partial(scores_kernel, scale), (pos, query_key, bias),
-            ((padded, bf), (padded, bf), ((rows, WIN), f32)), (padded, padded), 12, "scores",
+            ((padded, bf), (padded, bf), ((rows, WIN), bf)), (padded, padded, wide), 12, "scores", 1,
         )
 
     def attend(value, probs):
         return call(
             functools.partial(attend_kernel, low), (me, pos, value, probs),
             (((blocks // low * lanes, size), bf),) * low + ((plain, bf), (padded, bf)),
-            (padded, plain), 12, "attend",
+            (padded, padded), 12, "attend", 1,
         )
 
     def grad_value(grads, probs):
         return call(
-            functools.partial(value_kernel, low), (me, pos, probs, *grads),
-            (((blocks, lanes, size), bf), (plain, bf)), (plain, padded), 12, "grad_value",
+            functools.partial(value_kernel, low), (me, pos, *grads, probs),
+            (((blocks, lanes, size), bf), (plain, bf)), (padded, padded), 12, "grad_value", 1,
         )
 
     def rest(grad, attended, query, key, value, probs):
         return call(
             functools.partial(rest_kernel, scale),
             (pos, grad, attended, query, key, value, probs),
-            (((blocks, 2 * lanes, size), bf),), (plain, padded), 16, "rest",
+            (((blocks, 2 * lanes, size), bf),), (padded, padded, wide), 16, "rest",
         )[0]
 
     return scores, attend, grad_value, rest
@@ -455,8 +496,8 @@
         out_shape=jax.ShapeDtypeStruct((heads, rows, size), arrays[0].dtype),
         in_specs=[block(array) for array in arrays],
         out_specs=pl.BlockSpec((step, rows, size), lambda i: (i, 0, 0)),
-        compiler_params=PARAMS,
-        cost_estimate=lasts(3),
+        compiler_params=SMALL,
+        cost_estimate=lasts(0.1),
         name="pack",
     )(*arrays)
 
@@ -479,7 +520,7 @@
         out_shape=(jax.ShapeDtypeStruct((rows, heads * size), packed.dtype),) * parts,
         in_specs=[pl.BlockSpec((step, parts * rows, size), lambda i: (i, 0, 0))],
         out_specs=(pl.BlockSpec((rows, step * size), lambda i: (0, i)),) * parts,
-        compiler_params=PARAMS,
+        compiler_params=SMALL,
         cost_estimate=lasts(3),
         name="unpack",
     )(packed)
@@ -624,40 +665,59 @@
     owners = lax.axis_size("seq")
     columns_dev = out_weight.shape[1]
     high, low = split(owners)
-    stacks = [[h * low + p for h in range(high)] for p in range(low)]
-    bf = jnp.bfloat16
+    bf, f32 = jnp.bfloat16, jnp.float32
     together = lax.optimization_barrier
 
     def exchange(rows):
         return lax.all_to_all(rows, "seq", split_axis=0, concat_axis=0, tiled=True)
 
-    def swap(blocks, step=1):
-        pairs = [[(i, i ^ (k * step)) for i in range(owners)] for k in range(len(blocks))]
-        return [blocks[0]] + [
-            lax.ppermute(blocks[k], "seq", pairs[k]) for k in range(1, len(blocks))
-        ]
-
-    def gather_plane(block):
-        near = swap([block] * (low // 2), 2)
-        other = [(i, i ^ 1) for i in range(owners)]
-        return [x for one in near for x in (one, lax.ppermute(one, "seq", other))]
+    def send(block, bits):
+        return lax.ppermute(block, "seq", [(i, i ^ bits) for i in range(owners)])
+
+    def swap(blocks):
+        return [blocks[0]] + [send(blocks[k], k) for k in range(1, low)]
+
+    def gather_plane(block, after):
+        near = [block] + [send(block, k) for k in range(2, low, 2)]
+        near, after = together((near, after))
+        return [x for one in near for x in (one, send(one, 1))], after
+
+    def gather_stack(block, after):
+        blocks, bit = {0: block}, high // 2
+        while bit:
+            blocks |= {r | bit: send(one, bit * low) for r, one in blocks.items()}
+            bit //= 2
+            if bit == high // 4:
+                blocks, after = together((blocks, after))
+        return [blocks[r] for r in range(high)], after
+
+    def sum_stack(blocks):
+        blocks, bit = dict(enumerate(blocks)), 1
+        while bit < high:
+            blocks = {
+                r: (one.astype(f32) + send(blocks[r | bit], bit * low).astype(f32)).astype(bf)
+                for r, one in blocks.items()
+                if not r & bit
+            }
+            bit *= 2
+        return blocks[0]
 
     weight_rows = out_weight.T.reshape(columns_dev, heads_dev, head_size).transpose(1, 0, 2)
     ids = jnp.stack([cluster_id // rows_dev, cluster_id % rows_dev, slot_index], axis=1)
     ids = jnp.pad(ids, ((0, 0), (0, 13), (0, 0))).astype(bf)
     first = exchange(jnp.concatenate([weight_rows, ids], axis=1))
-    grad_out_stack = lax.all_gather(grad_out, "seq", axis=0, tiled=True, axis_index_groups=stacks)
+    grad_out_stack, first = gather_stack(grad_out, first)
     packed = pack((query_rows, key_rows), heads_dev)
     packed_value = pack((value_rows,), heads_dev)
     packed, packed_value, first = together((packed, packed_value, first))
     arrived = exchange(packed)
-    weights = gather_plane(first[:, :columns_dev].reshape(owners * columns_dev, head_size))
-    pos, bias = place(first[:, columns_dev:], CLU_DEV * owners)
-    packed_value, arrived, pos, bias, weights = together(
-        (packed_value, arrived, pos, bias, weights)
-    )
+    placed = place(first[:, columns_dev:], CLU_DEV * owners)
+    head_weight = first[:, :columns_dev].reshape(owners * columns_dev, head_size)
+    weights, (pos, bias) = gather_plane(head_weight, placed)
+    grad_heads = project_back(weights, grad_out_stack)
+    packed_value, arrived, grad_heads = together((packed_value, arrived, grad_heads))
     value = exchange(packed_value)
-    grad_heads = swap(project_back(weights, grad_out_stack))
+    grad_heads = swap(grad_heads)
     scores, attend, grad_of_value, rest = head_kernels(pos, head_size, low)
     query, key, probs = scores(arrived, bias)
     grad_value, grad_sorted = grad_of_value(grad_heads, probs)
@@ -669,10 +729,7 @@
     grads, attended = together((grads, attended))
     grads, back_value = together((grads, back_value))
     back = exchange(grads)
-    partial = project(weights, attended)
-    mixed = lax.psum_scatter(
-        partial, "seq", scatter_dimension=0, tiled=True, axis_index_groups=stacks
-    )
+    mixed = sum_stack(project(weights, attended, high))
     return (mixed, *unpack(back, 2), *unpack(back_value, 1))
 
 

time: 315 us -> 297 us (0.943)
  waiting for transfers between devices: 163 us -> 144 us
  between operations: 14.5 us -> 1.12 us
  starting transfers between devices: 43.7 us -> 56.8 us
  local copies, waits for them, and re-layouts: 14.1 us -> 6.25 us
  Pallas kernels: 76 us -> 82.2 us
    all_to_all x5, waiting for transfers between devices: 117 us -> 0.01 us  [exchange(): return lax.all_to_all(rows, 'seq', split_axis=0, concat_axis=0, tiled=True)]
    ppermute x21 -> x27, waiting for transfers between devices: 45.1 us -> 144 us  [send(): return lax.ppermute(block, 'seq', [(i, i ^ bits) for i in range(owners)])]
    ppermute x21 -> x27, starting transfers between devices: 18.1 us -> 28.9 us  [send(): return lax.ppermute(block, 'seq', [(i, i ^ bits) for i in range(owners)])]
    unnamed x66 -> x44, local copies, waits for them, and re-layouts: 11.7 us -> 2.62 us
    pallas_call x7, Pallas kernels: 66.7 us -> 74.8 us  [run(): pl.pallas_call(body, out_shape=tuple((jax.ShapeDtypeStruct(shape, kind) f...]
  transfers between devices with their start and end apart: 28 -> 32, of which waited for: 8 -> 10; matrix products, arithmetic and copies ran while one was open for 1% -> 2% of each run, Pallas kernels for 24% -> 27%
where the time goes in v4:
time: 297 us; the launch traced here: 296 us
  waiting for transfers between devices  144 us (48%)
  Pallas kernels  82.2 us (28%)
  starting transfers between devices  56.8 us (19%)
  local copies, waits for them, and re-layouts  6.25 us (2%)
  other arithmetic  5.26 us (2%)
    ppermute x27, waiting for transfers between devices, send(): return lax.ppermute(block, 'seq', [(i, i ^ bits) for i in range(owners)])  144 us
    pallas_call x7, Pallas kernels, run(): pl.pallas_call(body, out_shape=tuple((jax.ShapeDtypeStruct(shape, kind) f...  74.8 us
    ppermute x27, starting transfers between devices, send(): return lax.ppermute(block, 'seq', [(i, i ^ bits) for i in range(owners)])  28.9 us
    all_to_all x5, starting transfers between devices, exchange(): return lax.all_to_all(rows, 'seq', split_axis=0, concat_axis=0, tiled=True)  27.9 us
  transfers between devices with their start and end apart: 32, of which 10 were waited for; matrix products, arithmetic and copies ran while one was open for 2% of the time, Pallas kernels for 27%

profile of v4, /device:TPU:0, one launch (start us, length us, event | category | flops | bytes accessed | tf_op | source)
XLA Modules:
  0.0 295.6 jit_solution(2228140267529696734)
XLA Ops:
  3.4 7.3 %all-to-all-start = ((bf16[32,80,128]{2,1,0:T(8,128)(2,1)}), bf16[32,80,128]{2,1,0:T(8,128)(2,1)S(1)}, u32[]{:S(2)}, u32[]{:S(2)}) async-start(bf16[32,80,128]{2,1,0:T(8,128)(2,1)} %pad_maximum_fusion), calls=%async_computation | async-start | bytes 1310720 | tf_op jit(solution)/shard_map/all_to_all | solution.py:672
  10.7 2.7 collective-permute-start
  15.1 2.1 pack.2
  17.2 33.8 %collective-permute-done.refs_10_ = bf16[128,2048]{1,0:T(8,128)(2,1)} collective-permute-done((bf16[128,2048]{1,0:T(8,128)(2,1)S(1)}, bf16[128,2048]{1,0:T(8,128)(2,1)}, u32[]{:S(2)}, u32[]{:S(2)}) %collective-permute-start) | collective-permute-done | bytes 524320 | tf_op jit(solution)/shard_map/ppermute | solution.py:675
  51.9 3.6 %all-to-all-start.1 = ((bf16[32,256,128]{2,1,0:T(8,128)(2,1)}), bf16[32,256,128]{2,1,0:T(8,128)(2,1)S(1)}, u32[]{:S(2)}, u32[]{:S(2)}) async-start(bf16[32,256,128]{2,1,0:T(8,128)(2,1)} %pack.2), calls=%async_computation.1 | async-start | bytes 4194304 | tf_op jit(solution)/shard_map/all_to_all | solution.py:672
  55.5 1.9 slice.6
  57.4 2.7 collective-permute-start.3
  60.9 1.8 collective-permute-start.8
  64.5 8.7 %place.1 = (s32[32,128]{1,0:T(8,128)}, bf16[4096,128]{1,0:T(8,128)(2,1)}) custom-call(bf16[32,16,128]{2,1,0:T(8,128)(2,1)} %slice.7.refs_0_), custom_call_target="tpu_custom_call" | custom-call | bytes 28000000 | tf_op jit(solution)/shard_map/place/pallas_call | solution.py:60
  73.2 19.1 %collective-permute-done.3.refs_6_ = bf16[2048,128]{1,0:T(8,128)(2,1)} collective-permute-done((bf16[2048,128]{1,0:T(8,128)(2,1)}, bf16[2048,128]{1,0:T(8,128)(2,1)}, u32[]{:S(2)}, u32[]{:S(2)}) %collective-permute-start.3) | collective-permute-done | bytes 524320 | tf_op jit(solution)/shard_map/ppermute | solution.py:675
  92.4 11.1 %collective-permute-done.2.refs_4_ = bf16[2048,128]{1,0:T(8,128)(2,1)} collective-permute-done((bf16[2048,128]{1,0:T(8,128)(2,1)}, bf16[2048,128]{1,0:T(8,128)(2,1)}, u32[]{:S(2)}, u32[]{:S(2)}) %collective-permute-start.2) | collective-permute-done | bytes 524320 | tf_op jit(solution)/shard_map/ppermute | solution.py:675
  103.5 2.8 collective-permute-done.1.refs_2_
  107.3 7.4 %collective-permute-done.9.refs_11_ = bf16[128,2048]{1,0:T(8,128)(2,1)} collective-permute-done((bf16[128,2048]{1,0:T(8,128)(2,1)}, bf16[128,2048]{1,0:T(8,128)(2,1)}, u32[]{:S(2)}, u32[]{:S(2)}) %collective-permute-start.9) | collective-permute-done | bytes 524320 | tf_op jit(solution)/shard_map/ppermute | solution.py:675
  114.7 6.0 %project_back.1 = (bf16[512,128]{1,0:T(8,128)(2,1)}, bf16[512,128]{1,0:T(8,128)(2,1)}, bf16[512,128]{1,0:T(8,128)(2,1)}, bf16[512,128]{1,0:T(8,128)(2,1)}, bf16[...) custom-call(bf16[2048,128]{1,0:T(8,128)(2,1)} %bitcast.5.refs_0_, ...), custom_call_target="tpu_custom_call" | custom-call | bytes 28000000 | tf_op jit(solution)/shard_map/project_back/pallas_call | solution.py:60
  120.8 5.1 %all-to-all-start.2 = ((bf16[32,128,128]{2,1,0:T(8,128)(2,1)}), bf16[32,128,128]{2,1,0:T(8,128)(2,1)}, u32[]{:S(2)}, u32[]{:S(2)}) async-start(bf16[32,128,128]{2,1,0:T(8,128)(2,1)} %pack.3), calls=%async_computation.2 | async-start | bytes 2097152 | tf_op jit(solution)/shard_map/all_to_all | solution.py:672
  129.6 2.6 collective-permute-start.15
  132.2 8.1 %collective-permute-done.11.refs_4_ = bf16[512,128]{1,0:T(8,128)(2,1)S(1)} collective-permute-done((bf16[512,128]{1,0:T(8,128)(2,1)S(1)}, bf16[512,128]{1,0:T(8,128)(2,1)S(1)}, u32[]{:S(2)}, u32[]{:S(2)}) %collective-permute-start.11) | collective-permute-done | bytes 131104 | tf_op jit(solution)/shard_map/ppermute | solution.py:675
  141.1 12.3 %scores.1 = (bf16[4160,128]{1,0:T(8,128)(2,1)}, bf16[4160,128]{1,0:T(8,128)(2,1)}, bf16[4096,128]{1,0:T(8,128)(2,1)}) custom-call(s32[32,128]{1,0:T(8,128)} %get-tuple-element.78.refs_0_.refs_1_, bf16[32,256,128]{2,1,0:T(8,128)(2,1)} %copy-done.6, bf16[4096,128]{1,0:T(8,128)(2,1)} %get-tuple-element.100.refs_2_), custom_call_target="tpu_custom_call" | custom-call | bytes 42000000 | tf_op jit(solution)/shard_map/scores/pallas_call | solution.py:60
  154.1 13.2 %grad_value.1 = (bf16[32,128,128]{2,1,0:T(8,128)(2,1)}, bf16[4096,128]{1,0:T(8,128)(2,1)}) custom-call(s32[2]{0:T(128)} %pad_add_fusion.refs_0_, s32[32,128]{1,0:T(8,128)} %get-tuple-element.78.refs_0_.refs_1_, bf16[512,128]{1,0:T(8,128)(2,1)} %get-tuple-element.91.refs_2_, bf16[512,128]{1,0:T(8,128)(2,1)} %copy-done.10, bf16[512,128]{1,0:T(8,128)(2,1)} %copy-done.11, ...), custom_call_target="tpu_custom_call" | custom-call | bytes 42000000 | tf_op jit(solution)/shard_map/grad_value/pallas_call | solution.py:60
  167.3 5.5 %all-to-all-start.3 = ((bf16[32,128,128]{2,1,0:T(8,128)(2,1)}), bf16[32,128,128]{2,1,0:T(8,128)(2,1)S(1)}, u32[]{:S(2)}, u32[]{:S(2)}) async-start(bf16[32,128,128]{2,1,0:T(8,128)(2,1)} %get-tuple-element.131), calls=%async_computation.3 | async-start | bytes 2097152 | tf_op jit(solution)/shard_map/all_to_all | solution.py:672
  172.8 12.9 %attend.1 = (bf16[512,128]{1,0:T(8,128)(2,1)}, bf16[512,128]{1,0:T(8,128)(2,1)}, bf16[512,128]{1,0:T(8,128)(2,1)}, bf16[512,128]{1,0:T(8,128)(2,1)}, bf16[512,12...) custom-call(s32[2]{0:T(128)} %pad_add_fusion.refs_0_, ...), custom_call_target="tpu_custom_call" | custom-call | bytes 42000000 | tf_op jit(solution)/shard_map/attend/pallas_call | solution.py:60
  187.7 1.7 collective-permute-start.20
  189.5 2.6 collective-permute-start.22
  193.7 14.8 %rest.1 = bf16[32,256,128]{2,1,0:T(8,128)(2,1)} custom-call(s32[32,128]{1,0:T(8,128)} %get-tuple-element.78.refs_0_.refs_1_, bf16[4096,128]{1,0:T(8,128)(2,1)} %get-tuple-element.102.refs_1_, bf16[4096,128]{1,0:T(8,128)(2,1)} %get-tuple-element.106.refs_2_, bf16[4160,128]{1,0:T(8,128)(2,1)} %get-tuple-element.107.refs_3_, ...), custom_call_target="tpu_custom_call" | custom-call | bytes 56000000 | tf_op jit(solution)/shard_map/rest/pallas_call | solution.py:60
  209.8 6.4 %all-to-all-start.4 = ((bf16[32,256,128]{2,1,0:T(8,128)(2,1)}), bf16[32,256,128]{2,1,0:T(8,128)(2,1)S(1)}, u32[]{:S(2)}, u32[]{:S(2)}) async-start(bf16[32,256,128]{2,1,0:T(8,128)(2,1)} %rest.1), calls=%async_computation.4 | async-start | bytes 4194304 | tf_op jit(solution)/shard_map/all_to_all | solution.py:672
  216.2 6.8 %project.1 = (bf16[128,2048]{1,0:T(8,128)(2,1)}, bf16[128,2048]{1,0:T(8,128)(2,1)}, bf16[128,2048]{1,0:T(8,128)(2,1)}, bf16[128,2048]{1,0:T(8,128)(2,1)}) custom-call(bf16[2048,128]{1,0:T(8,128)(2,1)} %bitcast.5.refs_0_, bf16[2048,128]{1,0:T(8,128)(2,1)} %collective-permute-done.4.refs_1_, bf16[2048,128]{1,0:T(8,128)(2,1)} %collective-permute-done.1.refs_2_, ...), custom_call_target="tpu_custom_call" | custom-call | bytes 21000000 | tf_op jit(solution)/shard_map/project/pallas_call | solution.py:60
  223.0 1.8 collective-permute-start.25
  225.1 37.8 %collective-permute-done.25 = bf16[128,2048]{1,0:T(8,128)(2,1)S(1)} collective-permute-done((bf16[128,2048]{1,0:T(8,128)(2,1)}, bf16[128,2048]{1,0:T(8,128)(2,1)S(1)}, u32[]{:S(2)}, u32[]{:S(2)}) %collective-permute-start.25) | collective-permute-done | bytes 524320 | tf_op jit(solution)/shard_map/ppermute | solution.py:675
  264.1 4.3 %collective-permute-start.26 = (bf16[128,2048]{1,0:T(8,128)(2,1)S(1)}, bf16[128,2048]{1,0:T(8,128)(2,1)S(1)}, u32[]{:S(2)}, u32[]{:S(2)}) collective-permute-start(bf16[128,2048]{1,0:T(8,128)(2,1)S(1)} %add_convert_fusion.1), channel_id=1, source_target_pairs={{0,16},{1,17},{2,18},{3,19},{4,20},{5,21},{6,22},{7,23},{8,24},{9,... | collective-permute-start | bytes 1572872 | tf_op jit(solution)/shard_map/ppermute | solution.py:675
  268.4 15.9 %collective-permute-done.24 = bf16[128,2048]{1,0:T(8,128)(2,1)S(1)} collective-permute-done((bf16[128,2048]{1,0:T(8,128)(2,1)}, bf16[128,2048]{1,0:T(8,128)(2,1)S(1)}, u32[]{:S(2)}, u32[]{:S(2)}) %collective-permute-start.24) | collective-permute-done | bytes 524320 | tf_op jit(solution)/shard_map/ppermute | solution.py:675
  284.2 6.7 %collective-permute-done.26 = bf16[128,2048]{1,0:T(8,128)(2,1)S(1)} collective-permute-done((bf16[128,2048]{1,0:T(8,128)(2,1)S(1)}, bf16[128,2048]{1,0:T(8,128)(2,1)S(1)}, u32[]{:S(2)}, u32[]{:S(2)}) %collective-permute-start.26) | collective-permute-done | bytes 524320 | tf_op jit(solution)/shard_map/ppermute | solution.py:675
  293.6 2.0 unpack.2
  (100 shorter events, 22.9 us)
Async XLA Ops:
  3.4 47.7 %all-to-all-start = ((bf16[32,80,128]{2,1,0:T(8,128)(2,1)}), bf16[32,80,128]{2,1,0:T(8,128)(2,1)S(1)}, u32[]{:S(2)}, u32[]{:S(2)}) async-start(bf16[32,80,128]{2,1,0:T(8,128)(2,1)} %pad_maximum_fusion), calls=%async_computation | async-start | bytes 1310720 | tf_op jit(solution)/shard_map/all_to_all | solution.py:672
  10.7 40.4 %collective-permute-start = (bf16[128,2048]{1,0:T(8,128)(2,1)S(1)}, bf16[128,2048]{1,0:T(8,128)(2,1)}, u32[]{:S(2)}, u32[]{:S(2)}) collective-permute-start(bf16[128,2048]{1,0:T(8,128)(2,1)S(1)} %copy-done.8), channel_id=1, source_target_pairs={{0,16},{1,17},{2,18},{3,19},{4,20},{5,21},{6,22},{7,23},{8,24},{9,... | collective-permute-start | bytes 1572872 | tf_op jit(solution)/shard_map/ppermute | solution.py:675
  51.9 68.9 %all-to-all-start.1 = ((bf16[32,256,128]{2,1,0:T(8,128)(2,1)}), bf16[32,256,128]{2,1,0:T(8,128)(2,1)S(1)}, u32[]{:S(2)}, u32[]{:S(2)}) async-start(bf16[32,256,128]{2,1,0:T(8,128)(2,1)} %pack.2), calls=%async_computation.1 | async-start | bytes 4194304 | tf_op jit(solution)/shard_map/all_to_all | solution.py:672
  57.4 35.0 %collective-permute-start.3 = (bf16[2048,128]{1,0:T(8,128)(2,1)}, bf16[2048,128]{1,0:T(8,128)(2,1)}, u32[]{:S(2)}, u32[]{:S(2)}) collective-permute-start(bf16[2048,128]{1,0:T(8,128)(2,1)} %bitcast.5.refs_0_), channel_id=1, source_target_pairs={{0,6},{1,7},{2,4},{3,5},{4,2},{5,3},{6,0},{7,1},{8,14},{9,15},{10,... | collective-permute-start | bytes 1572872 | tf_op jit(solution)/shard_map/ppermute | solution.py:675
  60.1 43.4 %collective-permute-start.2 = (bf16[2048,128]{1,0:T(8,128)(2,1)}, bf16[2048,128]{1,0:T(8,128)(2,1)}, u32[]{:S(2)}, u32[]{:S(2)}) collective-permute-start(bf16[2048,128]{1,0:T(8,128)(2,1)} %bitcast.5.refs_0_), channel_id=1, source_target_pairs={{0,4},{1,5},{2,6},{3,7},{4,0},{5,1},{6,2},{7,3},{8,12},{9,13},{10,... | collective-permute-start | bytes 1572872 | tf_op jit(solution)/shard_map/ppermute | solution.py:675
  60.6 45.7 %collective-permute-start.1 = (bf16[2048,128]{1,0:T(8,128)(2,1)}, bf16[2048,128]{1,0:T(8,128)(2,1)}, u32[]{:S(2)}, u32[]{:S(2)}) collective-permute-start(bf16[2048,128]{1,0:T(8,128)(2,1)} %bitcast.5.refs_0_), channel_id=1, source_target_pairs={{0,2},{1,3},{2,0},{3,1},{4,6},{5,7},{6,4},{7,5},{8,10},{9,11},{10,... | collective-permute-start | bytes 1572872 | tf_op jit(solution)/shard_map/ppermute | solution.py:675
  60.9 45.9 %collective-permute-start.8 = (bf16[128,2048]{1,0:T(8,128)(2,1)}, bf16[128,2048]{1,0:T(8,128)(2,1)}, u32[]{:S(2)}, u32[]{:S(2)}) collective-permute-start(bf16[128,2048]{1,0:T(8,128)(2,1)} %refs_8_), channel_id=1, source_target_pairs={{0,8},{1,9},{2,10},{3,11},{4,12},{5,13},{6,14},{7,15},{8,0},{9,1},... | collective-permute-start | bytes 1572872 | tf_op jit(solution)/shard_map/ppermute | solution.py:675
  64.2 50.4 %collective-permute-start.9 = (bf16[128,2048]{1,0:T(8,128)(2,1)}, bf16[128,2048]{1,0:T(8,128)(2,1)}, u32[]{:S(2)}, u32[]{:S(2)}) collective-permute-start(bf16[128,2048]{1,0:T(8,128)(2,1)} %collective-permute-done.refs_10_), channel_id=1, source_target_pairs={{0,8},{1,9},{2,10},{3,11},{4,12},{5,13},{6,14},{7,15},{8,0},{9,1},... | collective-permute-start | bytes 1572872 | tf_op jit(solution)/shard_map/ppermute | solution.py:675
  106.3 8.4 %collective-permute-start.4 = (bf16[2048,128]{1,0:T(8,128)(2,1)}, bf16[2048,128]{1,0:T(8,128)(2,1)}, u32[]{:S(2)}, u32[]{:S(2)}) collective-permute-start(bf16[2048,128]{1,0:T(8,128)(2,1)} %bitcast.5.refs_0_), channel_id=1, source_target_pairs={{0,1},{1,0},{2,3},{3,2},{4,5},{5,4},{6,7},{7,6},{8,9},{9,8},{10,11... | collective-permute-start | bytes 1572872 | tf_op jit(solution)/shard_map/ppermute | solution.py:675
  106.3 8.4 %collective-permute-start.5 = (bf16[2048,128]{1,0:T(8,128)(2,1)}, bf16[2048,128]{1,0:T(8,128)(2,1)}, u32[]{:S(2)}, u32[]{:S(2)}) collective-permute-start(bf16[2048,128]{1,0:T(8,128)(2,1)} %collective-permute-done.1.refs_2_), channel_id=1, source_target_pairs={{0,1},{1,0},{2,3},{3,2},{4,5},{5,4},{6,7},{7,6},{8,9},{9,8},{10,11... | collective-permute-start | bytes 1572872 | tf_op jit(solution)/shard_map/ppermute | solution.py:675
  106.8 7.9 %collective-permute-start.6 = (bf16[2048,128]{1,0:T(8,128)(2,1)}, bf16[2048,128]{1,0:T(8,128)(2,1)}, u32[]{:S(2)}, u32[]{:S(2)}) collective-permute-start(bf16[2048,128]{1,0:T(8,128)(2,1)} %collective-permute-done.2.refs_4_), channel_id=1, source_target_pairs={{0,1},{1,0},{2,3},{3,2},{4,5},{5,4},{6,7},{7,6},{8,9},{9,8},{10,11... | collective-permute-start | bytes 1572872 | tf_op jit(solution)/shard_map/ppermute | solution.py:675
  106.8 7.9 %collective-permute-start.7 = (bf16[2048,128]{1,0:T(8,128)(2,1)}, bf16[2048,128]{1,0:T(8,128)(2,1)}, u32[]{:S(2)}, u32[]{:S(2)}) collective-permute-start(bf16[2048,128]{1,0:T(8,128)(2,1)} %collective-permute-done.3.refs_6_), channel_id=1, source_target_pairs={{0,1},{1,0},{2,3},{3,2},{4,5},{5,4},{6,7},{7,6},{8,9},{9,8},{10,11... | collective-permute-start | bytes 1572872 | tf_op jit(solution)/shard_map/ppermute | solution.py:675
  120.8 46.5 %all-to-all-start.2 = ((bf16[32,128,128]{2,1,0:T(8,128)(2,1)}), bf16[32,128,128]{2,1,0:T(8,128)(2,1)}, u32[]{:S(2)}, u32[]{:S(2)}) async-start(bf16[32,128,128]{2,1,0:T(8,128)(2,1)} %pack.3), calls=%async_computation.2 | async-start | bytes 2097152 | tf_op jit(solution)/shard_map/all_to_all | solution.py:672
  125.9 3.7 %collective-permute-start.10 = (bf16[512,128]{1,0:T(8,128)(2,1)S(1)}, bf16[512,128]{1,0:T(8,128)(2,1)S(1)}, u32[]{:S(2)}, u32[]{:S(2)}) collective-permute-start(bf16[512,128]{1,0:T(8,128)(2,1)S(1)} %copy-done.21), channel_id=1, source_target_pairs={{0,1},{1,0},{2,3},{3,2},{4,5},{5,4},{6,7},{7,6},{8,9},{9,8},{10,11... | collective-permute-start | bytes 393224 | tf_op jit(solution)/shard_map/ppermute | solution.py:675
  126.1 14.2 %collective-permute-start.11 = (bf16[512,128]{1,0:T(8,128)(2,1)S(1)}, bf16[512,128]{1,0:T(8,128)(2,1)S(1)}, u32[]{:S(2)}, u32[]{:S(2)}) collective-permute-start(bf16[512,128]{1,0:T(8,128)(2,1)S(1)} %copy-done.20), channel_id=1, source_target_pairs={{0,2},{1,3},{2,0},{3,1},{4,6},{5,7},{6,4},{7,5},{8,10},{9,11},{10,... | collective-permute-start | bytes 393224 | tf_op jit(solution)/shard_map/ppermute | solution.py:675
  127.8 25.6 %collective-permute-start.12 = (bf16[512,128]{1,0:T(8,128)(2,1)}, bf16[512,128]{1,0:T(8,128)(2,1)S(1)}, u32[]{:S(2)}, u32[]{:S(2)}) collective-permute-start(bf16[512,128]{1,0:T(8,128)(2,1)} %get-tuple-element.94), channel_id=1, source_target_pairs={{0,3},{1,2},{2,1},{3,0},{4,7},{5,6},{6,5},{7,4},{8,11},{9,10},{10,... | collective-permute-start | bytes 393224 | tf_op jit(solution)/shard_map/ppermute | solution.py:675
  127.8 25.6 %collective-permute-start.13 = (bf16[512,128]{1,0:T(8,128)(2,1)}, bf16[512,128]{1,0:T(8,128)(2,1)}, u32[]{:S(2)}, u32[]{:S(2)}) collective-permute-start(bf16[512,128]{1,0:T(8,128)(2,1)} %get-tuple-element.95), channel_id=1, source_target_pairs={{0,4},{1,5},{2,6},{3,7},{4,0},{5,1},{6,2},{7,3},{8,12},{9,13},{10,... | collective-permute-start | bytes 393224 | tf_op jit(solution)/shard_map/ppermute | solution.py:675
  129.5 23.9 %collective-permute-start.14 = (bf16[512,128]{1,0:T(8,128)(2,1)}, bf16[512,128]{1,0:T(8,128)(2,1)}, u32[]{:S(2)}, u32[]{:S(2)}) collective-permute-start(bf16[512,128]{1,0:T(8,128)(2,1)} %get-tuple-element.96), channel_id=1, source_target_pairs={{0,5},{1,4},{2,7},{3,6},{4,1},{5,0},{6,3},{7,2},{8,13},{9,12},{10,... | collective-permute-start | bytes 393224 | tf_op jit(solution)/shard_map/ppermute | solution.py:675
  129.6 23.8 %collective-permute-start.15 = (bf16[512,128]{1,0:T(8,128)(2,1)}, bf16[512,128]{1,0:T(8,128)(2,1)}, u32[]{:S(2)}, u32[]{:S(2)}) collective-permute-start(bf16[512,128]{1,0:T(8,128)(2,1)} %get-tuple-element.97), channel_id=1, source_target_pairs={{0,6},{1,7},{2,4},{3,5},{4,2},{5,3},{6,0},{7,1},{8,14},{9,15},{10,... | collective-permute-start | bytes 393224 | tf_op jit(solution)/shard_map/ppermute | solution.py:675
  140.3 13.1 %collective-permute-start.16 = (bf16[512,128]{1,0:T(8,128)(2,1)}, bf16[512,128]{1,0:T(8,128)(2,1)}, u32[]{:S(2)}, u32[]{:S(2)}) collective-permute-start(bf16[512,128]{1,0:T(8,128)(2,1)} %get-tuple-element.98), channel_id=1, source_target_pairs={{0,7},{1,6},{2,5},{3,4},{4,3},{5,2},{6,1},{7,0},{8,15},{9,14},{10,... | collective-permute-start | bytes 393224 | tf_op jit(solution)/shard_map/ppermute | solution.py:675
  167.3 41.4 %all-to-all-start.3 = ((bf16[32,128,128]{2,1,0:T(8,128)(2,1)}), bf16[32,128,128]{2,1,0:T(8,128)(2,1)S(1)}, u32[]{:S(2)}, u32[]{:S(2)}) async-start(bf16[32,128,128]{2,1,0:T(8,128)(2,1)} %get-tuple-element.131), calls=%async_computation.3 | async-start | bytes 2097152 | tf_op jit(solution)/shard_map/all_to_all | solution.py:672
  185.7 3.8 %collective-permute-start.17 = (bf16[512,128]{1,0:T(8,128)(2,1)}, bf16[512,128]{1,0:T(8,128)(2,1)S(1)}, u32[]{:S(2)}, u32[]{:S(2)}) collective-permute-start(bf16[512,128]{1,0:T(8,128)(2,1)} %get-tuple-element.111), channel_id=1, source_target_pairs={{0,1},{1,0},{2,3},{3,2},{4,5},{5,4},{6,7},{7,6},{8,9},{9,8},{10,11... | collective-permute-start | bytes 393224 | tf_op jit(solution)/shard_map/ppermute | solution.py:675
  186.0 7.2 %collective-permute-start.18 = (bf16[512,128]{1,0:T(8,128)(2,1)}, bf16[512,128]{1,0:T(8,128)(2,1)S(1)}, u32[]{:S(2)}, u32[]{:S(2)}) collective-permute-start(bf16[512,128]{1,0:T(8,128)(2,1)} %get-tuple-element.112), channel_id=1, source_target_pairs={{0,2},{1,3},{2,0},{3,1},{4,6},{5,7},{6,4},{7,5},{8,10},{9,11},{10,... | collective-permute-start | bytes 393224 | tf_op jit(solution)/shard_map/ppermute | solution.py:675
  187.7 20.9 %collective-permute-start.19 = (bf16[512,128]{1,0:T(8,128)(2,1)}, bf16[512,128]{1,0:T(8,128)(2,1)S(1)}, u32[]{:S(2)}, u32[]{:S(2)}) collective-permute-start(bf16[512,128]{1,0:T(8,128)(2,1)} %get-tuple-element.113), channel_id=1, source_target_pairs={{0,3},{1,2},{2,1},{3,0},{4,7},{5,6},{6,5},{7,4},{8,11},{9,10},{10,... | collective-permute-start | bytes 393224 | tf_op jit(solution)/shard_map/ppermute | solution.py:675
  187.7 20.9 %collective-permute-start.20 = (bf16[512,128]{1,0:T(8,128)(2,1)}, bf16[512,128]{1,0:T(8,128)(2,1)S(1)}, u32[]{:S(2)}, u32[]{:S(2)}) collective-permute-start(bf16[512,128]{1,0:T(8,128)(2,1)} %get-tuple-element.114), channel_id=1, source_target_pairs={{0,4},{1,5},{2,6},{3,7},{4,0},{5,1},{6,2},{7,3},{8,12},{9,13},{10,... | collective-permute-start | bytes 393224 | tf_op jit(solution)/shard_map/ppermute | solution.py:675
  189.4 19.2 %collective-permute-start.21 = (bf16[512,128]{1,0:T(8,128)(2,1)}, bf16[512,128]{1,0:T(8,128)(2,1)S(1)}, u32[]{:S(2)}, u32[]{:S(2)}) collective-permute-start(bf16[512,128]{1,0:T(8,128)(2,1)} %get-tuple-element.115), channel_id=1, source_target_pairs={{0,5},{1,4},{2,7},{3,6},{4,1},{5,0},{6,3},{7,2},{8,13},{9,12},{10,... | collective-permute-start | bytes 393224 | tf_op jit(solution)/shard_map/ppermute | solution.py:675
  189.5 19.1 %collective-permute-start.22 = (bf16[512,128]{1,0:T(8,128)(2,1)}, bf16[512,128]{1,0:T(8,128)(2,1)S(1)}, u32[]{:S(2)}, u32[]{:S(2)}) collective-permute-start(bf16[512,128]{1,0:T(8,128)(2,1)} %get-tuple-element.116), channel_id=1, source_target_pairs={{0,6},{1,7},{2,4},{3,5},{4,2},{5,3},{6,0},{7,1},{8,14},{9,15},{10,... | collective-permute-start | bytes 393224 | tf_op jit(solution)/shard_map/ppermute | solution.py:675
  193.3 15.4 %collective-permute-start.23 = (bf16[512,128]{1,0:T(8,128)(2,1)}, bf16[512,128]{1,0:T(8,128)(2,1)S(1)}, u32[]{:S(2)}, u32[]{:S(2)}) collective-permute-start(bf16[512,128]{1,0:T(8,128)(2,1)} %get-tuple-element.117), channel_id=1, source_target_pairs={{0,7},{1,6},{2,5},{3,4},{4,3},{5,2},{6,1},{7,0},{8,15},{9,14},{10,... | collective-permute-start | bytes 393224 | tf_op jit(solution)/shard_map/ppermute | solution.py:675
  209.8 83.8 %all-to-all-start.4 = ((bf16[32,256,128]{2,1,0:T(8,128)(2,1)}), bf16[32,256,128]{2,1,0:T(8,128)(2,1)S(1)}, u32[]{:S(2)}, u32[]{:S(2)}) async-start(bf16[32,256,128]{2,1,0:T(8,128)(2,1)} %rest.1), calls=%async_computation.4 | async-start | bytes 4194304 | tf_op jit(solution)/shard_map/all_to_all | solution.py:672
  223.0 39.9 %collective-permute-start.25 = (bf16[128,2048]{1,0:T(8,128)(2,1)}, bf16[128,2048]{1,0:T(8,128)(2,1)S(1)}, u32[]{:S(2)}, u32[]{:S(2)}) collective-permute-start(bf16[128,2048]{1,0:T(8,128)(2,1)} %get-tuple-element.129), channel_id=1, source_target_pairs={{0,8},{1,9},{2,10},{3,11},{4,12},{5,13},{6,14},{7,15},{8,0},{9,1},... | collective-permute-start | bytes 1572872 | tf_op jit(solution)/shard_map/ppermute | solution.py:675
  224.9 59.4 %collective-permute-start.24 = (bf16[128,2048]{1,0:T(8,128)(2,1)}, bf16[128,2048]{1,0:T(8,128)(2,1)S(1)}, u32[]{:S(2)}, u32[]{:S(2)}) collective-permute-start(bf16[128,2048]{1,0:T(8,128)(2,1)} %get-tuple-element.127), channel_id=1, source_target_pairs={{0,8},{1,9},{2,10},{3,11},{4,12},{5,13},{6,14},{7,15},{8,0},{9,1},... | collective-permute-start | bytes 1572872 | tf_op jit(solution)/shard_map/ppermute | solution.py:675
  264.1 26.8 %collective-permute-start.26 = (bf16[128,2048]{1,0:T(8,128)(2,1)S(1)}, bf16[128,2048]{1,0:T(8,128)(2,1)S(1)}, u32[]{:S(2)}, u32[]{:S(2)}) collective-permute-start(bf16[128,2048]{1,0:T(8,128)(2,1)S(1)} %add_convert_fusion.1), channel_id=1, source_target_pairs={{0,16},{1,17},{2,18},{3,19},{4,20},{5,21},{6,22},{7,23},{8,24},{9,... | collective-permute-start | bytes 1572872 | tf_op jit(solution)/shard_map/ppermute | solution.py:675
  (22 other events, 242.1 us)

commit v5 on v4

--- a/solution.py
+++ b/solution.py
@@ -73,18 +73,25 @@
     )(*operands)
 
 
-def place_kernel(clusters, ids_ref, pos_ref, bias_ref):
+def place_kernel(clusters, low, high, me_ref, *refs):
+    parts, (pos_ref, bias_ref, stage, *ids) = refs[:low], refs[low:]
     blocks, lanes = pos_ref.shape
     bf, f32 = jnp.bfloat16, jnp.float32
     cluster_ids = lax.broadcasted_iota(jnp.int32, (clusters, lanes), 0).astype(f32)
     slot_ids = lax.broadcasted_iota(jnp.int32, (CAP, lanes), 0).astype(f32)
+    count_rows = stage.shape[0]
+    for k in range(low):
+        for s in range(high):
+            b = (me_ref[1] ^ s) * low + (me_ref[0] ^ k)
+            stage[...] = parts[k][s, parts[k].shape[1] - count_rows :, :].astype(f32)
+            for kind, ref in enumerate(ids):
+                ref[pl.ds(b, 1), :] = stage[pl.ds(kind * low + me_ref[0], 1), :]
 
     def tables(b):
-        held = ids_ref[b].astype(f32)
-        cluster = held[0:1] * lanes + held[1:2]
+        cluster = ids[0][pl.ds(b, 1), :] * lanes + ids[1][pl.ds(b, 1), :]
         return (
             jnp.where(cluster_ids == cluster, 1.0, 0.0),
-            jnp.where(slot_ids == held[2:3], 1.0, 0.0),
+            jnp.where(slot_ids == ids[2][pl.ds(b, 1), :], 1.0, 0.0),
         )
 
     def count(step, occupied):
@@ -156,11 +163,17 @@
     lax.fori_loop(0, rows // TILE // UNROLL, labels, 0)
 
 
-def place(ids, clusters):
-    blocks, _, lanes = ids.shape
+def id_rows(low):
+    return -(-3 * low // 16) * 16
+
+
+def place(gathered, clusters):
+    low, (high, _, lanes) = len(gathered), gathered[0].shape
+    f32, blocks = jnp.float32, len(gathered) * high
     return run(
-        functools.partial(place_kernel, clusters), (ids,),
-        (((blocks, lanes), jnp.int32), ((blocks * lanes, WIN), jnp.bfloat16)), (), 8, "place",
+        functools.partial(place_kernel, clusters, low, high), (place_in_plane(low), *gathered),
+        (((blocks, lanes), jnp.int32), ((blocks * lanes, WIN), jnp.bfloat16)),
+        (((id_rows(low), lanes), f32),) + (((blocks, lanes), f32),) * 3, 8, "place",
     )
 
 
@@ -371,29 +384,37 @@
     )
 
 
-def project_back_kernel(low, *refs):
+def project_back_kernel(low, high, columns, me_ref, *refs):
     bf, f32 = jnp.bfloat16, jnp.float32
-    weights, blocks, outs, rows_ref = refs[:low], refs[low : -1 - low], refs[-1 - low : -1], refs[-1]
+    gathered, blocks = refs[:low], refs[low : low + high]
+    outs, weight_ref, rows_ref = refs[low + high : -2], refs[-2], refs[-1]
+    size = gathered[0].shape[2]
     rows = blocks[0].shape[0]
     for r, block in enumerate(blocks):
         rows_ref[pl.ds(r * rows, rows), :] = block[...]
     for k in range(0, low, 2):
-        weight = jnp.concatenate([weights[k][...], weights[k + 1][...]], axis=1)
+        for source in range(low):
+            for s in range(high):
+                first = ((me_ref[1] ^ s) * low + (me_ref[0] ^ source)) * columns
+                at = pl.ds(pl.multiple_of(first, columns), columns)
+                for head in (k, k + 1):
+                    start = pl.multiple_of((me_ref[0] ^ head) * columns, columns)
+                    weight_ref[head, at, :] = gathered[source][s, pl.ds(start, columns), :]
+        weight = jnp.concatenate([weight_ref[k], weight_ref[k + 1]], axis=1)
         both = jnp.dot(rows_ref[...], weight, preferred_element_type=f32).astype(bf)
-        size = both.shape[1] // 2
         outs[k][...] = both[:, :size]
         outs[k + 1][...] = both[:, size:]
 
 
-def project_kernel(low, chunk, *refs):
+def project_kernel(low, chunk, weight_ref, *refs):
     bf, f32 = jnp.bfloat16, jnp.float32
-    weights, parts, outs = refs[:low], refs[low : 2 * low], refs[2 * low :]
+    parts, outs = refs[:low], refs[low:]
     rows = jnp.concatenate([ref[...] for ref in parts], axis=1)
     count, columns = outs[0].shape
 
     def one(c, carry):
         at = pl.ds(pl.multiple_of(c * chunk, chunk), chunk)
-        weight = jnp.concatenate([ref[at, :] for ref in weights], axis=1)
+        weight = jnp.concatenate([weight_ref[k, at, :] for k in range(low)], axis=1)
         mixed = lax.dot_general(rows, weight, NT, preferred_element_type=f32).astype(bf)
         for r, out in enumerate(outs):
             out[:, at] = mixed[r * count : (r + 1) * count]
@@ -402,25 +423,46 @@
     lax.fori_loop(0, columns // chunk, one, 0)
 
 
+def pack_weight_kernel(low, me_ref, weight_ref, ids_ref, *outs):
+    size, columns = outs[0].shape[1], weight_ref.shape[0]
+    for s, out in enumerate(outs):
+        plane = me_ref[1] ^ s
+        for h in range(low):
+            at = pl.ds(pl.multiple_of((plane * low + h) * size, size), size)
+            out[pl.ds(h * columns, columns), :] = weight_ref[:, at]
+        out[low * columns :, :] = ids_ref[plane]
+
+
+def pack_weight(weight, ids, low):
+    high, rows, size = ids.shape
+    return run(
+        functools.partial(pack_weight_kernel, low), (place_in_plane(low), weight, ids),
+        (((low * weight.shape[0] + rows, size), weight.dtype),) * high, (), 2, "pack_weight",
+    )
+
+
 def place_in_plane(low):
     index = lax.axis_index("seq")
     return jnp.stack([index % low, index // low]).astype(jnp.int32)
 
 
-def project_back(weights, blocks):
-    low, bf = len(weights), jnp.bfloat16
-    size = weights[0].shape[1]
-    rows, depth = blocks[0].shape[0] * len(blocks), blocks[0].shape[1]
+def project_back(gathered, blocks):
+    low, high, bf = len(gathered), len(blocks), jnp.bfloat16
+    size = gathered[0].shape[-1]
+    rows, depth = blocks[0].shape[0] * high, blocks[0].shape[1]
+    *heads, weight = run(
+        functools.partial(project_back_kernel, low, high, depth // (low * high)),
+        (place_in_plane(low), *gathered, *blocks),
+        (((rows, size), bf),) * low + (((low, depth, size), bf),),
+        (((rows, depth), bf),), 8, "project_back",
+    )
+    return heads, weight
+
+
+def project(weight, parts, high):
+    low, columns = weight.shape[:2]
     return run(
-        functools.partial(project_back_kernel, low), (*weights, *blocks),
-        (((rows, size), bf),) * low, (((rows, depth), bf),), 8, "project_back",
-    )
-
-
-def project(weights, parts, high):
-    low, columns = len(weights), weights[0].shape[0]
-    return run(
-        functools.partial(project_kernel, low, math.gcd(columns, 512)), (*weights, *parts),
+        functools.partial(project_kernel, low, math.gcd(columns, 512)), (weight, *parts),
         (((parts[0].shape[0] // high, columns), jnp.bfloat16),) * high, (), 6, "project",
     )
 
@@ -663,7 +705,6 @@
     heads_dev = cluster_id.shape[0]
     head_size = width // heads_dev
     owners = lax.axis_size("seq")
-    columns_dev = out_weight.shape[1]
     high, low = split(owners)
     bf, f32 = jnp.bfloat16, jnp.float32
     together = lax.optimization_barrier
@@ -677,47 +718,53 @@
     def swap(blocks):
         return [blocks[0]] + [send(blocks[k], k) for k in range(1, low)]
 
-    def gather_plane(block, after):
-        near = [block] + [send(block, k) for k in range(2, low, 2)]
-        near, after = together((near, after))
-        return [x for one in near for x in (one, send(one, 1))], after
-
-    def gather_stack(block, after):
-        blocks, bit = {0: block}, high // 2
-        while bit:
-            blocks |= {r | bit: send(one, bit * low) for r, one in blocks.items()}
-            bit //= 2
-            if bit == high // 4:
-                blocks, after = together((blocks, after))
-        return [blocks[r] for r in range(high)], after
-
-    def sum_stack(blocks):
-        blocks, bit = dict(enumerate(blocks)), 1
-        while bit < high:
-            blocks = {
-                r: (one.astype(f32) + send(blocks[r | bit], bit * low).astype(f32)).astype(bf)
-                for r, one in blocks.items()
-                if not r & bit
-            }
-            bit *= 2
-        return blocks[0]
-
-    weight_rows = out_weight.T.reshape(columns_dev, heads_dev, head_size).transpose(1, 0, 2)
-    ids = jnp.stack([cluster_id // rows_dev, cluster_id % rows_dev, slot_index], axis=1)
-    ids = jnp.pad(ids, ((0, 0), (0, 13), (0, 0))).astype(bf)
-    first = exchange(jnp.concatenate([weight_rows, ids], axis=1))
-    grad_out_stack, first = gather_stack(grad_out, first)
+    ranks = [
+        [r for r in range(1, high) if bin(r).count("1") == count]
+        for count in range(1, high.bit_length())
+    ]
+
+    def over(block, r):
+        return send(block, (r & -r) * low)
+
+    def gather_stack(block):
+        blocks = {0: block}
+        for rank in ranks:
+            blocks |= {r: over(blocks[r & (r - 1)], r) for r in rank}
+        return [blocks[r] for r in range(high)]
+
+    def sum_stack(blocks, after):
+        blocks = {r: block.astype(f32) for r, block in enumerate(blocks)}
+        for rank in ranks[::-1]:
+            there = {r: over(blocks.pop(r).astype(bf), r) for r in rank}
+            if rank is ranks[0]:
+                there, after = together((there, after))
+            else:
+                there, blocks = together((there, blocks))
+            for r, block in there.items():
+                blocks[r & (r - 1)] += block.astype(f32)
+        return blocks[0].astype(bf), after
+
+    ids = jnp.stack([cluster_id // rows_dev, cluster_id % rows_dev, slot_index])
+    ids = ids.reshape(3, high, low, rows_dev).transpose(1, 0, 2, 3).reshape(high, 3 * low, rows_dev)
+    ids = jnp.pad(ids, ((0, 0), (0, id_rows(low) - 3 * low), (0, 0))).astype(bf)
+    weight = pack_weight(out_weight.T, ids, low)
+    weight = [weight[0]] + [send(weight[s], s * low) for s in range(1, high)]
+    weight, grad_out = together((weight, grad_out))
+    weight = jnp.stack(weight)
+    weight = [weight] + [send(weight, k) for k in range(2, low, 2)]
+    blocks = gather_stack(grad_out)
     packed = pack((query_rows, key_rows), heads_dev)
     packed_value = pack((value_rows,), heads_dev)
-    packed, packed_value, first = together((packed, packed_value, first))
+    packed, packed_value, weight, blocks = together((packed, packed_value, weight, blocks))
     arrived = exchange(packed)
-    placed = place(first[:, columns_dev:], CLU_DEV * owners)
-    head_weight = first[:, :columns_dev].reshape(owners * columns_dev, head_size)
-    weights, (pos, bias) = gather_plane(head_weight, placed)
-    grad_heads = project_back(weights, grad_out_stack)
-    packed_value, arrived, grad_heads = together((packed_value, arrived, grad_heads))
+    weight = [x for one in weight for x in (one, send(one, 1))]
+    grad_heads, rows_of_heads = project_back(weight, blocks)
+    grad_heads = swap(grad_heads)
+    pos, bias = place(weight, CLU_DEV * owners)
+    packed_value, arrived, grad_heads, pos, bias = together(
+        (packed_value, arrived, grad_heads, pos, bias)
+    )
     value = exchange(packed_value)
-    grad_heads = swap(grad_heads)
     scores, attend, grad_of_value, rest = head_kernels(pos, head_size, low)
     query, key, probs = scores(arrived, bias)
     grad_value, grad_sorted = grad_of_value(grad_heads, probs)
@@ -729,8 +776,9 @@
     grads, attended = together((grads, attended))
     grads, back_value = together((grads, back_value))
     back = exchange(grads)
-    mixed = sum_stack(project(weights, attended, high))
-    return (mixed, *unpack(back, 2), *unpack(back_value, 1))
+    outs = (*unpack(back, 2), *unpack(back_value, 1))
+    mixed, outs = sum_stack(project(rows_of_heads, attended, high), outs)
+    return (mixed, *outs)
 
 
 def split(owners):

time: 297 us -> 273 us (0.919)
  waiting for transfers between devices: 144 us -> 111 us
  Pallas kernels: 82.2 us -> 89.5 us
  other arithmetic: 5.26 us -> 9.04 us
    ppermute x27 -> x30, waiting for transfers between devices: 144 us -> 98.4 us  [send(): return lax.ppermute(block, 'seq', [(i, i ^ bits) for i in range(owners)])]
    all_to_all x5 -> x4, waiting for transfers between devices: 0.01 us -> 12.5 us  [exchange(): return lax.all_to_all(rows, 'seq', split_axis=0, concat_axis=0, tiled=True)]
    all_to_all x5 -> x4, starting transfers between devices: 27.9 us -> 18.4 us  [exchange(): return lax.all_to_all(rows, 'seq', split_axis=0, concat_axis=0, tiled=True)]
    ppermute x27 -> x30, starting transfers between devices: 28.9 us -> 36.6 us  [send(): return lax.ppermute(block, 'seq', [(i, i ^ bits) for i in range(owners)])]
    pallas_call x7 -> x8, Pallas kernels: 74.8 us -> 82 us  [run(): pl.pallas_call(body, out_shape=tuple((jax.ShapeDtypeStruct(shape, kind) f...]
    convert_element_type x2 -> x4, other arithmetic: 2.2 us -> 6.64 us  [the longest x2 3.38 us: sum_stack(): blocks = {r: block.astype(f32) for r, block in enumerate(blocks)}]
    slice x2 -> x0, local copies, waits for them, and re-layouts: 3.44 us -> none  [the longest x1 1.87 us: by_heads(): first[:, :columns_dev].reshape(owners * columns_dev, head_size)]
    unnamed x44 -> x58, local copies, waits for them, and re-layouts: 2.62 us -> 5.64 us
  transfers between devices with their start and end apart: 32 -> 34, of which waited for: 10 -> 14; matrix products, arithmetic and copies ran while one was open for 2% -> 2% of each run, Pallas kernels for 27% -> 32%
where the time goes in v5:
time: 273 us; the launch traced here: 272 us
  waiting for transfers between devices  111 us (41%)
  Pallas kernels  89.5 us (33%)
  starting transfers between devices  55 us (20%)
  other arithmetic  9.04 us (3%)
  local copies, waits for them, and re-layouts  6.24 us (2%)
    ppermute x30, waiting for transfers between devices, send(): return lax.ppermute(block, 'seq', [(i, i ^ bits) for i in range(owners)])  98.4 us
    pallas_call x8, Pallas kernels, run(): pl.pallas_call(body, out_shape=tuple((jax.ShapeDtypeStruct(shape, kind) f...  82 us
    ppermute x30, starting transfers between devices, send(): return lax.ppermute(block, 'seq', [(i, i ^ bits) for i in range(owners)])  36.6 us
    all_to_all x4, starting transfers between devices, exchange(): return lax.all_to_all(rows, 'seq', split_axis=0, concat_axis=0, tiled=True)  18.4 us
    all_to_all x4, waiting for transfers between devices, exchange(): return lax.all_to_all(rows, 'seq', split_axis=0, concat_axis=0, tiled=True)  12.5 us
    unnamed x58, local copies, waits for them, and re-layouts  5.64 us
  transfers between devices with their start and end apart: 34, of which 14 were waited for; matrix products, arithmetic and copies ran while one was open for 2% of the time, Pallas kernels for 32%

profile of v5, /device:TPU:0, one launch (start us, length us, event | category | flops | bytes accessed | tf_op | source)
XLA Modules:
  0.0 271.8 jit_solution(3973091646415867214)
XLA Ops:
  2.7 2.7 pack_weight.1
  5.4 3.1 %collective-permute-start = (bf16[544,128]{1,0:T(8,128)(2,1)}, bf16[544,128]{1,0:T(8,128)(2,1)S(1)}, u32[]{:S(2)}, u32[]{:S(2)}) collective-permute-start(bf16[544,128]{1,0:T(8,128)(2,1)} %get-tuple-element.90), channel_id=1, source_target_pairs={{0,8},{1,9},{2,10},{3,11},{4,12},{5,13},{6,14},{7,15},{8,0},{9,1},... | collective-permute-start | bytes 417800 | tf_op jit(solution)/shard_map/ppermute | solution.py:716
  8.5 2.6 collective-permute-start.1
  11.1 3.1 %collective-permute-done = bf16[544,128]{1,0:T(8,128)(2,1)S(1)} collective-permute-done((bf16[544,128]{1,0:T(8,128)(2,1)}, bf16[544,128]{1,0:T(8,128)(2,1)S(1)}, u32[]{:S(2)}, u32[]{:S(2)}) %collective-permute-start) | collective-permute-done | bytes 139296 | tf_op jit(solution)/shard_map/ppermute | solution.py:716
  14.1 8.0 %collective-permute-done.1 = bf16[544,128]{1,0:T(8,128)(2,1)S(1)} collective-permute-done((bf16[544,128]{1,0:T(8,128)(2,1)}, bf16[544,128]{1,0:T(8,128)(2,1)S(1)}, u32[]{:S(2)}, u32[]{:S(2)}) %collective-permute-start.1) | collective-permute-done | bytes 139296 | tf_op jit(solution)/shard_map/ppermute | solution.py:716
  22.2 3.1 %collective-permute-start.7 = (bf16[128,2048]{1,0:T(8,128)(2,1)}, bf16[128,2048]{1,0:T(8,128)(2,1)S(1)}, u32[]{:S(2)}, u32[]{:S(2)}) collective-permute-start(bf16[128,2048]{1,0:T(8,128)(2,1)} %refs_9_), channel_id=1, source_target_pairs={{0,16},{1,17},{2,18},{3,19},{4,20},{5,21},{6,22},{7,23},{8,24},{9,... | collective-permute-start | bytes 1572872 | tf_op jit(solution)/shard_map/ppermute | solution.py:716
  29.8 18.0 %collective-permute-done.7.refs_11_ = bf16[128,2048]{1,0:T(8,128)(2,1)S(1)} collective-permute-done((bf16[128,2048]{1,0:T(8,128)(2,1)}, bf16[128,2048]{1,0:T(8,128)(2,1)S(1)}, u32[]{:S(2)}, u32[]{:S(2)}) %collective-permute-start.7) | collective-permute-done | bytes 524320 | tf_op jit(solution)/shard_map/ppermute | solution.py:716
  49.5 2.1 pack.2
  51.7 2.6 collective-permute-done.6.refs_10_
  56.3 7.0 %collective-permute-done.8.refs_12_ = bf16[128,2048]{1,0:T(8,128)(2,1)} collective-permute-done((bf16[128,2048]{1,0:T(8,128)(2,1)S(1)}, bf16[128,2048]{1,0:T(8,128)(2,1)}, u32[]{:S(2)}, u32[]{:S(2)}) %collective-permute-start.8) | collective-permute-done | bytes 524320 | tf_op jit(solution)/shard_map/ppermute | solution.py:716
  63.2 2.8 %all-to-all-start = ((bf16[32,256,128]{2,1,0:T(8,128)(2,1)}), bf16[32,256,128]{2,1,0:T(8,128)(2,1)S(1)}, u32[]{:S(2)}, u32[]{:S(2)}) async-start(bf16[32,256,128]{2,1,0:T(8,128)(2,1)} %pack.2), calls=%async_computation | async-start | bytes 4194304 | tf_op jit(solution)/shard_map/all_to_all | solution.py:713
  71.6 8.4 %project_back.1 = (bf16[512,128]{1,0:T(8,128)(2,1)}, bf16[512,128]{1,0:T(8,128)(2,1)}, bf16[512,128]{1,0:T(8,128)(2,1)}, bf16[512,128]{1,0:T(8,128)(2,1)}, bf16[...) custom-call(s32[2]{0:T(128)} %pad_add_fusion.refs_0_, ...), custom_call_target="tpu_custom_call" | custom-call | bytes 28000000 | tf_op jit(solution)/shard_map/project_back/pallas_call | solution.py:60
  83.7 2.6 collective-permute-start.18
  88.0 4.0 %collective-permute-start.19 = (bf16[512,128]{1,0:T(8,128)(2,1)}, bf16[512,128]{1,0:T(8,128)(2,1)S(1)}, u32[]{:S(2)}, u32[]{:S(2)}) collective-permute-start(bf16[512,128]{1,0:T(8,128)(2,1)} %get-tuple-element.116), channel_id=1, source_target_pairs={{0,7},{1,6},{2,5},{3,4},{4,3},{5,2},{6,1},{7,0},{8,15},{9,14},{10,... | collective-permute-start | bytes 393224 | tf_op jit(solution)/shard_map/ppermute | solution.py:716
  92.0 11.0 %place.1 = (s32[32,128]{1,0:T(8,128)}, bf16[4096,128]{1,0:T(8,128)(2,1)}) custom-call(s32[2]{0:T(128)} %pad_add_fusion.refs_0_, bf16[4,544,128]{2,1,0:T(8,128)(2,1)} %copy-done.6, bf16[4,544,128]{2,1,0:T(8,128)(2,1)} %copy-done.10, bf16[4,544,128]{2,1,0:T(8,128)(2,1)} %copy-done.7, bf16[4,544,128]{2,1,0:T(8,128)(2,1)} %copy-done.11, ...), custom_call_target="tpu_custom_call" | custom-call | bytes 28000000 | tf_op jit(solution)/shard_map/place/pallas_call | solution.py:60
  103.1 11.9 %all-to-all-done.refs_1_ = bf16[32,256,128]{2,1,0:T(8,128)(2,1)S(1)} async-done(((bf16[32,256,128]{2,1,0:T(8,128)(2,1)}), bf16[32,256,128]{2,1,0:T(8,128)(2,1)S(1)}, u32[]{:S(2)}, u32[]{:S(2)}) %all-to-all-start) | async-done | bytes 2097184 | tf_op jit(solution)/shard_map/all_to_all | solution.py:713
  115.0 4.0 %all-to-all-start.1 = ((bf16[32,128,128]{2,1,0:T(8,128)(2,1)}), bf16[32,128,128]{2,1,0:T(8,128)(2,1)}, u32[]{:S(2)}, u32[]{:S(2)}) async-start(bf16[32,128,128]{2,1,0:T(8,128)(2,1)} %pack.3), calls=%async_computation.1 | async-start | bytes 2097152 | tf_op jit(solution)/shard_map/all_to_all | solution.py:713
  119.1 12.3 %scores.1 = (bf16[4160,128]{1,0:T(8,128)(2,1)}, bf16[4160,128]{1,0:T(8,128)(2,1)}, bf16[4096,128]{1,0:T(8,128)(2,1)}) custom-call(s32[32,128]{1,0:T(8,128)} %get-tuple-element.119.refs_0_.refs_1_, bf16[32,256,128]{2,1,0:T(8,128)(2,1)} %copy-done.5, bf16[4096,128]{1,0:T(8,128)(2,1)} %get-tuple-element.129.refs_2_), custom_call_target="tpu_custom_call" | custom-call | bytes 42000000 | tf_op jit(solution)/shard_map/scores/pallas_call | solution.py:60
  131.5 13.2 %grad_value.1 = (bf16[32,128,128]{2,1,0:T(8,128)(2,1)}, bf16[4096,128]{1,0:T(8,128)(2,1)}) custom-call(s32[2]{0:T(128)} %pad_add_fusion.refs_0_, s32[32,128]{1,0:T(8,128)} %get-tuple-element.119.refs_0_.refs_1_, bf16[512,128]{1,0:T(8,128)(2,1)} %get-tuple-element.120.refs_2_, bf16[512,128]{1,0:T(8,128)(2,1)} %copy-done.15, bf16[512,128]{1,0:T(8,128)(2,1)} %copy-done.16, ...), custom_call_target="tpu_custom_call" | custom-call | bytes 42000000 | tf_op jit(solution)/shard_map/grad_value/pallas_call | solution.py:60
  145.3 5.2 %all-to-all-start.2 = ((bf16[32,128,128]{2,1,0:T(8,128)(2,1)}), bf16[32,128,128]{2,1,0:T(8,128)(2,1)S(1)}, u32[]{:S(2)}, u32[]{:S(2)}) async-start(bf16[32,128,128]{2,1,0:T(8,128)(2,1)} %get-tuple-element.164), calls=%async_computation.2 | async-start | bytes 2097152 | tf_op jit(solution)/shard_map/all_to_all | solution.py:713
  150.5 12.9 %attend.1 = (bf16[512,128]{1,0:T(8,128)(2,1)}, bf16[512,128]{1,0:T(8,128)(2,1)}, bf16[512,128]{1,0:T(8,128)(2,1)}, bf16[512,128]{1,0:T(8,128)(2,1)}, bf16[512,12...) custom-call(s32[2]{0:T(128)} %pad_add_fusion.refs_0_, ...), custom_call_target="tpu_custom_call" | custom-call | bytes 42000000 | tf_op jit(solution)/shard_map/attend/pallas_call | solution.py:60
  167.2 2.6 collective-permute-start.25
  171.4 14.8 %rest.1 = bf16[32,256,128]{2,1,0:T(8,128)(2,1)} custom-call(s32[32,128]{1,0:T(8,128)} %get-tuple-element.119.refs_0_.refs_1_, bf16[4096,128]{1,0:T(8,128)(2,1)} %get-tuple-element.131.refs_1_, bf16[4096,128]{1,0:T(8,128)(2,1)} %get-tuple-element.135.refs_2_, bf16[4160,128]{1,0:T(8,128)(2,1)} %get-tuple-element.136.refs_3_, ...), custom_call_target="tpu_custom_call" | custom-call | bytes 56000000 | tf_op jit(solution)/shard_map/rest/pallas_call | solution.py:60
  187.5 6.4 %all-to-all-start.3 = ((bf16[32,256,128]{2,1,0:T(8,128)(2,1)}), bf16[32,256,128]{2,1,0:T(8,128)(2,1)S(1)}, u32[]{:S(2)}, u32[]{:S(2)}) async-start(bf16[32,256,128]{2,1,0:T(8,128)(2,1)} %rest.1), calls=%async_computation.3 | async-start | bytes 4194304 | tf_op jit(solution)/shard_map/all_to_all | solution.py:713
  193.9 6.7 %project.1 = (bf16[128,2048]{1,0:T(8,128)(2,1)}, bf16[128,2048]{1,0:T(8,128)(2,1)}, bf16[128,2048]{1,0:T(8,128)(2,1)}, bf16[128,2048]{1,0:T(8,128)(2,1)}) custom-call(bf16[8,2048,128]{2,1,0:T(8,128)(2,1)} %get-tuple-element.106.refs_0_, bf16[512,128]{1,0:T(8,128)(2,1)} %get-tuple-element.147.refs_1_, bf16[512,128]{1,0:T(8,128)(2,1)} %copy-done.17, ...), custom_call_target="tpu_custom_call" | custom-call | bytes 21000000 | tf_op jit(solution)/shard_map/project/pallas_call | solution.py:60
  202.5 2.1 convert_element_type.30
  205.9 34.4 %collective-permute-done.27 = bf16[128,2048]{1,0:T(8,128)(2,1)S(1)} collective-permute-done((bf16[128,2048]{1,0:T(8,128)(2,1)}, bf16[128,2048]{1,0:T(8,128)(2,1)S(1)}, u32[]{:S(2)}, u32[]{:S(2)}) %collective-permute-start.27) | collective-permute-done | bytes 524320 | tf_op jit(solution)/shard_map/ppermute | solution.py:716
  240.3 2.4 collective-permute-start.28
  246.9 2.0 unpack.2
  248.9 16.6 %collective-permute-done.28 = bf16[128,2048]{1,0:T(8,128)(2,1)S(1)} collective-permute-done((bf16[128,2048]{1,0:T(8,128)(2,1)}, bf16[128,2048]{1,0:T(8,128)(2,1)S(1)}, u32[]{:S(2)}, u32[]{:S(2)}) %collective-permute-start.28) | collective-permute-done | bytes 524320 | tf_op jit(solution)/shard_map/ppermute | solution.py:716
  265.5 3.9 %collective-permute-done.29 = bf16[128,2048]{1,0:T(8,128)(2,1)} collective-permute-done((bf16[128,2048]{1,0:T(8,128)(2,1)}, bf16[128,2048]{1,0:T(8,128)(2,1)}, u32[]{:S(2)}, u32[]{:S(2)}) %collective-permute-start.29) | collective-permute-done | bytes 524320 | tf_op jit(solution)/shard_map/ppermute | solution.py:716
  269.4 2.4 add_convert_fusion
  (115 shorter events, 35.8 us)
Async XLA Ops:
  5.4 8.7 %collective-permute-start = (bf16[544,128]{1,0:T(8,128)(2,1)}, bf16[544,128]{1,0:T(8,128)(2,1)S(1)}, u32[]{:S(2)}, u32[]{:S(2)}) collective-permute-start(bf16[544,128]{1,0:T(8,128)(2,1)} %get-tuple-element.90), channel_id=1, source_target_pairs={{0,8},{1,9},{2,10},{3,11},{4,12},{5,13},{6,14},{7,15},{8,0},{9,1},... | collective-permute-start | bytes 417800 | tf_op jit(solution)/shard_map/ppermute | solution.py:716
  8.5 13.7 %collective-permute-start.1 = (bf16[544,128]{1,0:T(8,128)(2,1)}, bf16[544,128]{1,0:T(8,128)(2,1)S(1)}, u32[]{:S(2)}, u32[]{:S(2)}) collective-permute-start(bf16[544,128]{1,0:T(8,128)(2,1)} %get-tuple-element.91), channel_id=1, source_target_pairs={{0,16},{1,17},{2,18},{3,19},{4,20},{5,21},{6,22},{7,23},{8,24},{9,... | collective-permute-start | bytes 417800 | tf_op jit(solution)/shard_map/ppermute | solution.py:716
  11.1 11.1 %collective-permute-start.2 = (bf16[544,128]{1,0:T(8,128)(2,1)}, bf16[544,128]{1,0:T(8,128)(2,1)S(1)}, u32[]{:S(2)}, u32[]{:S(2)}) collective-permute-start(bf16[544,128]{1,0:T(8,128)(2,1)} %get-tuple-element.92), channel_id=1, source_target_pairs={{0,24},{1,25},{2,26},{3,27},{4,28},{5,29},{6,30},{7,31},{8,16},{9,... | collective-permute-start | bytes 417800 | tf_op jit(solution)/shard_map/ppermute | solution.py:716
  22.2 25.7 %collective-permute-start.7 = (bf16[128,2048]{1,0:T(8,128)(2,1)}, bf16[128,2048]{1,0:T(8,128)(2,1)S(1)}, u32[]{:S(2)}, u32[]{:S(2)}) collective-permute-start(bf16[128,2048]{1,0:T(8,128)(2,1)} %refs_9_), channel_id=1, source_target_pairs={{0,16},{1,17},{2,18},{3,19},{4,20},{5,21},{6,22},{7,23},{8,24},{9,... | collective-permute-start | bytes 1572872 | tf_op jit(solution)/shard_map/ppermute | solution.py:716
  26.3 28.0 %collective-permute-start.3 = (bf16[4,544,128]{2,1,0:T(8,128)(2,1)S(1)}, bf16[4,544,128]{2,1,0:T(8,128)(2,1)S(1)}, u32[]{:S(2)}, u32[]{:S(2)}) collective-permute-start(bf16[4,544,128]{2,1,0:T(8,128)(2,1)S(1)} %pad_maximum_fusion.refs_1_), channel_id=1, source_target_pairs={{0,2},{1,3},{2,0},{3,1},{4,6},{5,7},{6,4},{7,5},{8,10},{9,11},{10,... | collective-permute-start | bytes 1671176 | tf_op jit(solution)/shard_map/ppermute | solution.py:716
  27.8 26.5 %collective-permute-start.4 = (bf16[4,544,128]{2,1,0:T(8,128)(2,1)S(1)}, bf16[4,544,128]{2,1,0:T(8,128)(2,1)S(1)}, u32[]{:S(2)}, u32[]{:S(2)}) collective-permute-start(bf16[4,544,128]{2,1,0:T(8,128)(2,1)S(1)} %pad_maximum_fusion.refs_1_), channel_id=1, source_target_pairs={{0,4},{1,5},{2,6},{3,7},{4,0},{5,1},{6,2},{7,3},{8,12},{9,13},{10,... | collective-permute-start | bytes 1671176 | tf_op jit(solution)/shard_map/ppermute | solution.py:716
  29.4 25.0 %collective-permute-start.5 = (bf16[4,544,128]{2,1,0:T(8,128)(2,1)S(1)}, bf16[4,544,128]{2,1,0:T(8,128)(2,1)S(1)}, u32[]{:S(2)}, u32[]{:S(2)}) collective-permute-start(bf16[4,544,128]{2,1,0:T(8,128)(2,1)S(1)} %pad_maximum_fusion.refs_1_), channel_id=1, source_target_pairs={{0,6},{1,7},{2,4},{3,5},{4,2},{5,3},{6,0},{7,1},{8,14},{9,15},{10,... | collective-permute-start | bytes 1671176 | tf_op jit(solution)/shard_map/ppermute | solution.py:716
  29.8 24.5 %collective-permute-start.6 = (bf16[128,2048]{1,0:T(8,128)(2,1)}, bf16[128,2048]{1,0:T(8,128)(2,1)S(1)}, u32[]{:S(2)}, u32[]{:S(2)}) collective-permute-start(bf16[128,2048]{1,0:T(8,128)(2,1)} %refs_9_), channel_id=1, source_target_pairs={{0,8},{1,9},{2,10},{3,11},{4,12},{5,13},{6,14},{7,15},{8,0},{9,1},... | collective-permute-start | bytes 1572872 | tf_op jit(solution)/shard_map/ppermute | solution.py:716
  47.8 15.4 %collective-permute-start.8 = (bf16[128,2048]{1,0:T(8,128)(2,1)S(1)}, bf16[128,2048]{1,0:T(8,128)(2,1)}, u32[]{:S(2)}, u32[]{:S(2)}) collective-permute-start(bf16[128,2048]{1,0:T(8,128)(2,1)S(1)} %collective-permute-done.7.refs_11_), channel_id=1, source_target_pairs={{0,8},{1,9},{2,10},{3,11},{4,12},{5,13},{6,14},{7,15},{8,0},{9,1},... | collective-permute-start | bytes 1572872 | tf_op jit(solution)/shard_map/ppermute | solution.py:716
  63.2 51.8 %all-to-all-start = ((bf16[32,256,128]{2,1,0:T(8,128)(2,1)}), bf16[32,256,128]{2,1,0:T(8,128)(2,1)S(1)}, u32[]{:S(2)}, u32[]{:S(2)}) async-start(bf16[32,256,128]{2,1,0:T(8,128)(2,1)} %pack.2), calls=%async_computation | async-start | bytes 4194304 | tf_op jit(solution)/shard_map/all_to_all | solution.py:713
  66.6 4.1 %collective-permute-start.11 = (bf16[4,544,128]{2,1,0:T(8,128)(2,1)}, bf16[4,544,128]{2,1,0:T(8,128)(2,1)S(1)}, u32[]{:S(2)}, u32[]{:S(2)}) collective-permute-start(bf16[4,544,128]{2,1,0:T(8,128)(2,1)} %copy-done.8), channel_id=1, source_target_pairs={{0,1},{1,0},{2,3},{3,2},{4,5},{5,4},{6,7},{7,6},{8,9},{9,8},{10,11... | collective-permute-start | bytes 1671176 | tf_op jit(solution)/shard_map/ppermute | solution.py:716
  66.9 4.7 %collective-permute-start.12 = (bf16[4,544,128]{2,1,0:T(8,128)(2,1)}, bf16[4,544,128]{2,1,0:T(8,128)(2,1)}, u32[]{:S(2)}, u32[]{:S(2)}) collective-permute-start(bf16[4,544,128]{2,1,0:T(8,128)(2,1)} %copy-done.9), channel_id=1, source_target_pairs={{0,1},{1,0},{2,3},{3,2},{4,5},{5,4},{6,7},{7,6},{8,9},{9,8},{10,11... | collective-permute-start | bytes 1671176 | tf_op jit(solution)/shard_map/ppermute | solution.py:716
  79.9 3.8 %collective-permute-start.13 = (bf16[512,128]{1,0:T(8,128)(2,1)}, bf16[512,128]{1,0:T(8,128)(2,1)S(1)}, u32[]{:S(2)}, u32[]{:S(2)}) collective-permute-start(bf16[512,128]{1,0:T(8,128)(2,1)} %get-tuple-element.110), channel_id=1, source_target_pairs={{0,1},{1,0},{2,3},{3,2},{4,5},{5,4},{6,7},{7,6},{8,9},{9,8},{10,11... | collective-permute-start | bytes 393224 | tf_op jit(solution)/shard_map/ppermute | solution.py:716
  80.2 7.8 %collective-permute-start.14 = (bf16[512,128]{1,0:T(8,128)(2,1)}, bf16[512,128]{1,0:T(8,128)(2,1)S(1)}, u32[]{:S(2)}, u32[]{:S(2)}) collective-permute-start(bf16[512,128]{1,0:T(8,128)(2,1)} %get-tuple-element.111), channel_id=1, source_target_pairs={{0,2},{1,3},{2,0},{3,1},{4,6},{5,7},{6,4},{7,5},{8,10},{9,11},{10,... | collective-permute-start | bytes 393224 | tf_op jit(solution)/shard_map/ppermute | solution.py:716
  81.9 21.1 %collective-permute-start.15 = (bf16[512,128]{1,0:T(8,128)(2,1)}, bf16[512,128]{1,0:T(8,128)(2,1)S(1)}, u32[]{:S(2)}, u32[]{:S(2)}) collective-permute-start(bf16[512,128]{1,0:T(8,128)(2,1)} %get-tuple-element.112), channel_id=1, source_target_pairs={{0,3},{1,2},{2,1},{3,0},{4,7},{5,6},{6,5},{7,4},{8,11},{9,10},{10,... | collective-permute-start | bytes 393224 | tf_op jit(solution)/shard_map/ppermute | solution.py:716
  81.9 21.1 %collective-permute-start.16 = (bf16[512,128]{1,0:T(8,128)(2,1)}, bf16[512,128]{1,0:T(8,128)(2,1)S(1)}, u32[]{:S(2)}, u32[]{:S(2)}) collective-permute-start(bf16[512,128]{1,0:T(8,128)(2,1)} %get-tuple-element.113), channel_id=1, source_target_pairs={{0,4},{1,5},{2,6},{3,7},{4,0},{5,1},{6,2},{7,3},{8,12},{9,13},{10,... | collective-permute-start | bytes 393224 | tf_op jit(solution)/shard_map/ppermute | solution.py:716
  83.6 19.5 %collective-permute-start.17 = (bf16[512,128]{1,0:T(8,128)(2,1)}, bf16[512,128]{1,0:T(8,128)(2,1)S(1)}, u32[]{:S(2)}, u32[]{:S(2)}) collective-permute-start(bf16[512,128]{1,0:T(8,128)(2,1)} %get-tuple-element.114), channel_id=1, source_target_pairs={{0,5},{1,4},{2,7},{3,6},{4,1},{5,0},{6,3},{7,2},{8,13},{9,12},{10,... | collective-permute-start | bytes 393224 | tf_op jit(solution)/shard_map/ppermute | solution.py:716
  83.7 19.4 %collective-permute-start.18 = (bf16[512,128]{1,0:T(8,128)(2,1)}, bf16[512,128]{1,0:T(8,128)(2,1)S(1)}, u32[]{:S(2)}, u32[]{:S(2)}) collective-permute-start(bf16[512,128]{1,0:T(8,128)(2,1)} %get-tuple-element.115), channel_id=1, source_target_pairs={{0,6},{1,7},{2,4},{3,5},{4,2},{5,3},{6,0},{7,1},{8,14},{9,15},{10,... | collective-permute-start | bytes 393224 | tf_op jit(solution)/shard_map/ppermute | solution.py:716
  88.0 15.1 %collective-permute-start.19 = (bf16[512,128]{1,0:T(8,128)(2,1)}, bf16[512,128]{1,0:T(8,128)(2,1)S(1)}, u32[]{:S(2)}, u32[]{:S(2)}) collective-permute-start(bf16[512,128]{1,0:T(8,128)(2,1)} %get-tuple-element.116), channel_id=1, source_target_pairs={{0,7},{1,6},{2,5},{3,4},{4,3},{5,2},{6,1},{7,0},{8,15},{9,14},{10,... | collective-permute-start | bytes 393224 | tf_op jit(solution)/shard_map/ppermute | solution.py:716
  115.0 30.3 %all-to-all-start.1 = ((bf16[32,128,128]{2,1,0:T(8,128)(2,1)}), bf16[32,128,128]{2,1,0:T(8,128)(2,1)}, u32[]{:S(2)}, u32[]{:S(2)}) async-start(bf16[32,128,128]{2,1,0:T(8,128)(2,1)} %pack.3), calls=%async_computation.1 | async-start | bytes 2097152 | tf_op jit(solution)/shard_map/all_to_all | solution.py:713
  145.3 41.1 %all-to-all-start.2 = ((bf16[32,128,128]{2,1,0:T(8,128)(2,1)}), bf16[32,128,128]{2,1,0:T(8,128)(2,1)S(1)}, u32[]{:S(2)}, u32[]{:S(2)}) async-start(bf16[32,128,128]{2,1,0:T(8,128)(2,1)} %get-tuple-element.164), calls=%async_computation.2 | async-start | bytes 2097152 | tf_op jit(solution)/shard_map/all_to_all | solution.py:713
  163.4 3.8 %collective-permute-start.20 = (bf16[512,128]{1,0:T(8,128)(2,1)}, bf16[512,128]{1,0:T(8,128)(2,1)S(1)}, u32[]{:S(2)}, u32[]{:S(2)}) collective-permute-start(bf16[512,128]{1,0:T(8,128)(2,1)} %get-tuple-element.140), channel_id=1, source_target_pairs={{0,1},{1,0},{2,3},{3,2},{4,5},{5,4},{6,7},{7,6},{8,9},{9,8},{10,11... | collective-permute-start | bytes 393224 | tf_op jit(solution)/shard_map/ppermute | solution.py:716
  163.7 7.2 %collective-permute-start.21 = (bf16[512,128]{1,0:T(8,128)(2,1)}, bf16[512,128]{1,0:T(8,128)(2,1)S(1)}, u32[]{:S(2)}, u32[]{:S(2)}) collective-permute-start(bf16[512,128]{1,0:T(8,128)(2,1)} %get-tuple-element.141), channel_id=1, source_target_pairs={{0,2},{1,3},{2,0},{3,1},{4,6},{5,7},{6,4},{7,5},{8,10},{9,11},{10,... | collective-permute-start | bytes 393224 | tf_op jit(solution)/shard_map/ppermute | solution.py:716
  165.4 20.9 %collective-permute-start.22 = (bf16[512,128]{1,0:T(8,128)(2,1)}, bf16[512,128]{1,0:T(8,128)(2,1)S(1)}, u32[]{:S(2)}, u32[]{:S(2)}) collective-permute-start(bf16[512,128]{1,0:T(8,128)(2,1)} %get-tuple-element.142), channel_id=1, source_target_pairs={{0,3},{1,2},{2,1},{3,0},{4,7},{5,6},{6,5},{7,4},{8,11},{9,10},{10,... | collective-permute-start | bytes 393224 | tf_op jit(solution)/shard_map/ppermute | solution.py:716
  165.4 20.9 %collective-permute-start.23 = (bf16[512,128]{1,0:T(8,128)(2,1)}, bf16[512,128]{1,0:T(8,128)(2,1)S(1)}, u32[]{:S(2)}, u32[]{:S(2)}) collective-permute-start(bf16[512,128]{1,0:T(8,128)(2,1)} %get-tuple-element.143), channel_id=1, source_target_pairs={{0,4},{1,5},{2,6},{3,7},{4,0},{5,1},{6,2},{7,3},{8,12},{9,13},{10,... | collective-permute-start | bytes 393224 | tf_op jit(solution)/shard_map/ppermute | solution.py:716
  167.1 19.2 %collective-permute-start.24 = (bf16[512,128]{1,0:T(8,128)(2,1)}, bf16[512,128]{1,0:T(8,128)(2,1)S(1)}, u32[]{:S(2)}, u32[]{:S(2)}) collective-permute-start(bf16[512,128]{1,0:T(8,128)(2,1)} %get-tuple-element.144), channel_id=1, source_target_pairs={{0,5},{1,4},{2,7},{3,6},{4,1},{5,0},{6,3},{7,2},{8,13},{9,12},{10,... | collective-permute-start | bytes 393224 | tf_op jit(solution)/shard_map/ppermute | solution.py:716
  167.2 19.1 %collective-permute-start.25 = (bf16[512,128]{1,0:T(8,128)(2,1)}, bf16[512,128]{1,0:T(8,128)(2,1)S(1)}, u32[]{:S(2)}, u32[]{:S(2)}) collective-permute-start(bf16[512,128]{1,0:T(8,128)(2,1)} %get-tuple-element.145), channel_id=1, source_target_pairs={{0,6},{1,7},{2,4},{3,5},{4,2},{5,3},{6,0},{7,1},{8,14},{9,15},{10,... | collective-permute-start | bytes 393224 | tf_op jit(solution)/shard_map/ppermute | solution.py:716
  171.0 15.4 %collective-permute-start.26 = (bf16[512,128]{1,0:T(8,128)(2,1)}, bf16[512,128]{1,0:T(8,128)(2,1)S(1)}, u32[]{:S(2)}, u32[]{:S(2)}) collective-permute-start(bf16[512,128]{1,0:T(8,128)(2,1)} %get-tuple-element.146), channel_id=1, source_target_pairs={{0,7},{1,6},{2,5},{3,4},{4,3},{5,2},{6,1},{7,0},{8,15},{9,14},{10,... | collective-permute-start | bytes 393224 | tf_op jit(solution)/shard_map/ppermute | solution.py:716
  187.5 59.4 %all-to-all-start.3 = ((bf16[32,256,128]{2,1,0:T(8,128)(2,1)}), bf16[32,256,128]{2,1,0:T(8,128)(2,1)S(1)}, u32[]{:S(2)}, u32[]{:S(2)}) async-start(bf16[32,256,128]{2,1,0:T(8,128)(2,1)} %rest.1), calls=%async_computation.3 | async-start | bytes 4194304 | tf_op jit(solution)/shard_map/all_to_all | solution.py:713
  200.7 39.6 %collective-permute-start.27 = (bf16[128,2048]{1,0:T(8,128)(2,1)}, bf16[128,2048]{1,0:T(8,128)(2,1)S(1)}, u32[]{:S(2)}, u32[]{:S(2)}) collective-permute-start(bf16[128,2048]{1,0:T(8,128)(2,1)} %get-tuple-element.155), channel_id=1, source_target_pairs={{0,8},{1,9},{2,10},{3,11},{4,12},{5,13},{6,14},{7,15},{8,0},{9,1},... | collective-permute-start | bytes 1572872 | tf_op jit(solution)/shard_map/ppermute | solution.py:716
  240.3 25.2 %collective-permute-start.28 = (bf16[128,2048]{1,0:T(8,128)(2,1)}, bf16[128,2048]{1,0:T(8,128)(2,1)S(1)}, u32[]{:S(2)}, u32[]{:S(2)}) collective-permute-start(bf16[128,2048]{1,0:T(8,128)(2,1)} %get-tuple-element.160), channel_id=1, source_target_pairs={{0,8},{1,9},{2,10},{3,11},{4,12},{5,13},{6,14},{7,15},{8,0},{9,1},... | collective-permute-start | bytes 1572872 | tf_op jit(solution)/shard_map/ppermute | solution.py:716
  243.6 25.8 %collective-permute-start.29 = (bf16[128,2048]{1,0:T(8,128)(2,1)}, bf16[128,2048]{1,0:T(8,128)(2,1)}, u32[]{:S(2)}, u32[]{:S(2)}) collective-permute-start(bf16[128,2048]{1,0:T(8,128)(2,1)} %add_convert_fusion.1), channel_id=1, source_target_pairs={{0,16},{1,17},{2,18},{3,19},{4,20},{5,21},{6,22},{7,23},{8,24},{9,... | collective-permute-start | bytes 1572872 | tf_op jit(solution)/shard_map/ppermute | solution.py:716
  (31 other events, 489.8 us)

commit v6 on v5

--- a/solution.py
+++ b/solution.py
@@ -264,9 +264,9 @@
 
 
 def attend_kernel(
-    low, arrive, me_ref, pos_ref, rows_ref, probs_ref, *refs
+    low, arrive, me_ref, pos_ref, rows_ref, probs_ref, grad_ref, *refs
 ):
-    parts, (sorted_ref, value_ref, wide, value, att) = refs[:low], refs[low:]
+    parts, scores_ref, (wide, value, value_low, att) = refs[:low], refs[low], refs[low + 1 :]
     bf, f32 = jnp.bfloat16, jnp.float32
     blocks, lanes = pos_ref.shape
     rows = blocks * lanes
@@ -275,17 +275,23 @@
     value[pl.ds(0, CAP), :] = edge
     value[pl.ds(rows + CAP, CAP), :] = edge
     move_in(pos_ref, lambda b: b, [lambda b: rows_ref[b]], [wide], [value], blocks)
-    value_ref[...] = value[...].astype(bf)
+    value_low[...] = value[...].astype(bf)
     arrive()
 
     def some(step, carry):
         tiles, windows, inner = tiles_of(step)
-        vs = [value_ref[at, :] for at in windows]
+        vs = [value_low[at, :] for at in windows]
+        gs = [grad_ref[at, :] for at in tiles]
         probs = [probs_ref[at, :] for at in tiles]
         attended = [jnp.dot(p, v, preferred_element_type=f32) for p, v in zip(probs, vs)]
-        for at, to, one in zip(tiles, inner, attended):
+        grad_probs = [lax.dot_general(g, v, NT, preferred_element_type=f32) for g, v in zip(gs, vs)]
+        deltas = [
+            jnp.sum(g.astype(f32) * one.astype(bf).astype(f32), axis=1, keepdims=True)
+            for g, one in zip(gs, attended)
+        ]
+        for at, to, one, p, gp, delta in zip(tiles, inner, attended, probs, grad_probs, deltas):
             att[to, :] = one
-            sorted_ref[at, :] = one.astype(bf)
+            scores_ref[at, :] = (p.astype(f32) * (gp - delta)).astype(bf)
         return carry
 
     lax.fori_loop(0, rows // TILE // UNROLL, some, 0)
@@ -338,8 +344,7 @@
 
 
 def rest_kernel(
-    scale, pos_ref, grad_ref, sorted_ref, query_ref, key_ref, value_ref, probs_ref,
-    out_ref, wide, grad_query, grad_key, more,
+    scale, pos_ref, scores_ref, query_ref, key_ref, out_ref, wide, more, grad_query, grad_key
 ):
     bf, f32 = jnp.bfloat16, jnp.float32
     blocks, lanes = pos_ref.shape
@@ -348,23 +353,12 @@
 
     def some(step, carry):
         tiles, windows, inner = tiles_of(step)
-        gs = [grad_ref[at, :] for at in tiles]
+        ds = [scores_ref[at, :] for at in tiles]
         qs = [query_ref[at, :] for at in inner]
         ks = [key_ref[at, :] for at in windows]
-        vs = [value_ref[at, :] for at in windows]
-        probs = [probs_ref[at, :] for at in tiles]
-        attended = [sorted_ref[at, :].astype(f32) for at in tiles]
-        grad_probs = [lax.dot_general(g, v, NT, preferred_element_type=f32) for g, v in zip(gs, vs)]
-        deltas = [
-            jnp.sum(g.astype(f32) * one, axis=1, keepdims=True) for g, one in zip(gs, attended)
-        ]
-        grad_scores = [
-            (p.astype(f32) * (gp - delta)).astype(bf)
-            for p, gp, delta in zip(probs, grad_probs, deltas)
-        ]
-        grad_queries = [jnp.dot(d, k, preferred_element_type=f32) for d, k in zip(grad_scores, ks)]
+        grad_queries = [jnp.dot(d, k, preferred_element_type=f32) for d, k in zip(ds, ks)]
         more_keys = [
-            lax.dot_general(d, q, TN, preferred_element_type=f32) for d, q in zip(grad_scores, qs)
+            lax.dot_general(d, q, TN, preferred_element_type=f32) for d, q in zip(ds, qs)
         ]
         for at, one in zip(inner, grad_queries):
             grad_query[at, :] = one
@@ -485,12 +479,13 @@
             ((padded, bf), (padded, bf), ((rows, WIN), bf)), (padded, padded, wide), 12, "scores", 1,
         )
 
-    def attend(value, probs):
-        return call(
-            functools.partial(attend_kernel, low), (me, pos, value, probs),
-            (((blocks // low * lanes, size), bf),) * low + ((plain, bf), (padded, bf)),
-            (padded, padded), 12, "attend", 1,
+    def attend(value, probs, grad):
+        *attended, scores = run(
+            functools.partial(attend_kernel, low), (me, pos, value, probs, grad),
+            (((blocks // low * lanes, size), bf),) * low + (((rows, WIN), bf),),
+            ((wide, f32), (padded, f32), (padded, bf), (padded, f32)), 12, "attend", 2,
         )
+        return attended, scores
 
     def grad_value(grads, probs):
         return call(
@@ -498,11 +493,10 @@
             (((blocks, lanes, size), bf), (plain, bf)), (padded, padded), 12, "grad_value", 1,
         )
 
-    def rest(grad, attended, query, key, value, probs):
+    def rest(scores, query, key):
         return call(
-            functools.partial(rest_kernel, scale),
-            (pos, grad, attended, query, key, value, probs),
-            (((blocks, 2 * lanes, size), bf),), (padded, padded, wide), 16, "rest",
+            functools.partial(rest_kernel, scale), (pos, scores, query, key),
+            (((blocks, 2 * lanes, size), bf),), (wide, padded, padded), 12, "rest",
         )[0]
 
     return scores, attend, grad_value, rest
@@ -738,8 +732,6 @@
             there = {r: over(blocks.pop(r).astype(bf), r) for r in rank}
             if rank is ranks[0]:
                 there, after = together((there, after))
-            else:
-                there, blocks = together((there, blocks))
             for r, block in there.items():
                 blocks[r & (r - 1)] += block.astype(f32)
         return blocks[0].astype(bf), after
@@ -769,10 +761,10 @@
     query, key, probs = scores(arrived, bias)
     grad_value, grad_sorted = grad_of_value(grad_heads, probs)
     value, grad_value = together((value, grad_value))
-    *attended, att_sorted, value_sorted = attend(value, probs)
+    attended, grad_scores = attend(value, probs, grad_sorted)
     back_value = exchange(grad_value)
     attended = swap(attended)
-    grads = rest(grad_sorted, att_sorted, query, key, value_sorted, probs)
+    grads = rest(grad_scores, query, key)
     grads, attended = together((grads, attended))
     grads, back_value = together((grads, back_value))
     back = exchange(grads)

time: 273 us -> 270 us (0.989)
  other arithmetic: 9.04 us -> 5.91 us
    convert_element_type x2 -> x0, other arithmetic: 3.38 us -> none  [sum_stack(): blocks = {r: block.astype(f32) for r, block in enumerate(blocks)}]
  transfers between devices with their start and end apart: 34 -> 34, of which waited for: 14 -> 14; matrix products, arithmetic and copies ran while one was open for 2% -> 1% of each run, Pallas kernels for 32% -> 32%
where the time goes in v6:
time: 270 us; the launch traced here: 269 us
  waiting for transfers between devices  112 us (41%)
  Pallas kernels  87.5 us (32%)
  starting transfers between devices  55.6 us (21%)
  local copies, waits for them, and re-layouts  6.19 us (2%)
  other arithmetic  5.91 us (2%)
    ppermute x30, waiting for transfers between devices, send(): return lax.ppermute(block, 'seq', [(i, i ^ bits) for i in range(owners)])  99.7 us
    pallas_call x8, Pallas kernels, run(): pl.pallas_call(body, out_shape=tuple((jax.ShapeDtypeStruct(shape, kind) f...  80 us
    ppermute x30, starting transfers between devices, send(): return lax.ppermute(block, 'seq', [(i, i ^ bits) for i in range(owners)])  37.6 us
    all_to_all x4, starting transfers between devices, exchange(): return lax.all_to_all(rows, 'seq', split_axis=0, concat_axis=0, tiled=True)  18 us
    all_to_all x4, waiting for transfers between devices, exchange(): return lax.all_to_all(rows, 'seq', split_axis=0, concat_axis=0, tiled=True)  12.6 us
    unnamed x58, local copies, waits for them, and re-layouts  5.59 us
  transfers between devices with their start and end apart: 34, of which 14 were waited for; matrix products, arithmetic and copies ran while one was open for 1% of the time, Pallas kernels for 32%

profile of v6, /device:TPU:0, one launch (start us, length us, event | category | flops | bytes accessed | tf_op | source)
XLA Modules:
  0.0 268.7 jit_solution(17100721442121005851)
XLA Ops:
  2.7 2.7 pack_weight.1
  5.3 3.1 %collective-permute-start = (bf16[544,128]{1,0:T(8,128)(2,1)}, bf16[544,128]{1,0:T(8,128)(2,1)S(1)}, u32[]{:S(2)}, u32[]{:S(2)}) collective-permute-start(bf16[544,128]{1,0:T(8,128)(2,1)} %get-tuple-element.85), channel_id=1, source_target_pairs={{0,8},{1,9},{2,10},{3,11},{4,12},{5,13},{6,14},{7,15},{8,0},{9,1},... | collective-permute-start | bytes 417800 | tf_op jit(solution)/shard_map/ppermute | solution.py:710
  8.4 2.6 collective-permute-start.1
  11.0 3.1 %collective-permute-done = bf16[544,128]{1,0:T(8,128)(2,1)S(1)} collective-permute-done((bf16[544,128]{1,0:T(8,128)(2,1)}, bf16[544,128]{1,0:T(8,128)(2,1)S(1)}, u32[]{:S(2)}, u32[]{:S(2)}) %collective-permute-start) | collective-permute-done | bytes 139296 | tf_op jit(solution)/shard_map/ppermute | solution.py:710
  14.1 8.0 %collective-permute-done.1 = bf16[544,128]{1,0:T(8,128)(2,1)S(1)} collective-permute-done((bf16[544,128]{1,0:T(8,128)(2,1)}, bf16[544,128]{1,0:T(8,128)(2,1)S(1)}, u32[]{:S(2)}, u32[]{:S(2)}) %collective-permute-start.1) | collective-permute-done | bytes 139296 | tf_op jit(solution)/shard_map/ppermute | solution.py:710
  22.1 3.1 %collective-permute-start.7 = (bf16[128,2048]{1,0:T(8,128)(2,1)}, bf16[128,2048]{1,0:T(8,128)(2,1)S(1)}, u32[]{:S(2)}, u32[]{:S(2)}) collective-permute-start(bf16[128,2048]{1,0:T(8,128)(2,1)} %refs_9_), channel_id=1, source_target_pairs={{0,16},{1,17},{2,18},{3,19},{4,20},{5,21},{6,22},{7,23},{8,24},{9,... | collective-permute-start | bytes 1572872 | tf_op jit(solution)/shard_map/ppermute | solution.py:710
  29.8 18.0 %collective-permute-done.7.refs_11_ = bf16[128,2048]{1,0:T(8,128)(2,1)S(1)} collective-permute-done((bf16[128,2048]{1,0:T(8,128)(2,1)}, bf16[128,2048]{1,0:T(8,128)(2,1)S(1)}, u32[]{:S(2)}, u32[]{:S(2)}) %collective-permute-start.7) | collective-permute-done | bytes 524320 | tf_op jit(solution)/shard_map/ppermute | solution.py:710
  49.5 2.1 pack.2
  51.6 2.6 collective-permute-done.6.refs_10_
  56.3 6.9 %collective-permute-done.8.refs_12_ = bf16[128,2048]{1,0:T(8,128)(2,1)} collective-permute-done((bf16[128,2048]{1,0:T(8,128)(2,1)S(1)}, bf16[128,2048]{1,0:T(8,128)(2,1)}, u32[]{:S(2)}, u32[]{:S(2)}) %collective-permute-start.8) | collective-permute-done | bytes 524320 | tf_op jit(solution)/shard_map/ppermute | solution.py:710
  63.2 2.8 %all-to-all-start = ((bf16[32,256,128]{2,1,0:T(8,128)(2,1)}), bf16[32,256,128]{2,1,0:T(8,128)(2,1)S(1)}, u32[]{:S(2)}, u32[]{:S(2)}) async-start(bf16[32,256,128]{2,1,0:T(8,128)(2,1)} %pack.2), calls=%async_computation | async-start | bytes 4194304 | tf_op jit(solution)/shard_map/all_to_all | solution.py:707
  71.5 8.3 %project_back.1 = (bf16[512,128]{1,0:T(8,128)(2,1)}, bf16[512,128]{1,0:T(8,128)(2,1)}, bf16[512,128]{1,0:T(8,128)(2,1)}, bf16[512,128]{1,0:T(8,128)(2,1)}, bf16[...) custom-call(s32[2]{0:T(128)} %pad_add_fusion.refs_0_, ...), custom_call_target="tpu_custom_call" | custom-call | bytes 28000000 | tf_op jit(solution)/shard_map/project_back/pallas_call | solution.py:60
  83.7 2.6 collective-permute-start.18
  88.0 4.0 %collective-permute-start.19 = (bf16[512,128]{1,0:T(8,128)(2,1)}, bf16[512,128]{1,0:T(8,128)(2,1)S(1)}, u32[]{:S(2)}, u32[]{:S(2)}) collective-permute-start(bf16[512,128]{1,0:T(8,128)(2,1)} %get-tuple-element.111), channel_id=1, source_target_pairs={{0,7},{1,6},{2,5},{3,4},{4,3},{5,2},{6,1},{7,0},{8,15},{9,14},{10,... | collective-permute-start | bytes 393224 | tf_op jit(solution)/shard_map/ppermute | solution.py:710
  92.0 11.0 %place.1 = (s32[32,128]{1,0:T(8,128)}, bf16[4096,128]{1,0:T(8,128)(2,1)}) custom-call(s32[2]{0:T(128)} %pad_add_fusion.refs_0_, bf16[4,544,128]{2,1,0:T(8,128)(2,1)} %copy-done.6, bf16[4,544,128]{2,1,0:T(8,128)(2,1)} %copy-done.10, bf16[4,544,128]{2,1,0:T(8,128)(2,1)} %copy-done.7, bf16[4,544,128]{2,1,0:T(8,128)(2,1)} %copy-done.11, ...), custom_call_target="tpu_custom_call" | custom-call | bytes 28000000 | tf_op jit(solution)/shard_map/place/pallas_call | solution.py:60
  103.1 11.9 %all-to-all-done.refs_1_ = bf16[32,256,128]{2,1,0:T(8,128)(2,1)S(1)} async-done(((bf16[32,256,128]{2,1,0:T(8,128)(2,1)}), bf16[32,256,128]{2,1,0:T(8,128)(2,1)S(1)}, u32[]{:S(2)}, u32[]{:S(2)}) %all-to-all-start) | async-done | bytes 2097184 | tf_op jit(solution)/shard_map/all_to_all | solution.py:707
  115.0 4.0 %all-to-all-start.1 = ((bf16[32,128,128]{2,1,0:T(8,128)(2,1)}), bf16[32,128,128]{2,1,0:T(8,128)(2,1)}, u32[]{:S(2)}, u32[]{:S(2)}) async-start(bf16[32,128,128]{2,1,0:T(8,128)(2,1)} %pack.3), calls=%async_computation.1 | async-start | bytes 2097152 | tf_op jit(solution)/shard_map/all_to_all | solution.py:707
  119.1 12.3 %scores.1 = (bf16[4160,128]{1,0:T(8,128)(2,1)}, bf16[4160,128]{1,0:T(8,128)(2,1)}, bf16[4096,128]{1,0:T(8,128)(2,1)}) custom-call(s32[32,128]{1,0:T(8,128)} %get-tuple-element.114.refs_0_.refs_1_, bf16[32,256,128]{2,1,0:T(8,128)(2,1)} %copy-done.5, bf16[4096,128]{1,0:T(8,128)(2,1)} %get-tuple-element.125.refs_2_), custom_call_target="tpu_custom_call" | custom-call | bytes 42000000 | tf_op jit(solution)/shard_map/scores/pallas_call | solution.py:60
  131.4 13.2 %grad_value.1 = (bf16[32,128,128]{2,1,0:T(8,128)(2,1)}, bf16[4096,128]{1,0:T(8,128)(2,1)}) custom-call(s32[2]{0:T(128)} %pad_add_fusion.refs_0_, s32[32,128]{1,0:T(8,128)} %get-tuple-element.114.refs_0_.refs_1_, bf16[512,128]{1,0:T(8,128)(2,1)} %get-tuple-element.116.refs_2_, bf16[512,128]{1,0:T(8,128)(2,1)} %copy-done.15, bf16[512,128]{1,0:T(8,128)(2,1)} %copy-done.16, ...), custom_call_target="tpu_custom_call" | custom-call | bytes 42000000 | tf_op jit(solution)/shard_map/grad_value/pallas_call | solution.py:60
  145.3 5.1 %all-to-all-start.2 = ((bf16[32,128,128]{2,1,0:T(8,128)(2,1)}), bf16[32,128,128]{2,1,0:T(8,128)(2,1)S(1)}, u32[]{:S(2)}, u32[]{:S(2)}) async-start(bf16[32,128,128]{2,1,0:T(8,128)(2,1)} %get-tuple-element.154), calls=%async_computation.2 | async-start | bytes 2097152 | tf_op jit(solution)/shard_map/all_to_all | solution.py:707
  150.4 13.9 %attend.1 = (bf16[512,128]{1,0:T(8,128)(2,1)}, bf16[512,128]{1,0:T(8,128)(2,1)}, bf16[512,128]{1,0:T(8,128)(2,1)}, bf16[512,128]{1,0:T(8,128)(2,1)}, bf16[512,12...) custom-call(s32[2]{0:T(128)} %pad_add_fusion.refs_0_, ...), custom_call_target="tpu_custom_call" | custom-call | bytes 42000000 | tf_op jit(solution)/shard_map/attend/pallas_call | solution.py:60
  168.1 2.6 collective-permute-start.25
  172.3 12.0 %rest.1 = bf16[32,256,128]{2,1,0:T(8,128)(2,1)} custom-call(s32[32,128]{1,0:T(8,128)} %get-tuple-element.114.refs_0_.refs_1_, bf16[4096,128]{1,0:T(8,128)(2,1)} %get-tuple-element.130.refs_1_, bf16[4160,128]{1,0:T(8,128)(2,1)} %get-tuple-element.131.refs_2_, bf16[4160,128]{1,0:T(8,128)(2,1)} %get-tuple-element.132.refs_3_), custom_call_target="tpu_custom_call" | custom-call | bytes 42000000 | tf_op jit(solution)/shard_map/rest/pallas_call | solution.py:60
  185.5 6.0 %all-to-all-start.3 = ((bf16[32,256,128]{2,1,0:T(8,128)(2,1)}), bf16[32,256,128]{2,1,0:T(8,128)(2,1)S(1)}, u32[]{:S(2)}, u32[]{:S(2)}) async-start(bf16[32,256,128]{2,1,0:T(8,128)(2,1)} %rest.1), calls=%async_computation.3 | async-start | bytes 4194304 | tf_op jit(solution)/shard_map/all_to_all | solution.py:707
  191.5 6.7 %project.1 = (bf16[128,2048]{1,0:T(8,128)(2,1)}, bf16[128,2048]{1,0:T(8,128)(2,1)}, bf16[128,2048]{1,0:T(8,128)(2,1)}, bf16[128,2048]{1,0:T(8,128)(2,1)}) custom-call(bf16[8,2048,128]{2,1,0:T(8,128)(2,1)} %get-tuple-element.101.refs_0_, bf16[512,128]{1,0:T(8,128)(2,1)} %get-tuple-element.141.refs_1_, bf16[512,128]{1,0:T(8,128)(2,1)} %copy-done.18, ...), custom_call_target="tpu_custom_call" | custom-call | bytes 21000000 | tf_op jit(solution)/shard_map/project/pallas_call | solution.py:60
  198.3 1.8 collective-permute-start.28
  200.4 37.8 %collective-permute-done.28 = bf16[128,2048]{1,0:T(8,128)(2,1)S(1)} collective-permute-done((bf16[128,2048]{1,0:T(8,128)(2,1)}, bf16[128,2048]{1,0:T(8,128)(2,1)S(1)}, u32[]{:S(2)}, u32[]{:S(2)}) %collective-permute-start.28) | collective-permute-done | bytes 524320 | tf_op jit(solution)/shard_map/ppermute | solution.py:710
  239.4 4.3 %collective-permute-start.29 = (bf16[128,2048]{1,0:T(8,128)(2,1)S(1)}, bf16[128,2048]{1,0:T(8,128)(2,1)}, u32[]{:S(2)}, u32[]{:S(2)}) collective-permute-start(bf16[128,2048]{1,0:T(8,128)(2,1)S(1)} %add_convert_fusion.1), channel_id=1, source_target_pairs={{0,16},{1,17},{2,18},{3,19},{4,20},{5,21},{6,22},{7,23},{8,24},{9,... | collective-permute-start | bytes 1572872 | tf_op jit(solution)/shard_map/ppermute | solution.py:710
  245.3 2.0 unpack.2
  247.3 12.3 %collective-permute-done.27 = bf16[128,2048]{1,0:T(8,128)(2,1)} collective-permute-done((bf16[128,2048]{1,0:T(8,128)(2,1)}, bf16[128,2048]{1,0:T(8,128)(2,1)}, u32[]{:S(2)}, u32[]{:S(2)}) %collective-permute-start.27) | collective-permute-done | bytes 524320 | tf_op jit(solution)/shard_map/ppermute | solution.py:710
  259.6 6.6 %collective-permute-done.29 = bf16[128,2048]{1,0:T(8,128)(2,1)} collective-permute-done((bf16[128,2048]{1,0:T(8,128)(2,1)S(1)}, bf16[128,2048]{1,0:T(8,128)(2,1)}, u32[]{:S(2)}, u32[]{:S(2)}) %collective-permute-start.29) | collective-permute-done | bytes 524320 | tf_op jit(solution)/shard_map/ppermute | solution.py:710
  266.3 2.4 add_convert_fusion
  (113 shorter events, 31.6 us)
Async XLA Ops:
  5.3 8.7 %collective-permute-start = (bf16[544,128]{1,0:T(8,128)(2,1)}, bf16[544,128]{1,0:T(8,128)(2,1)S(1)}, u32[]{:S(2)}, u32[]{:S(2)}) collective-permute-start(bf16[544,128]{1,0:T(8,128)(2,1)} %get-tuple-element.85), channel_id=1, source_target_pairs={{0,8},{1,9},{2,10},{3,11},{4,12},{5,13},{6,14},{7,15},{8,0},{9,1},... | collective-permute-start | bytes 417800 | tf_op jit(solution)/shard_map/ppermute | solution.py:710
  8.4 13.7 %collective-permute-start.1 = (bf16[544,128]{1,0:T(8,128)(2,1)}, bf16[544,128]{1,0:T(8,128)(2,1)S(1)}, u32[]{:S(2)}, u32[]{:S(2)}) collective-permute-start(bf16[544,128]{1,0:T(8,128)(2,1)} %get-tuple-element.86), channel_id=1, source_target_pairs={{0,16},{1,17},{2,18},{3,19},{4,20},{5,21},{6,22},{7,23},{8,24},{9,... | collective-permute-start | bytes 417800 | tf_op jit(solution)/shard_map/ppermute | solution.py:710
  11.0 11.1 %collective-permute-start.2 = (bf16[544,128]{1,0:T(8,128)(2,1)}, bf16[544,128]{1,0:T(8,128)(2,1)S(1)}, u32[]{:S(2)}, u32[]{:S(2)}) collective-permute-start(bf16[544,128]{1,0:T(8,128)(2,1)} %get-tuple-element.87), channel_id=1, source_target_pairs={{0,24},{1,25},{2,26},{3,27},{4,28},{5,29},{6,30},{7,31},{8,16},{9,... | collective-permute-start | bytes 417800 | tf_op jit(solution)/shard_map/ppermute | solution.py:710
  22.1 25.7 %collective-permute-start.7 = (bf16[128,2048]{1,0:T(8,128)(2,1)}, bf16[128,2048]{1,0:T(8,128)(2,1)S(1)}, u32[]{:S(2)}, u32[]{:S(2)}) collective-permute-start(bf16[128,2048]{1,0:T(8,128)(2,1)} %refs_9_), channel_id=1, source_target_pairs={{0,16},{1,17},{2,18},{3,19},{4,20},{5,21},{6,22},{7,23},{8,24},{9,... | collective-permute-start | bytes 1572872 | tf_op jit(solution)/shard_map/ppermute | solution.py:710
  26.2 28.0 %collective-permute-start.3 = (bf16[4,544,128]{2,1,0:T(8,128)(2,1)S(1)}, bf16[4,544,128]{2,1,0:T(8,128)(2,1)S(1)}, u32[]{:S(2)}, u32[]{:S(2)}) collective-permute-start(bf16[4,544,128]{2,1,0:T(8,128)(2,1)S(1)} %pad_maximum_fusion.refs_1_), channel_id=1, source_target_pairs={{0,2},{1,3},{2,0},{3,1},{4,6},{5,7},{6,4},{7,5},{8,10},{9,11},{10,... | collective-permute-start | bytes 1671176 | tf_op jit(solution)/shard_map/ppermute | solution.py:710
  27.8 26.5 %collective-permute-start.4 = (bf16[4,544,128]{2,1,0:T(8,128)(2,1)S(1)}, bf16[4,544,128]{2,1,0:T(8,128)(2,1)S(1)}, u32[]{:S(2)}, u32[]{:S(2)}) collective-permute-start(bf16[4,544,128]{2,1,0:T(8,128)(2,1)S(1)} %pad_maximum_fusion.refs_1_), channel_id=1, source_target_pairs={{0,4},{1,5},{2,6},{3,7},{4,0},{5,1},{6,2},{7,3},{8,12},{9,13},{10,... | collective-permute-start | bytes 1671176 | tf_op jit(solution)/shard_map/ppermute | solution.py:710
  29.3 25.0 %collective-permute-start.5 = (bf16[4,544,128]{2,1,0:T(8,128)(2,1)S(1)}, bf16[4,544,128]{2,1,0:T(8,128)(2,1)S(1)}, u32[]{:S(2)}, u32[]{:S(2)}) collective-permute-start(bf16[4,544,128]{2,1,0:T(8,128)(2,1)S(1)} %pad_maximum_fusion.refs_1_), channel_id=1, source_target_pairs={{0,6},{1,7},{2,4},{3,5},{4,2},{5,3},{6,0},{7,1},{8,14},{9,15},{10,... | collective-permute-start | bytes 1671176 | tf_op jit(solution)/shard_map/ppermute | solution.py:710
  29.8 24.5 %collective-permute-start.6 = (bf16[128,2048]{1,0:T(8,128)(2,1)}, bf16[128,2048]{1,0:T(8,128)(2,1)S(1)}, u32[]{:S(2)}, u32[]{:S(2)}) collective-permute-start(bf16[128,2048]{1,0:T(8,128)(2,1)} %refs_9_), channel_id=1, source_target_pairs={{0,8},{1,9},{2,10},{3,11},{4,12},{5,13},{6,14},{7,15},{8,0},{9,1},... | collective-permute-start | bytes 1572872 | tf_op jit(solution)/shard_map/ppermute | solution.py:710
  47.8 15.4 %collective-permute-start.8 = (bf16[128,2048]{1,0:T(8,128)(2,1)S(1)}, bf16[128,2048]{1,0:T(8,128)(2,1)}, u32[]{:S(2)}, u32[]{:S(2)}) collective-permute-start(bf16[128,2048]{1,0:T(8,128)(2,1)S(1)} %collective-permute-done.7.refs_11_), channel_id=1, source_target_pairs={{0,8},{1,9},{2,10},{3,11},{4,12},{5,13},{6,14},{7,15},{8,0},{9,1},... | collective-permute-start | bytes 1572872 | tf_op jit(solution)/shard_map/ppermute | solution.py:710
  63.2 51.8 %all-to-all-start = ((bf16[32,256,128]{2,1,0:T(8,128)(2,1)}), bf16[32,256,128]{2,1,0:T(8,128)(2,1)S(1)}, u32[]{:S(2)}, u32[]{:S(2)}) async-start(bf16[32,256,128]{2,1,0:T(8,128)(2,1)} %pack.2), calls=%async_computation | async-start | bytes 4194304 | tf_op jit(solution)/shard_map/all_to_all | solution.py:707
  66.6 4.1 %collective-permute-start.11 = (bf16[4,544,128]{2,1,0:T(8,128)(2,1)}, bf16[4,544,128]{2,1,0:T(8,128)(2,1)S(1)}, u32[]{:S(2)}, u32[]{:S(2)}) collective-permute-start(bf16[4,544,128]{2,1,0:T(8,128)(2,1)} %copy-done.8), channel_id=1, source_target_pairs={{0,1},{1,0},{2,3},{3,2},{4,5},{5,4},{6,7},{7,6},{8,9},{9,8},{10,11... | collective-permute-start | bytes 1671176 | tf_op jit(solution)/shard_map/ppermute | solution.py:710
  66.9 4.7 %collective-permute-start.12 = (bf16[4,544,128]{2,1,0:T(8,128)(2,1)}, bf16[4,544,128]{2,1,0:T(8,128)(2,1)}, u32[]{:S(2)}, u32[]{:S(2)}) collective-permute-start(bf16[4,544,128]{2,1,0:T(8,128)(2,1)} %copy-done.9), channel_id=1, source_target_pairs={{0,1},{1,0},{2,3},{3,2},{4,5},{5,4},{6,7},{7,6},{8,9},{9,8},{10,11... | collective-permute-start | bytes 1671176 | tf_op jit(solution)/shard_map/ppermute | solution.py:710
  79.9 3.8 %collective-permute-start.13 = (bf16[512,128]{1,0:T(8,128)(2,1)}, bf16[512,128]{1,0:T(8,128)(2,1)S(1)}, u32[]{:S(2)}, u32[]{:S(2)}) collective-permute-start(bf16[512,128]{1,0:T(8,128)(2,1)} %get-tuple-element.105), channel_id=1, source_target_pairs={{0,1},{1,0},{2,3},{3,2},{4,5},{5,4},{6,7},{7,6},{8,9},{9,8},{10,11... | collective-permute-start | bytes 393224 | tf_op jit(solution)/shard_map/ppermute | solution.py:710
  80.2 7.8 %collective-permute-start.14 = (bf16[512,128]{1,0:T(8,128)(2,1)}, bf16[512,128]{1,0:T(8,128)(2,1)S(1)}, u32[]{:S(2)}, u32[]{:S(2)}) collective-permute-start(bf16[512,128]{1,0:T(8,128)(2,1)} %get-tuple-element.106), channel_id=1, source_target_pairs={{0,2},{1,3},{2,0},{3,1},{4,6},{5,7},{6,4},{7,5},{8,10},{9,11},{10,... | collective-permute-start | bytes 393224 | tf_op jit(solution)/shard_map/ppermute | solution.py:710
  81.9 21.1 %collective-permute-start.15 = (bf16[512,128]{1,0:T(8,128)(2,1)}, bf16[512,128]{1,0:T(8,128)(2,1)S(1)}, u32[]{:S(2)}, u32[]{:S(2)}) collective-permute-start(bf16[512,128]{1,0:T(8,128)(2,1)} %get-tuple-element.107), channel_id=1, source_target_pairs={{0,3},{1,2},{2,1},{3,0},{4,7},{5,6},{6,5},{7,4},{8,11},{9,10},{10,... | collective-permute-start | bytes 393224 | tf_op jit(solution)/shard_map/ppermute | solution.py:710
  81.9 21.1 %collective-permute-start.16 = (bf16[512,128]{1,0:T(8,128)(2,1)}, bf16[512,128]{1,0:T(8,128)(2,1)S(1)}, u32[]{:S(2)}, u32[]{:S(2)}) collective-permute-start(bf16[512,128]{1,0:T(8,128)(2,1)} %get-tuple-element.108), channel_id=1, source_target_pairs={{0,4},{1,5},{2,6},{3,7},{4,0},{5,1},{6,2},{7,3},{8,12},{9,13},{10,... | collective-permute-start | bytes 393224 | tf_op jit(solution)/shard_map/ppermute | solution.py:710
  83.6 19.5 %collective-permute-start.17 = (bf16[512,128]{1,0:T(8,128)(2,1)}, bf16[512,128]{1,0:T(8,128)(2,1)S(1)}, u32[]{:S(2)}, u32[]{:S(2)}) collective-permute-start(bf16[512,128]{1,0:T(8,128)(2,1)} %get-tuple-element.109), channel_id=1, source_target_pairs={{0,5},{1,4},{2,7},{3,6},{4,1},{5,0},{6,3},{7,2},{8,13},{9,12},{10,... | collective-permute-start | bytes 393224 | tf_op jit(solution)/shard_map/ppermute | solution.py:710
  83.7 19.4 %collective-permute-start.18 = (bf16[512,128]{1,0:T(8,128)(2,1)}, bf16[512,128]{1,0:T(8,128)(2,1)S(1)}, u32[]{:S(2)}, u32[]{:S(2)}) collective-permute-start(bf16[512,128]{1,0:T(8,128)(2,1)} %get-tuple-element.110), channel_id=1, source_target_pairs={{0,6},{1,7},{2,4},{3,5},{4,2},{5,3},{6,0},{7,1},{8,14},{9,15},{10,... | collective-permute-start | bytes 393224 | tf_op jit(solution)/shard_map/ppermute | solution.py:710
  88.0 15.1 %collective-permute-start.19 = (bf16[512,128]{1,0:T(8,128)(2,1)}, bf16[512,128]{1,0:T(8,128)(2,1)S(1)}, u32[]{:S(2)}, u32[]{:S(2)}) collective-permute-start(bf16[512,128]{1,0:T(8,128)(2,1)} %get-tuple-element.111), channel_id=1, source_target_pairs={{0,7},{1,6},{2,5},{3,4},{4,3},{5,2},{6,1},{7,0},{8,15},{9,14},{10,... | collective-permute-start | bytes 393224 | tf_op jit(solution)/shard_map/ppermute | solution.py:710
  115.0 30.3 %all-to-all-start.1 = ((bf16[32,128,128]{2,1,0:T(8,128)(2,1)}), bf16[32,128,128]{2,1,0:T(8,128)(2,1)}, u32[]{:S(2)}, u32[]{:S(2)}) async-start(bf16[32,128,128]{2,1,0:T(8,128)(2,1)} %pack.3), calls=%async_computation.1 | async-start | bytes 2097152 | tf_op jit(solution)/shard_map/all_to_all | solution.py:707
  145.3 39.1 %all-to-all-start.2 = ((bf16[32,128,128]{2,1,0:T(8,128)(2,1)}), bf16[32,128,128]{2,1,0:T(8,128)(2,1)S(1)}, u32[]{:S(2)}, u32[]{:S(2)}) async-start(bf16[32,128,128]{2,1,0:T(8,128)(2,1)} %get-tuple-element.154), calls=%async_computation.2 | async-start | bytes 2097152 | tf_op jit(solution)/shard_map/all_to_all | solution.py:707
  164.3 3.8 %collective-permute-start.20 = (bf16[512,128]{1,0:T(8,128)(2,1)}, bf16[512,128]{1,0:T(8,128)(2,1)S(1)}, u32[]{:S(2)}, u32[]{:S(2)}) collective-permute-start(bf16[512,128]{1,0:T(8,128)(2,1)} %get-tuple-element.134), channel_id=1, source_target_pairs={{0,1},{1,0},{2,3},{3,2},{4,5},{5,4},{6,7},{7,6},{8,9},{9,8},{10,11... | collective-permute-start | bytes 393224 | tf_op jit(solution)/shard_map/ppermute | solution.py:710
  164.6 6.7 %collective-permute-start.21 = (bf16[512,128]{1,0:T(8,128)(2,1)}, bf16[512,128]{1,0:T(8,128)(2,1)S(1)}, u32[]{:S(2)}, u32[]{:S(2)}) collective-permute-start(bf16[512,128]{1,0:T(8,128)(2,1)} %get-tuple-element.135), channel_id=1, source_target_pairs={{0,2},{1,3},{2,0},{3,1},{4,6},{5,7},{6,4},{7,5},{8,10},{9,11},{10,... | collective-permute-start | bytes 393224 | tf_op jit(solution)/shard_map/ppermute | solution.py:710
  166.3 18.0 %collective-permute-start.22 = (bf16[512,128]{1,0:T(8,128)(2,1)}, bf16[512,128]{1,0:T(8,128)(2,1)S(1)}, u32[]{:S(2)}, u32[]{:S(2)}) collective-permute-start(bf16[512,128]{1,0:T(8,128)(2,1)} %get-tuple-element.136), channel_id=1, source_target_pairs={{0,3},{1,2},{2,1},{3,0},{4,7},{5,6},{6,5},{7,4},{8,11},{9,10},{10,... | collective-permute-start | bytes 393224 | tf_op jit(solution)/shard_map/ppermute | solution.py:710
  166.3 18.0 %collective-permute-start.23 = (bf16[512,128]{1,0:T(8,128)(2,1)}, bf16[512,128]{1,0:T(8,128)(2,1)S(1)}, u32[]{:S(2)}, u32[]{:S(2)}) collective-permute-start(bf16[512,128]{1,0:T(8,128)(2,1)} %get-tuple-element.137), channel_id=1, source_target_pairs={{0,4},{1,5},{2,6},{3,7},{4,0},{5,1},{6,2},{7,3},{8,12},{9,13},{10,... | collective-permute-start | bytes 393224 | tf_op jit(solution)/shard_map/ppermute | solution.py:710
  168.0 16.3 %collective-permute-start.24 = (bf16[512,128]{1,0:T(8,128)(2,1)}, bf16[512,128]{1,0:T(8,128)(2,1)S(1)}, u32[]{:S(2)}, u32[]{:S(2)}) collective-permute-start(bf16[512,128]{1,0:T(8,128)(2,1)} %get-tuple-element.138), channel_id=1, source_target_pairs={{0,5},{1,4},{2,7},{3,6},{4,1},{5,0},{6,3},{7,2},{8,13},{9,12},{10,... | collective-permute-start | bytes 393224 | tf_op jit(solution)/shard_map/ppermute | solution.py:710
  168.1 16.2 %collective-permute-start.25 = (bf16[512,128]{1,0:T(8,128)(2,1)}, bf16[512,128]{1,0:T(8,128)(2,1)S(1)}, u32[]{:S(2)}, u32[]{:S(2)}) collective-permute-start(bf16[512,128]{1,0:T(8,128)(2,1)} %get-tuple-element.139), channel_id=1, source_target_pairs={{0,6},{1,7},{2,4},{3,5},{4,2},{5,3},{6,0},{7,1},{8,14},{9,15},{10,... | collective-permute-start | bytes 393224 | tf_op jit(solution)/shard_map/ppermute | solution.py:710
  171.3 13.1 %collective-permute-start.26 = (bf16[512,128]{1,0:T(8,128)(2,1)}, bf16[512,128]{1,0:T(8,128)(2,1)S(1)}, u32[]{:S(2)}, u32[]{:S(2)}) collective-permute-start(bf16[512,128]{1,0:T(8,128)(2,1)} %get-tuple-element.140), channel_id=1, source_target_pairs={{0,7},{1,6},{2,5},{3,4},{4,3},{5,2},{6,1},{7,0},{8,15},{9,14},{10,... | collective-permute-start | bytes 393224 | tf_op jit(solution)/shard_map/ppermute | solution.py:710
  185.5 59.8 %all-to-all-start.3 = ((bf16[32,256,128]{2,1,0:T(8,128)(2,1)}), bf16[32,256,128]{2,1,0:T(8,128)(2,1)S(1)}, u32[]{:S(2)}, u32[]{:S(2)}) async-start(bf16[32,256,128]{2,1,0:T(8,128)(2,1)} %rest.1), calls=%async_computation.3 | async-start | bytes 4194304 | tf_op jit(solution)/shard_map/all_to_all | solution.py:707
  198.3 39.9 %collective-permute-start.28 = (bf16[128,2048]{1,0:T(8,128)(2,1)}, bf16[128,2048]{1,0:T(8,128)(2,1)S(1)}, u32[]{:S(2)}, u32[]{:S(2)}) collective-permute-start(bf16[128,2048]{1,0:T(8,128)(2,1)} %get-tuple-element.152), channel_id=1, source_target_pairs={{0,8},{1,9},{2,10},{3,11},{4,12},{5,13},{6,14},{7,15},{8,0},{9,1},... | collective-permute-start | bytes 1572872 | tf_op jit(solution)/shard_map/ppermute | solution.py:710
  200.1 59.5 %collective-permute-start.27 = (bf16[128,2048]{1,0:T(8,128)(2,1)}, bf16[128,2048]{1,0:T(8,128)(2,1)}, u32[]{:S(2)}, u32[]{:S(2)}) collective-permute-start(bf16[128,2048]{1,0:T(8,128)(2,1)} %get-tuple-element.150), channel_id=1, source_target_pairs={{0,8},{1,9},{2,10},{3,11},{4,12},{5,13},{6,14},{7,15},{8,0},{9,1},... | collective-permute-start | bytes 1572872 | tf_op jit(solution)/shard_map/ppermute | solution.py:710
  239.4 26.9 %collective-permute-start.29 = (bf16[128,2048]{1,0:T(8,128)(2,1)S(1)}, bf16[128,2048]{1,0:T(8,128)(2,1)}, u32[]{:S(2)}, u32[]{:S(2)}) collective-permute-start(bf16[128,2048]{1,0:T(8,128)(2,1)S(1)} %add_convert_fusion.1), channel_id=1, source_target_pairs={{0,16},{1,17},{2,18},{3,19},{4,20},{5,21},{6,22},{7,23},{8,24},{9,... | collective-permute-start | bytes 1572872 | tf_op jit(solution)/shard_map/ppermute | solution.py:710
  (31 other events, 487.3 us)

commit v7 on v6

--- a/solution.py
+++ b/solution.py
@@ -183,39 +183,43 @@
 def move_in(pos_ref, block_of, loads, wides, sorted_refs, count):
     lanes = pos_ref.shape[1]
 
-    def one(r, carry):
-        b = block_of(r)
-        for load, wide in zip(loads, wides):
-            wide[...] = load(r).astype(jnp.float32)
-        for first in range(0, lanes, ROWS_AT_ONCE):
-            rows = range(first, first + ROWS_AT_ONCE)
-            places = [pl.ds(pos_ref[b, row], 1) for row in rows]
-            held = [[wide[pl.ds(row, 1), :] for row in rows] for wide in wides]
-            for i, at in enumerate(places):
-                for ref, some in zip(sorted_refs, held):
-                    ref[at, :] = some[i]
+    def two(step, carry):
+        for half in range(2):
+            for load, wide in zip(loads, wides):
+                wide[pl.ds(half * lanes, lanes), :] = load(step * 2 + half).astype(jnp.float32)
+        for half in range(2):
+            b = block_of(step * 2 + half)
+            for first in range(0, lanes, ROWS_AT_ONCE):
+                rows = range(first, first + ROWS_AT_ONCE)
+                places = [pl.ds(pos_ref[b, row], 1) for row in rows]
+                held = [[wide[pl.ds(half * lanes + row, 1), :] for row in rows] for wide in wides]
+                for i, at in enumerate(places):
+                    for ref, some in zip(sorted_refs, held):
+                        ref[at, :] = some[i]
         return carry
 
-    lax.fori_loop(0, count, one, 0)
+    lax.fori_loop(0, count // 2, two, 0)
 
 
 def move_out(pos_ref, block_of, sorted_refs, wides, stores, count):
     lanes = pos_ref.shape[1]
 
-    def one(r, carry):
-        b = block_of(r)
-        for first in range(0, lanes, ROWS_AT_ONCE):
-            rows = range(first, first + ROWS_AT_ONCE)
-            places = [pl.ds(pos_ref[b, row], 1) for row in rows]
-            held = [[ref[at, :] for at in places] for ref in sorted_refs]
-            for i, row in enumerate(rows):
-                for wide, some in zip(wides, held):
-                    wide[pl.ds(row, 1), :] = some[i]
-        for store, wide in zip(stores, wides):
-            store(r, wide[...])
+    def two(step, carry):
+        for half in range(2):
+            b = block_of(step * 2 + half)
+            for first in range(0, lanes, ROWS_AT_ONCE):
+                rows = range(first, first + ROWS_AT_ONCE)
+                places = [pl.ds(pos_ref[b, row], 1) for row in rows]
+                held = [[ref[at, :] for at in places] for ref in sorted_refs]
+                for i, row in enumerate(rows):
+                    for wide, some in zip(wides, held):
+                        wide[pl.ds(half * lanes + row, 1), :] = some[i]
+        for half in range(2):
+            for store, wide in zip(stores, wides):
+                store(step * 2 + half, wide[pl.ds(half * lanes, lanes), :])
         return carry
 
-    lax.fori_loop(0, count, one, 0)
+    lax.fori_loop(0, count // 2, two, 0)
 
 
 def tiles_of(step):
@@ -466,7 +470,7 @@
     rows = blocks * lanes
     bf, f32 = jnp.bfloat16, jnp.float32
     scale = 1.0 / math.sqrt(size)
-    plain, padded, wide = (rows, size), (rows + 2 * CAP, size), (lanes, size)
+    plain, padded, wide = (rows, size), (rows + 2 * CAP, size), (2 * lanes, size)
     me = place_in_plane(low)
 
     def call(kernel, operands, outs, scratch, micros, name, late=0):

time: 270 us -> 269 us (level)
  transfers between devices with their start and end apart: 34 -> 34, of which waited for: 14 -> 14; matrix products, arithmetic and copies ran while one was open for 1% -> 1% of each run, Pallas kernels for 32% -> 31%
where the time goes in v7:
time: 269 us; the launch traced here: 268 us
  waiting for transfers between devices  113 us (42%)
  Pallas kernels  86.5 us (32%)
  starting transfers between devices  54.9 us (20%)
  local copies, waits for them, and re-layouts  6.19 us (2%)
  other arithmetic  5.91 us (2%)
    ppermute x30, waiting for transfers between devices, send(): return lax.ppermute(block, 'seq', [(i, i ^ bits) for i in range(owners)])  100 us
    pallas_call x8, Pallas kernels, run(): pl.pallas_call(body, out_shape=tuple((jax.ShapeDtypeStruct(shape, kind) f...  79 us
    ppermute x30, starting transfers between devices, send(): return lax.ppermute(block, 'seq', [(i, i ^ bits) for i in range(owners)])  37.1 us
    all_to_all x4, starting transfers between devices, exchange(): return lax.all_to_all(rows, 'seq', split_axis=0, concat_axis=0, tiled=True)  17.8 us
    all_to_all x4, waiting for transfers between devices, exchange(): return lax.all_to_all(rows, 'seq', split_axis=0, concat_axis=0, tiled=True)  13.1 us
    unnamed x58, local copies, waits for them, and re-layouts  5.59 us
  transfers between devices with their start and end apart: 34, of which 14 were waited for; matrix products, arithmetic and copies ran while one was open for 1% of the time, Pallas kernels for 31%

profile of v7, /device:TPU:0, one launch (start us, length us, event | category | flops | bytes accessed | tf_op | source)
XLA Modules:
  0.0 267.8 jit_solution(7730229280136655382)
XLA Ops:
  2.7 2.7 pack_weight.1
  5.3 3.1 %collective-permute-start = (bf16[544,128]{1,0:T(8,128)(2,1)}, bf16[544,128]{1,0:T(8,128)(2,1)S(1)}, u32[]{:S(2)}, u32[]{:S(2)}) collective-permute-start(bf16[544,128]{1,0:T(8,128)(2,1)} %get-tuple-element.85), channel_id=1, source_target_pairs={{0,8},{1,9},{2,10},{3,11},{4,12},{5,13},{6,14},{7,15},{8,0},{9,1},... | collective-permute-start | bytes 417800 | tf_op jit(solution)/shard_map/ppermute | solution.py:714
  8.4 2.6 collective-permute-start.1
  11.0 3.1 %collective-permute-done = bf16[544,128]{1,0:T(8,128)(2,1)S(1)} collective-permute-done((bf16[544,128]{1,0:T(8,128)(2,1)}, bf16[544,128]{1,0:T(8,128)(2,1)S(1)}, u32[]{:S(2)}, u32[]{:S(2)}) %collective-permute-start) | collective-permute-done | bytes 139296 | tf_op jit(solution)/shard_map/ppermute | solution.py:714
  14.1 8.0 %collective-permute-done.1 = bf16[544,128]{1,0:T(8,128)(2,1)S(1)} collective-permute-done((bf16[544,128]{1,0:T(8,128)(2,1)}, bf16[544,128]{1,0:T(8,128)(2,1)S(1)}, u32[]{:S(2)}, u32[]{:S(2)}) %collective-permute-start.1) | collective-permute-done | bytes 139296 | tf_op jit(solution)/shard_map/ppermute | solution.py:714
  22.1 3.1 %collective-permute-start.7 = (bf16[128,2048]{1,0:T(8,128)(2,1)}, bf16[128,2048]{1,0:T(8,128)(2,1)S(1)}, u32[]{:S(2)}, u32[]{:S(2)}) collective-permute-start(bf16[128,2048]{1,0:T(8,128)(2,1)} %refs_9_), channel_id=1, source_target_pairs={{0,16},{1,17},{2,18},{3,19},{4,20},{5,21},{6,22},{7,23},{8,24},{9,... | collective-permute-start | bytes 1572872 | tf_op jit(solution)/shard_map/ppermute | solution.py:714
  29.8 18.0 %collective-permute-done.7.refs_11_ = bf16[128,2048]{1,0:T(8,128)(2,1)S(1)} collective-permute-done((bf16[128,2048]{1,0:T(8,128)(2,1)}, bf16[128,2048]{1,0:T(8,128)(2,1)S(1)}, u32[]{:S(2)}, u32[]{:S(2)}) %collective-permute-start.7) | collective-permute-done | bytes 524320 | tf_op jit(solution)/shard_map/ppermute | solution.py:714
  49.5 2.1 pack.2
  51.6 2.6 collective-permute-done.6.refs_10_
  56.3 6.9 %collective-permute-done.8.refs_12_ = bf16[128,2048]{1,0:T(8,128)(2,1)} collective-permute-done((bf16[128,2048]{1,0:T(8,128)(2,1)S(1)}, bf16[128,2048]{1,0:T(8,128)(2,1)}, u32[]{:S(2)}, u32[]{:S(2)}) %collective-permute-start.8) | collective-permute-done | bytes 524320 | tf_op jit(solution)/shard_map/ppermute | solution.py:714
  63.2 2.8 %all-to-all-start = ((bf16[32,256,128]{2,1,0:T(8,128)(2,1)}), bf16[32,256,128]{2,1,0:T(8,128)(2,1)S(1)}, u32[]{:S(2)}, u32[]{:S(2)}) async-start(bf16[32,256,128]{2,1,0:T(8,128)(2,1)} %pack.2), calls=%async_computation | async-start | bytes 4194304 | tf_op jit(solution)/shard_map/all_to_all | solution.py:711
  71.5 8.3 %project_back.1 = (bf16[512,128]{1,0:T(8,128)(2,1)}, bf16[512,128]{1,0:T(8,128)(2,1)}, bf16[512,128]{1,0:T(8,128)(2,1)}, bf16[512,128]{1,0:T(8,128)(2,1)}, bf16[...) custom-call(s32[2]{0:T(128)} %pad_add_fusion.refs_0_, ...), custom_call_target="tpu_custom_call" | custom-call | bytes 28000000 | tf_op jit(solution)/shard_map/project_back/pallas_call | solution.py:60
  83.7 2.6 collective-permute-start.18
  88.0 4.0 %collective-permute-start.19 = (bf16[512,128]{1,0:T(8,128)(2,1)}, bf16[512,128]{1,0:T(8,128)(2,1)S(1)}, u32[]{:S(2)}, u32[]{:S(2)}) collective-permute-start(bf16[512,128]{1,0:T(8,128)(2,1)} %get-tuple-element.111), channel_id=1, source_target_pairs={{0,7},{1,6},{2,5},{3,4},{4,3},{5,2},{6,1},{7,0},{8,15},{9,14},{10,... | collective-permute-start | bytes 393224 | tf_op jit(solution)/shard_map/ppermute | solution.py:714
  92.0 11.0 %place.1 = (s32[32,128]{1,0:T(8,128)}, bf16[4096,128]{1,0:T(8,128)(2,1)}) custom-call(s32[2]{0:T(128)} %pad_add_fusion.refs_0_, bf16[4,544,128]{2,1,0:T(8,128)(2,1)} %copy-done.6, bf16[4,544,128]{2,1,0:T(8,128)(2,1)} %copy-done.10, bf16[4,544,128]{2,1,0:T(8,128)(2,1)} %copy-done.7, bf16[4,544,128]{2,1,0:T(8,128)(2,1)} %copy-done.11, ...), custom_call_target="tpu_custom_call" | custom-call | bytes 28000000 | tf_op jit(solution)/shard_map/place/pallas_call | solution.py:60
  103.1 11.9 %all-to-all-done.refs_1_ = bf16[32,256,128]{2,1,0:T(8,128)(2,1)S(1)} async-done(((bf16[32,256,128]{2,1,0:T(8,128)(2,1)}), bf16[32,256,128]{2,1,0:T(8,128)(2,1)S(1)}, u32[]{:S(2)}, u32[]{:S(2)}) %all-to-all-start) | async-done | bytes 2097184 | tf_op jit(solution)/shard_map/all_to_all | solution.py:711
  115.0 4.0 %all-to-all-start.1 = ((bf16[32,128,128]{2,1,0:T(8,128)(2,1)}), bf16[32,128,128]{2,1,0:T(8,128)(2,1)}, u32[]{:S(2)}, u32[]{:S(2)}) async-start(bf16[32,128,128]{2,1,0:T(8,128)(2,1)} %pack.3), calls=%async_computation.1 | async-start | bytes 2097152 | tf_op jit(solution)/shard_map/all_to_all | solution.py:711
  119.1 12.2 %scores.1 = (bf16[4160,128]{1,0:T(8,128)(2,1)}, bf16[4160,128]{1,0:T(8,128)(2,1)}, bf16[4096,128]{1,0:T(8,128)(2,1)}) custom-call(s32[32,128]{1,0:T(8,128)} %get-tuple-element.114.refs_0_.refs_1_, bf16[32,256,128]{2,1,0:T(8,128)(2,1)} %copy-done.5, bf16[4096,128]{1,0:T(8,128)(2,1)} %get-tuple-element.125.refs_2_), custom_call_target="tpu_custom_call" | custom-call | bytes 42000000 | tf_op jit(solution)/shard_map/scores/pallas_call | solution.py:60
  131.3 12.8 %grad_value.1 = (bf16[32,128,128]{2,1,0:T(8,128)(2,1)}, bf16[4096,128]{1,0:T(8,128)(2,1)}) custom-call(s32[2]{0:T(128)} %pad_add_fusion.refs_0_, s32[32,128]{1,0:T(8,128)} %get-tuple-element.114.refs_0_.refs_1_, bf16[512,128]{1,0:T(8,128)(2,1)} %get-tuple-element.116.refs_2_, bf16[512,128]{1,0:T(8,128)(2,1)} %copy-done.15, bf16[512,128]{1,0:T(8,128)(2,1)} %copy-done.16, ...), custom_call_target="tpu_custom_call" | custom-call | bytes 42000000 | tf_op jit(solution)/shard_map/grad_value/pallas_call | solution.py:60
  145.3 4.8 %all-to-all-start.2 = ((bf16[32,128,128]{2,1,0:T(8,128)(2,1)}), bf16[32,128,128]{2,1,0:T(8,128)(2,1)S(1)}, u32[]{:S(2)}, u32[]{:S(2)}) async-start(bf16[32,128,128]{2,1,0:T(8,128)(2,1)} %get-tuple-element.154), calls=%async_computation.2 | async-start | bytes 2097152 | tf_op jit(solution)/shard_map/all_to_all | solution.py:711
  150.1 13.5 %attend.1 = (bf16[512,128]{1,0:T(8,128)(2,1)}, bf16[512,128]{1,0:T(8,128)(2,1)}, bf16[512,128]{1,0:T(8,128)(2,1)}, bf16[512,128]{1,0:T(8,128)(2,1)}, bf16[512,12...) custom-call(s32[2]{0:T(128)} %pad_add_fusion.refs_0_, ...), custom_call_target="tpu_custom_call" | custom-call | bytes 42000000 | tf_op jit(solution)/shard_map/attend/pallas_call | solution.py:60
  167.3 2.6 collective-permute-start.25
  171.5 11.8 %rest.1 = bf16[32,256,128]{2,1,0:T(8,128)(2,1)} custom-call(s32[32,128]{1,0:T(8,128)} %get-tuple-element.114.refs_0_.refs_1_, bf16[4096,128]{1,0:T(8,128)(2,1)} %get-tuple-element.130.refs_1_, bf16[4160,128]{1,0:T(8,128)(2,1)} %get-tuple-element.131.refs_2_, bf16[4160,128]{1,0:T(8,128)(2,1)} %get-tuple-element.132.refs_3_), custom_call_target="tpu_custom_call" | custom-call | bytes 42000000 | tf_op jit(solution)/shard_map/rest/pallas_call | solution.py:60
  184.5 6.1 %all-to-all-start.3 = ((bf16[32,256,128]{2,1,0:T(8,128)(2,1)}), bf16[32,256,128]{2,1,0:T(8,128)(2,1)S(1)}, u32[]{:S(2)}, u32[]{:S(2)}) async-start(bf16[32,256,128]{2,1,0:T(8,128)(2,1)} %rest.1), calls=%async_computation.3 | async-start | bytes 4194304 | tf_op jit(solution)/shard_map/all_to_all | solution.py:711
  190.7 6.7 %project.1 = (bf16[128,2048]{1,0:T(8,128)(2,1)}, bf16[128,2048]{1,0:T(8,128)(2,1)}, bf16[128,2048]{1,0:T(8,128)(2,1)}, bf16[128,2048]{1,0:T(8,128)(2,1)}) custom-call(bf16[8,2048,128]{2,1,0:T(8,128)(2,1)} %get-tuple-element.101.refs_0_, bf16[512,128]{1,0:T(8,128)(2,1)} %get-tuple-element.141.refs_1_, bf16[512,128]{1,0:T(8,128)(2,1)} %copy-done.18, ...), custom_call_target="tpu_custom_call" | custom-call | bytes 21000000 | tf_op jit(solution)/shard_map/project/pallas_call | solution.py:60
  197.4 1.8 collective-permute-start.28
  199.5 37.8 %collective-permute-done.28 = bf16[128,2048]{1,0:T(8,128)(2,1)S(1)} collective-permute-done((bf16[128,2048]{1,0:T(8,128)(2,1)}, bf16[128,2048]{1,0:T(8,128)(2,1)S(1)}, u32[]{:S(2)}, u32[]{:S(2)}) %collective-permute-start.28) | collective-permute-done | bytes 524320 | tf_op jit(solution)/shard_map/ppermute | solution.py:714
  238.5 4.3 %collective-permute-start.29 = (bf16[128,2048]{1,0:T(8,128)(2,1)S(1)}, bf16[128,2048]{1,0:T(8,128)(2,1)}, u32[]{:S(2)}, u32[]{:S(2)}) collective-permute-start(bf16[128,2048]{1,0:T(8,128)(2,1)S(1)} %add_convert_fusion.1), channel_id=1, source_target_pairs={{0,16},{1,17},{2,18},{3,19},{4,20},{5,21},{6,22},{7,23},{8,24},{9,... | collective-permute-start | bytes 1572872 | tf_op jit(solution)/shard_map/ppermute | solution.py:714
  244.4 2.0 unpack.2
  246.4 12.3 %collective-permute-done.27 = bf16[128,2048]{1,0:T(8,128)(2,1)} collective-permute-done((bf16[128,2048]{1,0:T(8,128)(2,1)}, bf16[128,2048]{1,0:T(8,128)(2,1)}, u32[]{:S(2)}, u32[]{:S(2)}) %collective-permute-start.27) | collective-permute-done | bytes 524320 | tf_op jit(solution)/shard_map/ppermute | solution.py:714
  258.7 6.6 %collective-permute-done.29 = bf16[128,2048]{1,0:T(8,128)(2,1)} collective-permute-done((bf16[128,2048]{1,0:T(8,128)(2,1)S(1)}, bf16[128,2048]{1,0:T(8,128)(2,1)}, u32[]{:S(2)}, u32[]{:S(2)}) %collective-permute-start.29) | collective-permute-done | bytes 524320 | tf_op jit(solution)/shard_map/ppermute | solution.py:714
  265.4 2.4 add_convert_fusion
  (113 shorter events, 31.9 us)
Async XLA Ops:
  5.3 8.7 %collective-permute-start = (bf16[544,128]{1,0:T(8,128)(2,1)}, bf16[544,128]{1,0:T(8,128)(2,1)S(1)}, u32[]{:S(2)}, u32[]{:S(2)}) collective-permute-start(bf16[544,128]{1,0:T(8,128)(2,1)} %get-tuple-element.85), channel_id=1, source_target_pairs={{0,8},{1,9},{2,10},{3,11},{4,12},{5,13},{6,14},{7,15},{8,0},{9,1},... | collective-permute-start | bytes 417800 | tf_op jit(solution)/shard_map/ppermute | solution.py:714
  8.4 13.7 %collective-permute-start.1 = (bf16[544,128]{1,0:T(8,128)(2,1)}, bf16[544,128]{1,0:T(8,128)(2,1)S(1)}, u32[]{:S(2)}, u32[]{:S(2)}) collective-permute-start(bf16[544,128]{1,0:T(8,128)(2,1)} %get-tuple-element.86), channel_id=1, source_target_pairs={{0,16},{1,17},{2,18},{3,19},{4,20},{5,21},{6,22},{7,23},{8,24},{9,... | collective-permute-start | bytes 417800 | tf_op jit(solution)/shard_map/ppermute | solution.py:714
  11.0 11.1 %collective-permute-start.2 = (bf16[544,128]{1,0:T(8,128)(2,1)}, bf16[544,128]{1,0:T(8,128)(2,1)S(1)}, u32[]{:S(2)}, u32[]{:S(2)}) collective-permute-start(bf16[544,128]{1,0:T(8,128)(2,1)} %get-tuple-element.87), channel_id=1, source_target_pairs={{0,24},{1,25},{2,26},{3,27},{4,28},{5,29},{6,30},{7,31},{8,16},{9,... | collective-permute-start | bytes 417800 | tf_op jit(solution)/shard_map/ppermute | solution.py:714
  22.1 25.7 %collective-permute-start.7 = (bf16[128,2048]{1,0:T(8,128)(2,1)}, bf16[128,2048]{1,0:T(8,128)(2,1)S(1)}, u32[]{:S(2)}, u32[]{:S(2)}) collective-permute-start(bf16[128,2048]{1,0:T(8,128)(2,1)} %refs_9_), channel_id=1, source_target_pairs={{0,16},{1,17},{2,18},{3,19},{4,20},{5,21},{6,22},{7,23},{8,24},{9,... | collective-permute-start | bytes 1572872 | tf_op jit(solution)/shard_map/ppermute | solution.py:714
  26.2 28.0 %collective-permute-start.3 = (bf16[4,544,128]{2,1,0:T(8,128)(2,1)S(1)}, bf16[4,544,128]{2,1,0:T(8,128)(2,1)S(1)}, u32[]{:S(2)}, u32[]{:S(2)}) collective-permute-start(bf16[4,544,128]{2,1,0:T(8,128)(2,1)S(1)} %pad_maximum_fusion.refs_1_), channel_id=1, source_target_pairs={{0,2},{1,3},{2,0},{3,1},{4,6},{5,7},{6,4},{7,5},{8,10},{9,11},{10,... | collective-permute-start | bytes 1671176 | tf_op jit(solution)/shard_map/ppermute | solution.py:714
  27.8 26.5 %collective-permute-start.4 = (bf16[4,544,128]{2,1,0:T(8,128)(2,1)S(1)}, bf16[4,544,128]{2,1,0:T(8,128)(2,1)S(1)}, u32[]{:S(2)}, u32[]{:S(2)}) collective-permute-start(bf16[4,544,128]{2,1,0:T(8,128)(2,1)S(1)} %pad_maximum_fusion.refs_1_), channel_id=1, source_target_pairs={{0,4},{1,5},{2,6},{3,7},{4,0},{5,1},{6,2},{7,3},{8,12},{9,13},{10,... | collective-permute-start | bytes 1671176 | tf_op jit(solution)/shard_map/ppermute | solution.py:714
  29.3 25.0 %collective-permute-start.5 = (bf16[4,544,128]{2,1,0:T(8,128)(2,1)S(1)}, bf16[4,544,128]{2,1,0:T(8,128)(2,1)S(1)}, u32[]{:S(2)}, u32[]{:S(2)}) collective-permute-start(bf16[4,544,128]{2,1,0:T(8,128)(2,1)S(1)} %pad_maximum_fusion.refs_1_), channel_id=1, source_target_pairs={{0,6},{1,7},{2,4},{3,5},{4,2},{5,3},{6,0},{7,1},{8,14},{9,15},{10,... | collective-permute-start | bytes 1671176 | tf_op jit(solution)/shard_map/ppermute | solution.py:714
  29.8 24.5 %collective-permute-start.6 = (bf16[128,2048]{1,0:T(8,128)(2,1)}, bf16[128,2048]{1,0:T(8,128)(2,1)S(1)}, u32[]{:S(2)}, u32[]{:S(2)}) collective-permute-start(bf16[128,2048]{1,0:T(8,128)(2,1)} %refs_9_), channel_id=1, source_target_pairs={{0,8},{1,9},{2,10},{3,11},{4,12},{5,13},{6,14},{7,15},{8,0},{9,1},... | collective-permute-start | bytes 1572872 | tf_op jit(solution)/shard_map/ppermute | solution.py:714
  47.8 15.4 %collective-permute-start.8 = (bf16[128,2048]{1,0:T(8,128)(2,1)S(1)}, bf16[128,2048]{1,0:T(8,128)(2,1)}, u32[]{:S(2)}, u32[]{:S(2)}) collective-permute-start(bf16[128,2048]{1,0:T(8,128)(2,1)S(1)} %collective-permute-done.7.refs_11_), channel_id=1, source_target_pairs={{0,8},{1,9},{2,10},{3,11},{4,12},{5,13},{6,14},{7,15},{8,0},{9,1},... | collective-permute-start | bytes 1572872 | tf_op jit(solution)/shard_map/ppermute | solution.py:714
  63.2 51.8 %all-to-all-start = ((bf16[32,256,128]{2,1,0:T(8,128)(2,1)}), bf16[32,256,128]{2,1,0:T(8,128)(2,1)S(1)}, u32[]{:S(2)}, u32[]{:S(2)}) async-start(bf16[32,256,128]{2,1,0:T(8,128)(2,1)} %pack.2), calls=%async_computation | async-start | bytes 4194304 | tf_op jit(solution)/shard_map/all_to_all | solution.py:711
  66.6 4.1 %collective-permute-start.11 = (bf16[4,544,128]{2,1,0:T(8,128)(2,1)}, bf16[4,544,128]{2,1,0:T(8,128)(2,1)S(1)}, u32[]{:S(2)}, u32[]{:S(2)}) collective-permute-start(bf16[4,544,128]{2,1,0:T(8,128)(2,1)} %copy-done.8), channel_id=1, source_target_pairs={{0,1},{1,0},{2,3},{3,2},{4,5},{5,4},{6,7},{7,6},{8,9},{9,8},{10,11... | collective-permute-start | bytes 1671176 | tf_op jit(solution)/shard_map/ppermute | solution.py:714
  66.9 4.7 %collective-permute-start.12 = (bf16[4,544,128]{2,1,0:T(8,128)(2,1)}, bf16[4,544,128]{2,1,0:T(8,128)(2,1)}, u32[]{:S(2)}, u32[]{:S(2)}) collective-permute-start(bf16[4,544,128]{2,1,0:T(8,128)(2,1)} %copy-done.9), channel_id=1, source_target_pairs={{0,1},{1,0},{2,3},{3,2},{4,5},{5,4},{6,7},{7,6},{8,9},{9,8},{10,11... | collective-permute-start | bytes 1671176 | tf_op jit(solution)/shard_map/ppermute | solution.py:714
  79.9 3.8 %collective-permute-start.13 = (bf16[512,128]{1,0:T(8,128)(2,1)}, bf16[512,128]{1,0:T(8,128)(2,1)S(1)}, u32[]{:S(2)}, u32[]{:S(2)}) collective-permute-start(bf16[512,128]{1,0:T(8,128)(2,1)} %get-tuple-element.105), channel_id=1, source_target_pairs={{0,1},{1,0},{2,3},{3,2},{4,5},{5,4},{6,7},{7,6},{8,9},{9,8},{10,11... | collective-permute-start | bytes 393224 | tf_op jit(solution)/shard_map/ppermute | solution.py:714
  80.2 7.8 %collective-permute-start.14 = (bf16[512,128]{1,0:T(8,128)(2,1)}, bf16[512,128]{1,0:T(8,128)(2,1)S(1)}, u32[]{:S(2)}, u32[]{:S(2)}) collective-permute-start(bf16[512,128]{1,0:T(8,128)(2,1)} %get-tuple-element.106), channel_id=1, source_target_pairs={{0,2},{1,3},{2,0},{3,1},{4,6},{5,7},{6,4},{7,5},{8,10},{9,11},{10,... | collective-permute-start | bytes 393224 | tf_op jit(solution)/shard_map/ppermute | solution.py:714
  81.9 21.1 %collective-permute-start.15 = (bf16[512,128]{1,0:T(8,128)(2,1)}, bf16[512,128]{1,0:T(8,128)(2,1)S(1)}, u32[]{:S(2)}, u32[]{:S(2)}) collective-permute-start(bf16[512,128]{1,0:T(8,128)(2,1)} %get-tuple-element.107), channel_id=1, source_target_pairs={{0,3},{1,2},{2,1},{3,0},{4,7},{5,6},{6,5},{7,4},{8,11},{9,10},{10,... | collective-permute-start | bytes 393224 | tf_op jit(solution)/shard_map/ppermute | solution.py:714
  81.9 21.1 %collective-permute-start.16 = (bf16[512,128]{1,0:T(8,128)(2,1)}, bf16[512,128]{1,0:T(8,128)(2,1)S(1)}, u32[]{:S(2)}, u32[]{:S(2)}) collective-permute-start(bf16[512,128]{1,0:T(8,128)(2,1)} %get-tuple-element.108), channel_id=1, source_target_pairs={{0,4},{1,5},{2,6},{3,7},{4,0},{5,1},{6,2},{7,3},{8,12},{9,13},{10,... | collective-permute-start | bytes 393224 | tf_op jit(solution)/shard_map/ppermute | solution.py:714
  83.6 19.5 %collective-permute-start.17 = (bf16[512,128]{1,0:T(8,128)(2,1)}, bf16[512,128]{1,0:T(8,128)(2,1)S(1)}, u32[]{:S(2)}, u32[]{:S(2)}) collective-permute-start(bf16[512,128]{1,0:T(8,128)(2,1)} %get-tuple-element.109), channel_id=1, source_target_pairs={{0,5},{1,4},{2,7},{3,6},{4,1},{5,0},{6,3},{7,2},{8,13},{9,12},{10,... | collective-permute-start | bytes 393224 | tf_op jit(solution)/shard_map/ppermute | solution.py:714
  83.7 19.4 %collective-permute-start.18 = (bf16[512,128]{1,0:T(8,128)(2,1)}, bf16[512,128]{1,0:T(8,128)(2,1)S(1)}, u32[]{:S(2)}, u32[]{:S(2)}) collective-permute-start(bf16[512,128]{1,0:T(8,128)(2,1)} %get-tuple-element.110), channel_id=1, source_target_pairs={{0,6},{1,7},{2,4},{3,5},{4,2},{5,3},{6,0},{7,1},{8,14},{9,15},{10,... | collective-permute-start | bytes 393224 | tf_op jit(solution)/shard_map/ppermute | solution.py:714
  88.0 15.1 %collective-permute-start.19 = (bf16[512,128]{1,0:T(8,128)(2,1)}, bf16[512,128]{1,0:T(8,128)(2,1)S(1)}, u32[]{:S(2)}, u32[]{:S(2)}) collective-permute-start(bf16[512,128]{1,0:T(8,128)(2,1)} %get-tuple-element.111), channel_id=1, source_target_pairs={{0,7},{1,6},{2,5},{3,4},{4,3},{5,2},{6,1},{7,0},{8,15},{9,14},{10,... | collective-permute-start | bytes 393224 | tf_op jit(solution)/shard_map/ppermute | solution.py:714
  115.0 30.3 %all-to-all-start.1 = ((bf16[32,128,128]{2,1,0:T(8,128)(2,1)}), bf16[32,128,128]{2,1,0:T(8,128)(2,1)}, u32[]{:S(2)}, u32[]{:S(2)}) async-start(bf16[32,128,128]{2,1,0:T(8,128)(2,1)} %pack.3), calls=%async_computation.1 | async-start | bytes 2097152 | tf_op jit(solution)/shard_map/all_to_all | solution.py:711
  145.3 38.1 %all-to-all-start.2 = ((bf16[32,128,128]{2,1,0:T(8,128)(2,1)}), bf16[32,128,128]{2,1,0:T(8,128)(2,1)S(1)}, u32[]{:S(2)}, u32[]{:S(2)}) async-start(bf16[32,128,128]{2,1,0:T(8,128)(2,1)} %get-tuple-element.154), calls=%async_computation.2 | async-start | bytes 2097152 | tf_op jit(solution)/shard_map/all_to_all | solution.py:711
  163.7 3.6 %collective-permute-start.20 = (bf16[512,128]{1,0:T(8,128)(2,1)}, bf16[512,128]{1,0:T(8,128)(2,1)S(1)}, u32[]{:S(2)}, u32[]{:S(2)}) collective-permute-start(bf16[512,128]{1,0:T(8,128)(2,1)} %get-tuple-element.134), channel_id=1, source_target_pairs={{0,1},{1,0},{2,3},{3,2},{4,5},{5,4},{6,7},{7,6},{8,9},{9,8},{10,11... | collective-permute-start | bytes 393224 | tf_op jit(solution)/shard_map/ppermute | solution.py:714
  163.8 7.0 %collective-permute-start.21 = (bf16[512,128]{1,0:T(8,128)(2,1)}, bf16[512,128]{1,0:T(8,128)(2,1)S(1)}, u32[]{:S(2)}, u32[]{:S(2)}) collective-permute-start(bf16[512,128]{1,0:T(8,128)(2,1)} %get-tuple-element.135), channel_id=1, source_target_pairs={{0,2},{1,3},{2,0},{3,1},{4,6},{5,7},{6,4},{7,5},{8,10},{9,11},{10,... | collective-permute-start | bytes 393224 | tf_op jit(solution)/shard_map/ppermute | solution.py:714
  165.5 17.8 %collective-permute-start.22 = (bf16[512,128]{1,0:T(8,128)(2,1)}, bf16[512,128]{1,0:T(8,128)(2,1)S(1)}, u32[]{:S(2)}, u32[]{:S(2)}) collective-permute-start(bf16[512,128]{1,0:T(8,128)(2,1)} %get-tuple-element.136), channel_id=1, source_target_pairs={{0,3},{1,2},{2,1},{3,0},{4,7},{5,6},{6,5},{7,4},{8,11},{9,10},{10,... | collective-permute-start | bytes 393224 | tf_op jit(solution)/shard_map/ppermute | solution.py:714
  165.6 17.7 %collective-permute-start.23 = (bf16[512,128]{1,0:T(8,128)(2,1)}, bf16[512,128]{1,0:T(8,128)(2,1)S(1)}, u32[]{:S(2)}, u32[]{:S(2)}) collective-permute-start(bf16[512,128]{1,0:T(8,128)(2,1)} %get-tuple-element.137), channel_id=1, source_target_pairs={{0,4},{1,5},{2,6},{3,7},{4,0},{5,1},{6,2},{7,3},{8,12},{9,13},{10,... | collective-permute-start | bytes 393224 | tf_op jit(solution)/shard_map/ppermute | solution.py:714
  167.2 16.2 %collective-permute-start.24 = (bf16[512,128]{1,0:T(8,128)(2,1)}, bf16[512,128]{1,0:T(8,128)(2,1)S(1)}, u32[]{:S(2)}, u32[]{:S(2)}) collective-permute-start(bf16[512,128]{1,0:T(8,128)(2,1)} %get-tuple-element.138), channel_id=1, source_target_pairs={{0,5},{1,4},{2,7},{3,6},{4,1},{5,0},{6,3},{7,2},{8,13},{9,12},{10,... | collective-permute-start | bytes 393224 | tf_op jit(solution)/shard_map/ppermute | solution.py:714
  167.3 16.1 %collective-permute-start.25 = (bf16[512,128]{1,0:T(8,128)(2,1)}, bf16[512,128]{1,0:T(8,128)(2,1)S(1)}, u32[]{:S(2)}, u32[]{:S(2)}) collective-permute-start(bf16[512,128]{1,0:T(8,128)(2,1)} %get-tuple-element.139), channel_id=1, source_target_pairs={{0,6},{1,7},{2,4},{3,5},{4,2},{5,3},{6,0},{7,1},{8,14},{9,15},{10,... | collective-permute-start | bytes 393224 | tf_op jit(solution)/shard_map/ppermute | solution.py:714
  170.8 12.6 %collective-permute-start.26 = (bf16[512,128]{1,0:T(8,128)(2,1)}, bf16[512,128]{1,0:T(8,128)(2,1)S(1)}, u32[]{:S(2)}, u32[]{:S(2)}) collective-permute-start(bf16[512,128]{1,0:T(8,128)(2,1)} %get-tuple-element.140), channel_id=1, source_target_pairs={{0,7},{1,6},{2,5},{3,4},{4,3},{5,2},{6,1},{7,0},{8,15},{9,14},{10,... | collective-permute-start | bytes 393224 | tf_op jit(solution)/shard_map/ppermute | solution.py:714
  184.5 59.9 %all-to-all-start.3 = ((bf16[32,256,128]{2,1,0:T(8,128)(2,1)}), bf16[32,256,128]{2,1,0:T(8,128)(2,1)S(1)}, u32[]{:S(2)}, u32[]{:S(2)}) async-start(bf16[32,256,128]{2,1,0:T(8,128)(2,1)} %rest.1), calls=%async_computation.3 | async-start | bytes 4194304 | tf_op jit(solution)/shard_map/all_to_all | solution.py:711
  197.4 39.9 %collective-permute-start.28 = (bf16[128,2048]{1,0:T(8,128)(2,1)}, bf16[128,2048]{1,0:T(8,128)(2,1)S(1)}, u32[]{:S(2)}, u32[]{:S(2)}) collective-permute-start(bf16[128,2048]{1,0:T(8,128)(2,1)} %get-tuple-element.152), channel_id=1, source_target_pairs={{0,8},{1,9},{2,10},{3,11},{4,12},{5,13},{6,14},{7,15},{8,0},{9,1},... | collective-permute-start | bytes 1572872 | tf_op jit(solution)/shard_map/ppermute | solution.py:714
  199.2 59.5 %collective-permute-start.27 = (bf16[128,2048]{1,0:T(8,128)(2,1)}, bf16[128,2048]{1,0:T(8,128)(2,1)}, u32[]{:S(2)}, u32[]{:S(2)}) collective-permute-start(bf16[128,2048]{1,0:T(8,128)(2,1)} %get-tuple-element.150), channel_id=1, source_target_pairs={{0,8},{1,9},{2,10},{3,11},{4,12},{5,13},{6,14},{7,15},{8,0},{9,1},... | collective-permute-start | bytes 1572872 | tf_op jit(solution)/shard_map/ppermute | solution.py:714
  238.5 26.9 %collective-permute-start.29 = (bf16[128,2048]{1,0:T(8,128)(2,1)S(1)}, bf16[128,2048]{1,0:T(8,128)(2,1)}, u32[]{:S(2)}, u32[]{:S(2)}) collective-permute-start(bf16[128,2048]{1,0:T(8,128)(2,1)S(1)} %add_convert_fusion.1), channel_id=1, source_target_pairs={{0,16},{1,17},{2,18},{3,19},{4,20},{5,21},{6,22},{7,23},{8,24},{9,... | collective-permute-start | bytes 1572872 | tf_op jit(solution)/shard_map/ppermute | solution.py:714
  (31 other events, 486.6 us)
